TPU v7x, 128 devices: a whole 4x4x4 slice. The times are simulated.
128 devices in a mesh: ch: 32 (over y, z_hi, x), img: 4 (over z_lo, core).
Axes of the slice: x: 4, y: 4, z: 4 (z_hi: 2, z_lo: 2; z = z_hi * 2 + z_lo), core: 2. Of those that a mesh axis runs over, the one named last changes fastest.
Arguments:
- inputs: bfloat16 [256, 128, 256], P('ch', 'img'), may hold values from -6 to 6
- timesteps: int32 [128], P('img'), may hold values from 0 to 999
- keep_mask: int32 [256, 128, 256], P('ch', 'img'), may hold values 0 or 1
- norm_gain: float32 [3, 256], P(None, 'ch'), may hold values from 0.1 to 1.9
- norm_bias: float32 [3, 256], P(None, 'ch'), may hold values from -4 to 4
- conv_weight: bfloat16 [2, 9, 256, 256], P(None, None, 'ch'), may hold values from -0.125 to 0.125
- conv_bias: float32 [2, 256], P(None, 'ch'), may hold values from -4 to 4
- temb_weight: bfloat16 [512, 256], P(None, 'ch'), may hold values from -0.25 to 0.25
- temb_bias: float32 [256], P('ch'), may hold values from -4 to 4
- qkv_weight: bfloat16 [3, 256, 256], P(None, 'ch'), may hold values from -0.375 to 0.375
- qv_bias: float32 [2, 256], P(None, 'ch'), may hold values from -4 to 4
- out_weight: bfloat16 [256, 256], P('ch'), may hold values from -3 to 3
- out_bias: float32 [256], P('ch'), may hold values from -4 to 4
- cotangent: bfloat16 [256, 128, 256], P('ch', 'img'), may hold values from -6 to 6
Outputs:
- outputs: bfloat16 [256, 128, 256], P('ch', 'img')
- input_grad: bfloat16 [256, 128, 256], P('ch', 'img')
- norm_gain_grad: float32 [3, 256], P(None, 'ch')
- norm_bias_grad: float32 [3, 256], P(None, 'ch')
- conv_weight_grad: float32 [2, 9, 256, 256], P(None, None, 'ch')
- conv_bias_grad: float32 [2, 256], P(None, 'ch')
- temb_weight_grad: float32 [512, 256], P(None, 'ch')
- temb_bias_grad: float32 [256], P('ch')
- qkv_weight_grad: float32 [3, 256, 256], P(None, 'ch')
- qv_bias_grad: float32 [2, 256], P(None, 'ch')
- out_weight_grad: float32 [256, 256], P('ch')
- out_bias_grad: float32 [256], P('ch')
All inputs are finite; a program needn't handle non-finite values. No bound on the sum of `keep_mask` on one device may be relied on, other than what follows from the above.
Results may differ from a plain program's by a relative error of at most 0.04.
Values may be sent and summed in bfloat16 or wider, within the bound.
No kernel may reach another device: no remote copies, remote signals or barrier semaphores. Data moves between devices by JAX's collectives and lax.ppermute only.
A program may use at most 256 MiB of HBM per device.

v0:
```python
import math

import jax
import jax.numpy as jnp
from jax import lax
from jax.sharding import PartitionSpec as P

C = 256
TEMB = 512
GROUPS = 32
SIDE = 16


norm_eps = 1e-06


def swish(values):
    return values * jax.nn.sigmoid(values)


def swish_slope(values):
    sigma = jax.nn.sigmoid(values)
    return sigma * (1.0 + values * (1.0 - sigma))


def norm_stats(values):
    local_rows, images, positions = values.shape
    per_group = C // GROUPS
    grouped = values.reshape(local_rows // per_group, per_group, images, positions)
    average = jnp.mean(grouped, axis=(1, 3), keepdims=True)
    centered = grouped - average
    spread = jnp.mean(centered * centered, axis=(1, 3), keepdims=True)
    inverse = lax.rsqrt(spread + norm_eps)
    return ((centered * inverse).reshape(values.shape), inverse)


def norm_back(normalized, inverse, grad_out, gain_row):
    local_rows, images, positions = normalized.shape
    per_group = C // GROUPS
    gain_grad = jnp.sum(grad_out * normalized, axis=(1, 2))
    bias_grad = jnp.sum(grad_out, axis=(1, 2))
    grad_hat = (grad_out * gain_row[:, None, None]).reshape(
        local_rows // per_group, per_group, images, positions
    )
    hat_grouped = normalized.reshape(grad_hat.shape)
    first_mean = jnp.mean(grad_hat, axis=(1, 3), keepdims=True)
    second_mean = jnp.mean(grad_hat * hat_grouped, axis=(1, 3), keepdims=True)
    grad_in = inverse * (grad_hat - first_mean - hat_grouped * second_mean)
    return (grad_in.reshape(normalized.shape), gain_grad, bias_grad)


def shift_cells(values, row_step, col_step):
    margin = SIDE + 1
    positions = values.shape[2]
    padded = jnp.pad(values, ((0, 0), (0, 0), (margin, margin)))
    offset = margin + row_step * SIDE + col_step
    moved = lax.slice_in_dim(padded, offset, offset + positions, axis=2)
    column = jnp.arange(positions, dtype=jnp.int32) % SIDE + col_step
    valid = ((column >= 0) & (column < SIDE)).astype(values.dtype)
    return moved * valid


def shifted(values, tap_index, direction, kernel_taps):
    if kernel_taps == 1:
        return values
    return shift_cells(values, direction * (tap_index // 3 - 1), direction * (tap_index % 3 - 1))


def time_features(timesteps):
    half_dim = TEMB // 2
    rates = jnp.exp(-math.log(10000.0) * jnp.arange(half_dim, dtype=jnp.float32) / (half_dim - 1))
    angles = timesteps.astype(jnp.float32)[:, None] * rates[None, :]
    return jnp.concatenate([jnp.sin(angles), jnp.cos(angles)], axis=1)


def project_forward(local_acts, weight):
    groups, kernel_taps, out_rows, in_rows = weight.shape
    local_rows, images, positions = local_acts.shape
    initial = jnp.zeros((groups, out_rows, images, positions), jnp.float32)
    summed = initial
    shard_piece = lax.all_gather(local_acts, "ch", axis=0, tiled=True)
    piece_rows = shard_piece.shape[0]
    for tap_index in range(kernel_taps):
        matrix = weight[:, tap_index].reshape(groups * out_rows, piece_rows)
        moved = shifted(shard_piece, tap_index, 1, kernel_taps).reshape(
            piece_rows, images * positions
        )
        product = jnp.dot(matrix, moved, preferred_element_type=jnp.float32)
        summed = summed + product.reshape(summed.shape)
    return summed


def project_weight_grad(local_acts, gradients, kernel_taps):
    groups, out_rows, images, positions = gradients.shape
    flattened = gradients.reshape(groups * out_rows, images * positions)
    shard_piece = lax.all_gather(local_acts, "ch", axis=0, tiled=True)
    piece_rows = shard_piece.shape[0]
    blocks = []
    for tap_index in range(kernel_taps):
        moved = shifted(shard_piece, tap_index, 1, kernel_taps).reshape(
            piece_rows, images * positions
        )
        blocks.append(
            lax.dot_general(
                flattened, moved, (((1,), (1,)), ((), ())), preferred_element_type=jnp.float32
            )
        )
    return (
        jnp.stack(blocks).reshape(kernel_taps, groups, out_rows, piece_rows).transpose(1, 0, 2, 3)
    )


def project_input_grad(gradients, weight):
    groups, kernel_taps, out_rows, in_rows = weight.shape
    images = gradients.shape[2]
    positions = gradients.shape[3]
    moved_taps = [
        jnp.stack(
            [
                shifted(gradients[group_index], tap_index, -1, kernel_taps)
                for group_index in range(groups)
            ]
        ).reshape(groups * out_rows, images * positions)
        for tap_index in range(kernel_taps)
    ]
    row_count = lax.axis_size("ch") * out_rows
    total = jnp.zeros((row_count, images * positions), jnp.float32)
    for tap_index in range(kernel_taps):
        matrix = weight[:, tap_index].reshape(groups * out_rows, row_count)
        total = total + lax.dot_general(
            matrix,
            moved_taps[tap_index],
            (((0,), (0,)), ((), ())),
            preferred_element_type=jnp.float32,
        )
    return lax.psum_scatter(
        total.reshape(row_count, images, positions).astype(jnp.bfloat16),
        "ch",
        scatter_dimension=0,
        tiled=True,
    ).astype(jnp.float32)


def softmax_share(scores):
    row_max = jnp.max(scores, axis=-1, keepdims=True)
    shifted_exp = jnp.exp(scores - row_max)
    row_total = jnp.sum(shifted_exp, axis=-1, keepdims=True)
    probs_low = (shifted_exp / row_total).astype(jnp.bfloat16)
    return (probs_low, (row_max + jnp.log(row_total))[..., 0])


def score_gradient(scores, dprobs, log_total):
    probs = jnp.exp(scores - log_total[..., None])
    row_dot = jnp.sum(probs * dprobs, axis=-1, keepdims=True)
    return (probs.astype(jnp.bfloat16), (probs * (dprobs - row_dot)).astype(jnp.bfloat16))


def attend(queries, keys_proj, vals):
    local_rows, images, positions = queries.shape
    score_scale = C ** (-0.5)
    block = min(16, images)

    def one_block(carry, block_index):
        first_image = block_index * block
        query_block = lax.dynamic_slice_in_dim(queries, first_image, block, 1)
        key_block = lax.dynamic_slice_in_dim(keys_proj, first_image, block, 1)
        value_block = lax.dynamic_slice_in_dim(vals, first_image, block, 1)
        partial_scores = jnp.einsum(
            "cbp,cbj->bpj", query_block, key_block, preferred_element_type=jnp.float32
        )
        scores = (
            lax.psum_scatter(partial_scores, "ch", scatter_dimension=1, tiled=True) * score_scale
        )
        probs_share, log_total = softmax_share(scores)
        probs_low = lax.all_gather(probs_share, "ch", axis=1, tiled=True)
        mixed = jnp.einsum(
            "cbj,bpj->cbp", value_block, probs_low, preferred_element_type=jnp.float32
        ).astype(jnp.bfloat16)
        return (carry, (mixed, log_total))

    unused, (mixed_blocks, log_totals) = lax.scan(
        one_block, jnp.zeros((), jnp.int32), jnp.arange(images // block, dtype=jnp.int32)
    )
    attended = mixed_blocks.transpose(1, 0, 2, 3).reshape(local_rows, images, positions)
    return (attended, log_totals)


def attend_back(queries, keys_proj, vals, attended_grad, log_totals):
    local_rows, images, positions = queries.shape
    score_scale = C ** (-0.5)
    block = min(16, images)

    def one_block(carry, block_index):
        first_image = block_index * block
        query_block = lax.dynamic_slice_in_dim(queries, first_image, block, 1)
        key_block = lax.dynamic_slice_in_dim(keys_proj, first_image, block, 1)
        value_block = lax.dynamic_slice_in_dim(vals, first_image, block, 1)
        grad_block = lax.dynamic_slice_in_dim(attended_grad, first_image, block, 1)
        log_total = log_totals[block_index]
        partial_scores = jnp.einsum(
            "cbp,cbj->bpj", query_block, key_block, preferred_element_type=jnp.float32
        )
        partial_dprobs = jnp.einsum(
            "cbp,cbj->bpj", grad_block, value_block, preferred_element_type=jnp.float32
        )
        scores, dprobs = (
            lax.psum_scatter(partial_scores, "ch", scatter_dimension=1, tiled=True),
            lax.psum_scatter(partial_dprobs, "ch", scatter_dimension=1, tiled=True),
        )
        probs_share, dscore_share = score_gradient(scores * score_scale, dprobs, log_total)
        probs_low, dscores = (
            lax.all_gather(probs_share, "ch", axis=1, tiled=True),
            lax.all_gather(dscore_share, "ch", axis=1, tiled=True),
        )
        query_grad = score_scale * jnp.einsum(
            "cbj,bpj->cbp", key_block, dscores, preferred_element_type=jnp.float32
        )
        key_grad = score_scale * jnp.einsum(
            "cbp,bpj->cbj", query_block, dscores, preferred_element_type=jnp.float32
        )
        value_grad = jnp.einsum(
            "cbp,bpj->cbj", grad_block, probs_low, preferred_element_type=jnp.float32
        )
        return (carry, jnp.stack([query_grad, key_grad, value_grad]).astype(jnp.bfloat16))

    unused, grad_blocks = lax.scan(
        one_block, jnp.zeros((), jnp.int32), jnp.arange(images // block, dtype=jnp.int32)
    )
    return grad_blocks.transpose(1, 2, 0, 3, 4).reshape(3, local_rows, images, positions)


def run_block(source, keep_scale, cotangent, timesteps, params):
    (
        norm_gain,
        norm_bias,
        conv_weight,
        conv_bias,
        temb_weight,
        temb_bias,
        qkv_weight,
        qv_bias,
        out_weight,
        out_bias,
    ) = params
    highest = lax.Precision.HIGHEST
    hat_one, inverse_one = norm_stats(source)
    pre_one = hat_one * norm_gain[0][:, None, None] + norm_bias[0][:, None, None]
    first_act = swish(pre_one).astype(jnp.bfloat16)
    conv_one = project_forward(first_act, conv_weight[0][None])[0]
    swished_time = swish(time_features(timesteps))
    offsets = (
        jnp.dot(swished_time, temb_weight.astype(jnp.float32), precision=highest)
        + temb_bias[None, :]
    )
    middle = conv_one + conv_bias[0][:, None, None] + offsets.T[:, :, None]
    hat_two, inverse_two = norm_stats(middle)
    pre_two = hat_two * norm_gain[1][:, None, None] + norm_bias[1][:, None, None]
    second_act = (swish(pre_two) * keep_scale).astype(jnp.bfloat16)
    conv_two = project_forward(second_act, conv_weight[1][None])[0]
    residual = source + conv_two + conv_bias[1][:, None, None]
    hat_three, inverse_three = norm_stats(residual)
    normed = (hat_three * norm_gain[2][:, None, None] + norm_bias[2][:, None, None]).astype(
        jnp.bfloat16
    )
    projected = project_forward(normed, qkv_weight[:, None])
    queries = (projected[0] + qv_bias[0][:, None, None]).astype(jnp.bfloat16)
    keys_proj = projected[1].astype(jnp.bfloat16)
    vals = (projected[2] + qv_bias[1][:, None, None]).astype(jnp.bfloat16)
    attended, log_totals = attend(queries, keys_proj, vals)
    out_proj = project_forward(attended, out_weight[None, None])[0]
    outputs = (residual + out_proj + out_bias[:, None, None]).astype(jnp.bfloat16)
    cot_float = cotangent.astype(jnp.float32)
    out_bias_grad = jnp.sum(cot_float, axis=(1, 2))
    out_weight_grad = project_weight_grad(attended, cotangent[None], 1)[0, 0]
    attended_grad = project_input_grad(cotangent[None], out_weight[None, None]).astype(jnp.bfloat16)
    qkv_grads = attend_back(queries, keys_proj, vals, attended_grad, log_totals)
    qkv_float = qkv_grads.astype(jnp.float32)
    qv_bias_grad = jnp.stack(
        [jnp.sum(qkv_float[0], axis=(1, 2)), jnp.sum(qkv_float[2], axis=(1, 2))]
    )
    qkv_weight_grad = project_weight_grad(normed, qkv_grads, 1)[:, 0]
    normed_grad = project_input_grad(qkv_grads, qkv_weight[:, None])
    branch_three, gain_three, bias_three = norm_back(
        hat_three, inverse_three, normed_grad, norm_gain[2]
    )
    residual_grad = cot_float + branch_three
    conv_two_bias = jnp.sum(residual_grad, axis=(1, 2))
    residual_low = residual_grad.astype(jnp.bfloat16)[None]
    conv_two_grad = project_weight_grad(second_act, residual_low, 9)[0]
    second_grad = project_input_grad(residual_low, conv_weight[1][None])
    pre_two_grad = second_grad * keep_scale * swish_slope(pre_two)
    middle_grad, gain_two, bias_two = norm_back(hat_two, inverse_two, pre_two_grad, norm_gain[1])
    conv_one_bias = jnp.sum(middle_grad, axis=(1, 2))
    offsets_grad = jnp.sum(middle_grad, axis=2).T
    temb_bias_grad = jnp.sum(offsets_grad, axis=0)
    temb_weight_grad = jnp.dot(swished_time.T, offsets_grad, precision=highest)
    middle_low = middle_grad.astype(jnp.bfloat16)[None]
    conv_one_grad = project_weight_grad(first_act, middle_low, 9)[0]
    first_grad = project_input_grad(middle_low, conv_weight[0][None])
    pre_one_grad = first_grad * swish_slope(pre_one)
    branch_one, gain_one, bias_one = norm_back(hat_one, inverse_one, pre_one_grad, norm_gain[0])
    input_grad = (residual_grad + branch_one).astype(jnp.bfloat16)
    grads = (
        jnp.stack([gain_one, gain_two, gain_three]),
        jnp.stack([bias_one, bias_two, bias_three]),
        jnp.stack([conv_one_grad, conv_two_grad]),
        jnp.stack([conv_one_bias, conv_two_bias]),
        temb_weight_grad,
        temb_bias_grad,
        qkv_weight_grad,
        qv_bias_grad,
        out_weight_grad,
        out_bias_grad,
    )
    return (outputs, input_grad, grads)


def on_device(
    inputs,
    timesteps,
    keep_mask,
    norm_gain,
    norm_bias,
    conv_weight,
    conv_bias,
    temb_weight,
    temb_bias,
    qkv_weight,
    qv_bias,
    out_weight,
    out_bias,
    cotangent,
):
    keep_scale = keep_mask.astype(jnp.float32) * (1.0 / 0.9)
    params = (
        norm_gain,
        norm_bias,
        conv_weight,
        conv_bias,
        temb_weight,
        temb_bias,
        qkv_weight,
        qv_bias,
        out_weight,
        out_bias,
    )
    outputs, input_grad, grads = run_block(
        inputs.astype(jnp.float32), keep_scale, cotangent, timesteps, params
    )
    summed = (
        lax.psum(grads[0].astype(jnp.bfloat16), "img").astype(jnp.float32),
        lax.psum(grads[1].astype(jnp.bfloat16), "img").astype(jnp.float32),
        lax.psum(grads[2].astype(jnp.bfloat16), "img").astype(jnp.float32),
        lax.psum(grads[3].astype(jnp.bfloat16), "img").astype(jnp.float32),
        lax.psum(grads[4].astype(jnp.bfloat16), "img").astype(jnp.float32),
        lax.psum(grads[5].astype(jnp.bfloat16), "img").astype(jnp.float32),
        lax.psum(grads[6].astype(jnp.bfloat16), "img").astype(jnp.float32),
        lax.psum(grads[7].astype(jnp.bfloat16), "img").astype(jnp.float32),
        lax.psum(grads[8].astype(jnp.bfloat16), "img").astype(jnp.float32),
        lax.psum(grads[9].astype(jnp.bfloat16), "img").astype(jnp.float32),
    )
    return (
        outputs,
        input_grad,
        summed[0],
        summed[1],
        summed[2],
        summed[3],
        summed[4],
        summed[5],
        summed[6],
        summed[7],
        summed[8],
        summed[9],
    )


def solution(mesh):
    placed = (
        P("ch", "img", None),
        P("img"),
        P("ch", "img", None),
        P(None, "ch"),
        P(None, "ch"),
        P(None, None, "ch", None),
        P(None, "ch"),
        P(None, "ch"),
        P("ch"),
        P(None, "ch", None),
        P(None, "ch"),
        P("ch", None),
        P("ch"),
        P("ch", "img", None),
    )
    return jax.shard_map(
        on_device,
        mesh=mesh,
        in_specs=placed,
        out_specs=(
            P("ch", "img", None),
            P("ch", "img", None),
            P(None, "ch"),
            P(None, "ch"),
            P(None, None, "ch", None),
            P(None, "ch"),
            P(None, "ch"),
            P("ch"),
            P(None, "ch", None),
            P(None, "ch"),
            P("ch", None),
            P("ch"),
        ),
        check_vma=False,
    )
```

profile of v0, /device:TPU:1, one launch (start us, length us, event | category | flops | bytes accessed | tf_op | source)
XLA Modules:
  0.0 3028.6 jit_solution(16284734036737890888)
XLA Ops:
  16.0 80.8 %all-gather.8.cloned.1.call-done = bf16[256,32,256]{2,1,0:T(8,128)(2,1)} async-done(((bf16[8,32,256]{2,1,0:T(8,128)(2,1)}), bf16[256,32,256]{2,1,0:T(8,128)(2,1)}) %all-gather.8.cloned.1.call-update) | async-done | bytes 4194320 | tf_op jit(solution)/shard_map/all_gather | solution.py:81
  96.8 32.6 %fusion.46 = (bf16[256,32,256]{2,1,0:T(8,128)(2,1)S(1)}, bf16[256,32,256]{2,1,0:T(8,128)(2,1)}, bf16[256,32,256]{2,1,0:T(8,128)(2,1)}, bf16[256,32,256]{2,1,0:T(...) fusion(bf16[256,32,256]{2,1,0:T(8,128)(2,1)} %all-gather.8.clon, ...), kind=kLoop, calls=%fused_computation.109 | loop fusion | flops 62914560 | bytes 41944576 | tf_op jit(solution)/shard_map/mul | solution.py:60
  129.5 10.0 copy.217
  193.6 79.4 %all-gather.10.cloned.1.call-done = bf16[256,32,256]{2,1,0:T(8,128)(2,1)} async-done(((bf16[8,32,256]{2,1,0:T(8,128)(2,1)}), bf16[256,32,256]{2,1,0:T(8,128)(2,1)}) %all-gather.10.cloned.1.call-update) | async-done | bytes 4194320 | tf_op jit(solution)/shard_map/all_gather | solution.py:81
  273.0 33.0 %fusion.54 = (bf16[256,32,256]{2,1,0:T(8,128)(2,1)S(1)}, bf16[256,32,256]{2,1,0:T(8,128)(2,1)}, bf16[256,32,256]{2,1,0:T(8,128)(2,1)}, bf16[256,32,256]{2,1,0:T(...) fusion(bf16[256,32,256]{2,1,0:T(8,128)(2,1)} %all-gather.10.clo, ...), kind=kLoop, calls=%fused_computation.117 | loop fusion | flops 62914560 | bytes 41944576 | tf_op jit(solution)/shard_map/mul | solution.py:60
  306.1 8.0 copy.228
  373.3 74.7 %all-gather.12.cloned.1.call-done = bf16[256,32,256]{2,1,0:T(8,128)(2,1)} async-done(((bf16[8,32,256]{2,1,0:T(8,128)(2,1)}), bf16[256,32,256]{2,1,0:T(8,128)(2,1)}) %all-gather.12.cloned.1.call-update) | async-done | bytes 4194320 | tf_op jit(solution)/shard_map/all_gather | solution.py:81
  455.4 162.8 %reduce-scatter.16.cloned.1.call-done = bf16[8,8192]{1,0:T(8,128)(2,1)} async-done(((bf16[256,8192]{1,0:T(8,128)(2,1)}), bf16[8,8192]{1,0:T(8,128)(2,1)}) %reduce-scatter.16.cloned.1.call-update) | async-done | bytes 131088
  618.2 561.2 %while.22 = (s32[]{:T(128)}, bf16[2,8,16,256]{3,1,2,0:T(8,128)(2,1)S(1)}, f32[2,16,8]{1,2,0:T(8,128)S(1)}, s32[2]{0:T(128)S(1)}, bf16[8,32,256]{2,0,1:T(8,128)(2...) while((s32[]{:T(128)}, ...), condition=%wide.region_12.13_spmd, body=%wide.region_8.0_spmd.sunk | while | flops 33881988 | bytes 26491148 | solution.py:181
  622.2 186.7 %reduce-scatter.18.cloned.1.call-done = f32[16,8,256]{2,1,0:T(8,128)} async-done(((f32[16,256,256]{2,1,0:T(8,128)}), f32[16,8,256]{2,1,0:T(8,128)}) %reduce-scatter.18.cloned.1.call-update) | async-done | bytes 131088 | tf_op jit(solution)/shard_map/while/body/eval_jaxpr/reduce_scatter | solution.py:172
  812.8 93.1 %all-gather.16.cloned.1.call-done = bf16[16,256,256]{2,1,0:T(8,128)(2,1)} async-done(((bf16[16,8,256]{2,1,0:T(8,128)(2,1)}), bf16[16,256,256]{2,1,0:T(8,128)(2,1)}) %all-gather.16.cloned.1.call-update) | async-done | bytes 2097168 | tf_op jit(solution)/shard_map/while/body/eval_jaxpr/all_gather | solution.py:175
  912.2 167.8 %reduce-scatter.18.cloned.1.call-done = f32[16,8,256]{2,1,0:T(8,128)} async-done(((f32[16,256,256]{2,1,0:T(8,128)}), f32[16,8,256]{2,1,0:T(8,128)}) %reduce-scatter.18.cloned.1.call-update) | async-done | bytes 131088 | tf_op jit(solution)/shard_map/while/body/eval_jaxpr/reduce_scatter | solution.py:172
  1083.8 93.4 %all-gather.16.cloned.1.call-done = bf16[16,256,256]{2,1,0:T(8,128)(2,1)} async-done(((bf16[16,8,256]{2,1,0:T(8,128)(2,1)}), bf16[16,256,256]{2,1,0:T(8,128)(2,1)}) %all-gather.16.cloned.1.call-update) | async-done | bytes 2097168 | tf_op jit(solution)/shard_map/while/body/eval_jaxpr/all_gather | solution.py:175
  1180.1 1075.2 %while.23 = (s32[]{:T(128)}, bf16[2,3,8,16,256]{4,2,3,1,0:T(8,128)(2,1)S(1)}, s32[2]{0:T(128)S(1)}, bf16[8,32,256]{2,0,1:T(8,128)(2,1)S(1)}, bf16[8,32,256]{2,0,...) while((s32[]{:T(128)}, ...), condition=%wide.region_18.19_spmd, body=%wide.region_14.18_spmd.sunk | while | flops 85000576 | bytes 55186836 | solution.py:226
  1189.0 163.3 %reduce-scatter.20.cloned.1.call-done = f32[16,8,256]{2,1,0:T(8,128)} async-done(((f32[16,256,256]{2,1,0:T(8,128)}), f32[16,8,256]{2,1,0:T(8,128)}) %reduce-scatter.20.cloned.1.call-update) | async-done | bytes 131088 | tf_op jit(solution)/shard_map/while/body/eval_jaxpr/reduce_scatter | solution.py:207
  1352.3 189.7 %reduce-scatter.22.cloned.1.call-done = f32[16,8,256]{2,1,0:T(8,128)} async-done(((f32[16,256,256]{2,1,0:T(8,128)}), f32[16,8,256]{2,1,0:T(8,128)}) %reduce-scatter.22.cloned.1.call-update) | async-done | bytes 131088 | tf_op jit(solution)/shard_map/while/body/eval_jaxpr/reduce_scatter | solution.py:208
  1546.0 92.3 %all-gather.20.cloned.1.call-done = bf16[16,256,256]{2,1,0:T(8,128)(2,1)} async-done(((bf16[16,8,256]{2,1,0:T(8,128)(2,1)}), bf16[16,256,256]{2,1,0:T(8,128)(2,1)}) %all-gather.20.cloned.1.call-update) | async-done | bytes 2097168 | tf_op jit(solution)/shard_map/while/body/eval_jaxpr/all_gather | solution.py:213
  1642.6 73.1 %all-gather.18.cloned.1.call-done = bf16[16,256,256]{2,1,0:T(8,128)(2,1)} async-done(((bf16[16,8,256]{2,1,0:T(8,128)(2,1)}), bf16[16,256,256]{2,1,0:T(8,128)(2,1)}) %all-gather.18.cloned.1.call-update) | async-done | bytes 2097168 | tf_op jit(solution)/shard_map/while/body/eval_jaxpr/all_gather | solution.py:212
  1726.6 163.3 %reduce-scatter.20.cloned.1.call-done = f32[16,8,256]{2,1,0:T(8,128)} async-done(((f32[16,256,256]{2,1,0:T(8,128)}), f32[16,8,256]{2,1,0:T(8,128)}) %reduce-scatter.20.cloned.1.call-update) | async-done | bytes 131088 | tf_op jit(solution)/shard_map/while/body/eval_jaxpr/reduce_scatter | solution.py:207
  1889.9 189.6 %reduce-scatter.22.cloned.1.call-done = f32[16,8,256]{2,1,0:T(8,128)} async-done(((f32[16,256,256]{2,1,0:T(8,128)}), f32[16,8,256]{2,1,0:T(8,128)}) %reduce-scatter.22.cloned.1.call-update) | async-done | bytes 131088 | tf_op jit(solution)/shard_map/while/body/eval_jaxpr/reduce_scatter | solution.py:208
  2083.6 92.4 %all-gather.20.cloned.1.call-done = bf16[16,256,256]{2,1,0:T(8,128)(2,1)} async-done(((bf16[16,8,256]{2,1,0:T(8,128)(2,1)}), bf16[16,256,256]{2,1,0:T(8,128)(2,1)}) %all-gather.20.cloned.1.call-update) | async-done | bytes 2097168 | tf_op jit(solution)/shard_map/while/body/eval_jaxpr/all_gather | solution.py:213
  2180.2 73.1 %all-gather.18.cloned.1.call-done = bf16[16,256,256]{2,1,0:T(8,128)(2,1)} async-done(((bf16[16,8,256]{2,1,0:T(8,128)(2,1)}), bf16[16,256,256]{2,1,0:T(8,128)(2,1)}) %all-gather.18.cloned.1.call-update) | async-done | bytes 2097168 | tf_op jit(solution)/shard_map/while/body/eval_jaxpr/all_gather | solution.py:212
  2259.3 7.9 copy.173
  2267.3 84.2 %all-gather.14.cloned.1.call-done = bf16[256,32,256]{2,0,1:T(8,128)(2,1)} async-done(((bf16[8,32,256]{2,0,1:T(8,128)(2,1)}), bf16[256,32,256]{2,0,1:T(8,128)(2,1)}) %all-gather.14.cloned.1.call-update) | async-done | bytes 4194320 | tf_op jit(solution)/shard_map/all_gather | solution.py:81
  2361.8 159.3 %reduce-scatter.10.cloned.1.call-done = bf16[8,32,256]{2,1,0:T(8,128)(2,1)} async-done(((bf16[256,32,256]{2,1,0:T(8,128)(2,1)}), bf16[8,32,256]{2,1,0:T(8,128)(2,1)}) %reduce-scatter.10.cloned.1.call-update) | async-done | bytes 131088 | tf_op jit(solution)/shard_map/reduce_scatter | solution.py:136
  2539.3 7.9 copy.174
  2547.3 187.0 %reduce-scatter.12.cloned.1.call-done = bf16[8,32,256]{2,1,0:T(8,128)(2,1)} async-done(((bf16[256,32,256]{2,1,0:T(8,128)(2,1)}), bf16[8,32,256]{2,1,0:T(8,128)(2,1)}) %reduce-scatter.12.cloned.1.call-update) | async-done | bytes 131088 | tf_op jit(solution)/shard_map/reduce_scatter | solution.py:136
  2751.6 7.9 copy.175
  2760.0 7.4 reshape.639
  2862.3 85.0 %reduce-scatter.14.cloned.1.call-done = bf16[8,32,256]{2,1,0:T(8,128)(2,1)} async-done(((bf16[256,32,256]{2,1,0:T(8,128)(2,1)}), bf16[8,32,256]{2,1,0:T(8,128)(2,1)}) %reduce-scatter.14.cloned.1.call-update) | async-done | bytes 131088 | tf_op jit(solution)/shard_map/reduce_scatter | solution.py:136
  2948.7 54.9 %all-reduce.7.cloned.1.call-done = bf16[2,9,8,256]{3,2,1,0:T(8,128)(2,1)} async-done(((bf16[2,9,8,256]{3,2,1,0:T(8,128)(2,1)}), bf16[2,9,8,256]{3,2,1,0:T(8,128)(2,1)}) %all-reduce.7.cloned.1.call-update) | async-done | bytes 73744 | tf_op jit(solution)/shard_map/psum | solution.py:353
  3005.2 10.4 all-reduce.4
  (415 shorter events, 335.2 us)
Async XLA Ops:
  7.2 447.3 %copy-start = (bf16[3,8,256]{2,1,0:T(8,128)(2,1)S(1)}, bf16[3,8,256]{2,1,0:T(8,128)(2,1)}, u32[]{:S(2)}) copy-start(bf16[3,8,256]{2,1,0:T(8,128)(2,1)} %param.27) | copy-start | bytes 36868
  7.2 89.6 %all-gather.8.cloned.1.call-start = ((), (), s32[]{:S(2)}) async-start(), calls=%async_computation.7 | async-start | bytes 4325376 | tf_op jit(solution)/shard_map/all_gather | solution.py:81
  10.3 182.3 %copy-start.62 = (f32[8]{0:T(128)}, f32[8]{0:T(128)S(1)}, u32[]{:S(2)}) copy-start(f32[8]{0:T(128)S(1)} %get-tuple-element.236) | copy-start | bytes 100
  12.5 260.5 %all-gather.10.cloned.1.call-start = ((), (), s32[]{:S(2)}) async-start(), calls=%async_computation.8 | async-start | bytes 4325376 | tf_op jit(solution)/shard_map/all_gather | solution.py:81
  193.5 254.5 %all-gather.12.cloned.1.call-start = ((), (), s32[]{:S(2)}) async-start(), calls=%async_computation.9 | async-start | bytes 4325376 | tf_op jit(solution)/shard_map/all_gather | solution.py:81
  368.5 249.6 %reduce-scatter.16.cloned.1.call-start = ((), (), s32[]{:S(2)}) async-start(), calls=%async_computation.15 | async-start | bytes 4325376
  618.2 561.3 %copy-start.44 = (bf16[8,8192]{1,0:T(8,128)(2,1)S(1)}, bf16[8,8192]{1,0:T(8,128)(2,1)}, u32[]{:S(2)}) copy-start(bf16[8,8192]{1,0:T(8,128)(2,1)} %reduce-scatter.16.cloned.1.call-done) | copy-start | bytes 393220
  618.2 190.8 %reduce-scatter.18.cloned.1.call-start = ((), (), s32[]{:S(2)}) async-start(), calls=%async_computation.16 | async-start | bytes 4325376 | tf_op jit(solution)/shard_map/while/body/eval_jaxpr/reduce_scatter | solution.py:172
  622.2 283.7 %all-gather.16.cloned.1.call-start = ((), (), s32[]{:S(2)}) async-start(), calls=%async_computation.17 | async-start | bytes 2162688 | tf_op jit(solution)/shard_map/while/body/eval_jaxpr/all_gather | solution.py:175
  908.1 171.9 %reduce-scatter.18.cloned.1.call-start = ((), (), s32[]{:S(2)}) async-start(), calls=%async_computation.16 | async-start | bytes 4325376 | tf_op jit(solution)/shard_map/while/body/eval_jaxpr/reduce_scatter | solution.py:172
  912.1 265.1 %all-gather.16.cloned.1.call-start = ((), (), s32[]{:S(2)}) async-start(), calls=%async_computation.17 | async-start | bytes 2162688 | tf_op jit(solution)/shard_map/while/body/eval_jaxpr/all_gather | solution.py:175
  1180.1 172.2 %reduce-scatter.20.cloned.1.call-start = ((), (), s32[]{:S(2)}) async-start(), calls=%async_computation.18 | async-start | bytes 4325376 | tf_op jit(solution)/shard_map/while/body/eval_jaxpr/reduce_scatter | solution.py:207
  1184.1 357.9 %reduce-scatter.22.cloned.1.call-start = ((), (), s32[]{:S(2)}) async-start(), calls=%async_computation.20 | async-start | bytes 4325376 | tf_op jit(solution)/shard_map/while/body/eval_jaxpr/reduce_scatter | solution.py:208
  1186.9 451.4 %all-gather.20.cloned.1.call-start = ((), (), s32[]{:S(2)}) async-start(), calls=%async_computation.21 | async-start | bytes 2162688 | tf_op jit(solution)/shard_map/while/body/eval_jaxpr/all_gather | solution.py:213
  1544.3 171.3 %all-gather.18.cloned.1.call-start = ((), (), s32[]{:S(2)}) async-start(), calls=%async_computation.19 | async-start | bytes 2162688 | tf_op jit(solution)/shard_map/while/body/eval_jaxpr/all_gather | solution.py:212
  1717.7 172.2 %reduce-scatter.20.cloned.1.call-start = ((), (), s32[]{:S(2)}) async-start(), calls=%async_computation.18 | async-start | bytes 4325376 | tf_op jit(solution)/shard_map/while/body/eval_jaxpr/reduce_scatter | solution.py:207
  1721.7 357.8 %reduce-scatter.22.cloned.1.call-start = ((), (), s32[]{:S(2)}) async-start(), calls=%async_computation.20 | async-start | bytes 4325376 | tf_op jit(solution)/shard_map/while/body/eval_jaxpr/reduce_scatter | solution.py:208
  1724.6 451.4 %all-gather.20.cloned.1.call-start = ((), (), s32[]{:S(2)}) async-start(), calls=%async_computation.21 | async-start | bytes 2162688 | tf_op jit(solution)/shard_map/while/body/eval_jaxpr/all_gather | solution.py:213
  2081.8 171.4 %all-gather.18.cloned.1.call-start = ((), (), s32[]{:S(2)}) async-start(), calls=%async_computation.19 | async-start | bytes 2162688 | tf_op jit(solution)/shard_map/while/body/eval_jaxpr/all_gather | solution.py:212
  2255.3 96.2 %all-gather.14.cloned.1.call-start = ((), (), s32[]{:S(2)}) async-start(), calls=%async_computation.10 | async-start | bytes 4325376 | tf_op jit(solution)/shard_map/all_gather | solution.py:81
  2255.9 265.2 %reduce-scatter.10.cloned.1.call-start = ((), (), s32[]{:S(2)}) async-start(), calls=%async_computation.11 | async-start | bytes 4325376 | tf_op jit(solution)/shard_map/reduce_scatter | solution.py:136
  2267.2 467.1 %reduce-scatter.12.cloned.1.call-start = ((), (), s32[]{:S(2)}) async-start(), calls=%async_computation.12 | async-start | bytes 4325376 | tf_op jit(solution)/shard_map/reduce_scatter | solution.py:136
  2547.2 187.2 %copy-start.41 = (f32[8192,8]{0,1:T(8,128)S(1)}, f32[8192,8]{0,1:T(8,128)}, u32[]{:S(2)}) copy-start(f32[8192,8]{0,1:T(8,128)} %copy-done.40) | copy-start | bytes 786436
  2547.2 187.2 %copy-start.48 = (s32[8,32,256]{2,1,0:T(8,128)S(1)}, s32[8,32,256]{2,1,0:T(8,128)}, u32[]{:S(2)}) copy-start(s32[8,32,256]{2,1,0:T(8,128)} %param.20) | copy-start | bytes 786436
  2547.2 187.2 %copy-start.52 = (f32[8,32]{1,0:T(8,128)S(1)}, f32[8,32]{1,0:T(8,128)}, u32[]{:S(2)}) copy-start(f32[8,32]{1,0:T(8,128)} %copy-done.51) | copy-start | bytes 3076
  2547.2 187.2 %copy-start.58 = (f32[8]{0:T(128)S(1)}, f32[8]{0:T(128)}, u32[]{:S(2)}) copy-start(f32[8]{0:T(128)} %copy-done.57) | copy-start | bytes 100
  2547.2 187.2 %copy-start.61 = (f32[32]{0:T(128)S(1)}, f32[32]{0:T(128)}, u32[]{:S(2)}) copy-start(f32[32]{0:T(128)} %copy-done.60) | copy-start | bytes 388
  2547.2 187.2 %copy-start.63 = (f32[8]{0:T(128)S(1)}, f32[8]{0:T(128)}, u32[]{:S(2)}) copy-start(f32[8]{0:T(128)} %copy-done.62) | copy-start | bytes 100
  2547.2 187.2 %copy-start.69 = (f32[32]{0:T(128)S(1)}, f32[32]{0:T(128)}, u32[]{:S(2)}) copy-start(f32[32]{0:T(128)} %copy-done.68) | copy-start | bytes 388
  2547.2 187.2 %copy-start.73 = (f32[8]{0:T(128)S(1)}, f32[8]{0:T(128)}, u32[]{:S(2)}) copy-start(f32[8]{0:T(128)} %copy-done.72) | copy-start | bytes 100
  2547.3 400.0 %reduce-scatter.14.cloned.1.call-start = ((), (), s32[]{:S(2)}) async-start(), calls=%async_computation.13 | async-start | bytes 4325376 | tf_op jit(solution)/shard_map/reduce_scatter | solution.py:136
  2759.5 244.1 %all-reduce.7.cloned.1.call-start = ((), (), s32[]{:S(2)}) async-start(), calls=%async_computation.14 | async-start | bytes 147456 | tf_op jit(solution)/shard_map/psum | solution.py:353
  (67 other events, 2196.6 us)
Sparse Core Ops, SparseCore 0:
  12.6 84.1 all-gather.7
  193.7 79.3 all-gather.9
  368.6 79.3 all-gather.11
  450.2 167.8 reduce-scatter.15
  622.3 186.5 reduce-scatter.17
  812.8 92.9 all-gather.15
  912.2 167.6 reduce-scatter.17
  1083.8 93.3 all-gather.15
  1184.2 167.9 reduce-scatter.19
  1354.6 187.3 reduce-scatter.21
  1545.8 92.5 all-gather.19
  1642.0 73.6 all-gather.17
  1721.9 167.9 reduce-scatter.19
  1892.3 187.2 reduce-scatter.21
  2083.1 92.8 all-gather.19
  2179.6 73.6 all-gather.17
  2259.1 92.2 all-gather.13
  2353.7 167.3 reduce-scatter.9
  2547.4 186.9 reduce-scatter.11
  2759.6 187.6 reduce-scatter.13
  2950.3 53.2 all-reduce.6
where the time goes:
time: 3030 us
  waiting for transfers between devices  2550 us (84%)
  matrix products  181 us (6%)
  local copies, waits for them, and re-layouts  163 us (5%)
  other arithmetic  104 us (3%)
    reduce_scatter x4, waiting for transfers between devices, one_block(): lax.psum_scatter(partial_scores, 'ch', scatter_dimension=1, tiled=True)  681 us
    reduce_scatter x3, waiting for transfers between devices, project_input_grad(): lax.psum_scatter(total.reshape(row_count, images, positions).astype(jnp.b...  431 us
    reduce_scatter x2, waiting for transfers between devices, one_block(): lax.psum_scatter(partial_dprobs, 'ch', scatter_dimension=1, tiled=True)  379 us
    all_gather x4, waiting for transfers between devices, project_forward(): shard_piece = lax.all_gather(local_acts, 'ch', axis=0, tiled=True)  319 us
    all_gather x2, waiting for transfers between devices, one_block(): probs_low = lax.all_gather(probs_share, 'ch', axis=1, tiled=True)  186 us
    all_gather x2, waiting for transfers between devices, one_block(): lax.all_gather(dscore_share, 'ch', axis=1, tiled=True)  185 us
    unnamed x10, waiting for transfers between devices  163 us
    all_gather x2, waiting for transfers between devices, one_block(): lax.all_gather(probs_share, 'ch', axis=1, tiled=True)  146 us
  transfers between devices with their start and end apart: 21, of which 21 were waited for; matrix products, arithmetic and copies ran while one was open for 5% of the time, Pallas kernels for 0%

commit v1 on v0

v1 whole, which is shorter than its diff:
```python
import functools
import math

import jax
import jax.numpy as jnp
from jax import lax
from jax.experimental import pallas as pl
from jax.experimental.pallas import tpu as pltpu
from jax.sharding import PartitionSpec as P

C = 256
TEMB = 512
SIDE = 16
POS = 256
SHARDS = 32
ROWS = C // SHARDS
HALF = 128
WBLOCKS = 22
WROWS = WBLOCKS * ROWS
NORM_EPS = 1e-06
GROUP_SIZE = ROWS * POS
F32 = jnp.float32
BF16 = jnp.bfloat16

OFFSETS, GAINS, BIASES, CONV_BIAS, QV_BIAS, OUT_BIAS = 0, 1, 4, 7, 9, 11
D_GAINS, D_BIASES, D_CONV_BIAS, D_QV_BIAS, D_OUT_BIAS = 0, 3, 6, 8, 10
PART = 16


def dot_nn(a, b):
    return lax.dot_general(a, b, (((1,), (0,)), ((), ())), preferred_element_type=F32)


def dot_nt(a, b):
    return lax.dot_general(a, b, (((1,), (1,)), ((), ())), preferred_element_type=F32)


def dot_tn(a, b):
    return lax.dot_general(a, b, (((0,), (0,)), ((), ())), preferred_element_type=F32)


def group_sum(values):
    column = jnp.sum(values, axis=1, keepdims=True)
    return group_column(column)


def group_column(column):
    grouped = column.reshape(SHARDS, ROWS, 1)
    total = jnp.sum(grouped, axis=1, keepdims=True)
    return jnp.broadcast_to(total, grouped.shape).reshape(C, 1)


def norm_hat(values):
    average = group_sum(values) * (1.0 / GROUP_SIZE)
    centered = values - average
    spread = group_sum(centered * centered) * (1.0 / GROUP_SIZE)
    inverse = lax.rsqrt(spread + NORM_EPS)
    return centered * inverse, inverse


def norm_back(hat, inverse, grad_out, gain):
    gain_grad = jnp.sum(grad_out * hat, axis=1, keepdims=True)
    bias_grad = jnp.sum(grad_out, axis=1, keepdims=True)
    first_mean = group_column(bias_grad * gain) * (1.0 / GROUP_SIZE)
    second_mean = group_column(gain_grad * gain) * (1.0 / GROUP_SIZE)
    grad_in = inverse * (grad_out * gain - first_mean - hat * second_mean)
    return grad_in, gain_grad, bias_grad


def sigmoid(values):
    return 1.0 / (1.0 + jnp.exp(-values))


def tap_steps(tap):
    return tap // 3 - 1, tap % 3 - 1


def shifted(values, row_step, col_step, axis):
    if row_step == 0 and col_step == 0:
        return values
    moved = pltpu.roll(values, (-(row_step * SIDE + col_step)) % POS, axis)
    shape = (1, POS) if axis == 1 else (POS, POS)
    cell = lax.broadcasted_iota(jnp.int32, shape, axis)
    valid = None
    if col_step:
        column = (cell & (SIDE - 1)) + col_step
        valid = (column >= 0) & (column < SIDE)
    if row_step:
        row = cell + row_step * SIDE
        inside = (row >= 0) & (row < POS)
        valid = inside if valid is None else valid & inside
    return moved * valid.astype(F32)


def block_kernel(
    core_ref, recv_ref, other_ref, send_ref, swap_ref, weights, taps_one, taps_two, back
):
    first_core = core_ref[0] == 0

    for pair in range(WBLOCKS // 2):
        mine = recv_ref[:, 16 * pair : 16 * pair + 16, :].astype(F32)
        theirs = other_ref[:, 16 * pair : 16 * pair + 16, :].astype(F32)
        for part in range(2):
            rows = slice(ROWS * part, ROWS * part + ROWS)
            a = mine[:, rows, :].reshape(C, HALF)
            b = theirs[:, rows, :].reshape(C, HALF)
            weights[2 * pair + part, :, 0:HALF] = jnp.where(first_core, a, b).astype(BF16)
            weights[2 * pair + part, :, HALF:C] = jnp.where(first_core, b, a).astype(BF16)

    def image(at):
        block = recv_ref[:, at : at + 16, :].astype(F32)
        left = block[:, 0:ROWS, :].reshape(C, HALF)
        right = block[:, ROWS : 2 * ROWS, :].reshape(C, HALF)
        return jnp.concatenate([left, right], axis=1)

    source = image(WROWS)
    keep = image(WROWS + 16) * (1.0 / 0.9)
    cotangent = image(WROWS + 32)
    columns = recv_ref[:, WROWS + 48 : WROWS + 56, :].astype(F32).reshape(C, HALF)

    def param(lane):
        high = columns[:, lane : lane + 1]
        middle_part = columns[:, PART + lane : PART + lane + 1]
        low = columns[:, 2 * PART + lane : 2 * PART + lane + 1]
        return high + middle_part + low

    gains = [param(GAINS + j) for j in range(3)]
    biases = [param(BIASES + j) for j in range(3)]

    def store_taps(target, values):
        for tap in range(9):
            row_step, col_step = tap_steps(tap)
            target[tap, :, :] = shifted(values, row_step, col_step, 1).astype(BF16)

    def convolve(first_block, taps):
        total = None
        for tap in range(9):
            product = dot_nn(weights[first_block + tap], taps[tap])
            total = product if total is None else total + product
        return total

    hat_one, inverse_one = norm_hat(source)
    pre_one = hat_one * gains[0] + biases[0]
    first_act = (pre_one * sigmoid(pre_one)).astype(BF16).astype(F32)
    store_taps(taps_one, first_act)
    middle = convolve(0, taps_one) + (param(CONV_BIAS) + param(OFFSETS))
    hat_two, inverse_two = norm_hat(middle)
    pre_two = hat_two * gains[1] + biases[1]
    second_act = (pre_two * sigmoid(pre_two) * keep).astype(BF16).astype(F32)
    store_taps(taps_two, second_act)
    residual = source + convolve(9, taps_two) + param(CONV_BIAS + 1)
    hat_three, inverse_three = norm_hat(residual)
    normed = (hat_three * gains[2] + biases[2]).astype(BF16)
    queries = (dot_nn(weights[18], normed) + param(QV_BIAS)).astype(BF16)
    keys = dot_nn(weights[19], normed).astype(BF16)
    vals = (dot_nn(weights[20], normed) + param(QV_BIAS + 1)).astype(BF16)
    scale = C ** (-0.5)
    scores = dot_tn(queries, keys) * scale
    exps = jnp.exp(scores - jnp.max(scores, axis=1, keepdims=True))
    probs = exps / jnp.sum(exps, axis=1, keepdims=True)
    probs_low = probs.astype(BF16)
    attended = dot_nt(vals, probs_low).astype(BF16)
    outputs = residual + dot_nn(weights[21], attended) + param(OUT_BIAS)

    def put_image(at, values):
        left = values[:, 0:HALF].reshape(SHARDS, ROWS, HALF)
        right = values[:, HALF:C].reshape(SHARDS, ROWS, HALF)
        send_ref[:, at : at + 16, :] = jnp.concatenate([left, right], axis=1).astype(BF16)

    put_image(WROWS, outputs)

    pending = {}

    def put_weight_grad(block, values):
        pending[block] = values
        pair = block // 2
        if 2 * pair in pending and 2 * pair + 1 in pending:
            a, b = pending.pop(2 * pair), pending.pop(2 * pair + 1)
            low = [v[:, 0:HALF].reshape(SHARDS, ROWS, HALF) for v in (a, b)]
            high = [v[:, HALF:C].reshape(SHARDS, ROWS, HALF) for v in (a, b)]
            low, high = jnp.concatenate(low, axis=1), jnp.concatenate(high, axis=1)
            rows = slice(16 * pair, 16 * pair + 16)
            send_ref[:, rows, :] = jnp.where(first_core, low, high).astype(BF16)
            swap_ref[:, rows, :] = jnp.where(first_core, high, low).astype(BF16)

    cot_low = cotangent.astype(BF16)
    out_bias_grad = jnp.sum(cotangent, axis=1, keepdims=True)
    put_weight_grad(21, dot_nt(cot_low, attended))
    attended_grad = dot_tn(weights[21], cot_low).astype(BF16)
    dprobs = dot_tn(attended_grad, vals)
    row_dot = jnp.sum(probs * dprobs, axis=1, keepdims=True)
    dscores = (probs * (dprobs - row_dot)).astype(BF16)
    query_grad = (dot_nt(keys, dscores) * scale).astype(BF16)
    key_grad = (dot_nn(queries, dscores) * scale).astype(BF16)
    value_grad = dot_nn(attended_grad, probs_low).astype(BF16)
    query_bias_grad = jnp.sum(query_grad.astype(F32), axis=1, keepdims=True)
    value_bias_grad = jnp.sum(value_grad.astype(F32), axis=1, keepdims=True)
    normed_grad = None
    for k, gradient in enumerate((query_grad, key_grad, value_grad)):
        put_weight_grad(18 + k, dot_nt(gradient, normed))
        product = dot_tn(weights[18 + k], gradient)
        normed_grad = product if normed_grad is None else normed_grad + product
    branch_three, gain_three, bias_three = norm_back(
        hat_three, inverse_three, normed_grad, gains[2]
    )
    residual_grad = cotangent + branch_three
    conv_two_bias = jnp.sum(residual_grad, axis=1, keepdims=True)

    def conv_back(first_block, gradient, taps):
        low = gradient.astype(BF16)
        for tap in range(9):
            put_weight_grad(first_block + tap, dot_nt(low, taps[tap]))
        turned = low.astype(F32).T
        total = None
        for tap in range(9):
            row_step, col_step = tap_steps(tap)
            moved = shifted(turned, -row_step, -col_step, 0).astype(BF16)
            product = dot_nn(moved, weights[first_block + tap])
            total = product if total is None else total + product
        return total.T

    def slope(values):
        sigma = sigmoid(values)
        return sigma * (1.0 + values * (1.0 - sigma))

    second_grad = conv_back(9, residual_grad, taps_two)
    pre_two_grad = second_grad * keep * slope(pre_two)
    middle_grad, gain_two, bias_two = norm_back(hat_two, inverse_two, pre_two_grad, gains[1])
    conv_one_bias = jnp.sum(middle_grad, axis=1, keepdims=True)
    first_grad = conv_back(0, middle_grad, taps_one)
    pre_one_grad = first_grad * slope(pre_one)
    branch_one, gain_one, bias_one = norm_back(hat_one, inverse_one, pre_one_grad, gains[0])
    put_image(WROWS + 16, residual_grad + branch_one)

    lane = lax.broadcasted_iota(jnp.int32, (C, HALF), 1)
    table = jnp.zeros((C, HALF), F32)
    listed = (
        gain_one, gain_two, gain_three, bias_one, bias_two, bias_three,
        conv_one_bias, conv_two_bias, query_bias_grad, value_bias_grad, out_bias_grad,
    )
    for k, column in enumerate(listed):
        table = jnp.where((lane & (PART - 1)) == k, column, table)
    high = table.astype(BF16).astype(F32)
    table = jnp.where(lane < PART, high, jnp.where(lane < 2 * PART, table - high, 0.0))
    send_ref[:, WROWS + 32 : WROWS + 40, :] = table.reshape(SHARDS, ROWS, HALF).astype(BF16)


IN_ROWS = WROWS + 56
OUT_ROWS = WROWS + 40


def run_block(core, received, other):
    return pl.pallas_call(
        block_kernel,
        out_shape=(
            jax.ShapeDtypeStruct((SHARDS, OUT_ROWS, HALF), BF16),
            jax.ShapeDtypeStruct((SHARDS, WROWS, HALF), BF16),
        ),
        in_specs=[
            pl.BlockSpec(memory_space=pltpu.SMEM),
            pl.BlockSpec(memory_space=pltpu.VMEM),
            pl.BlockSpec(memory_space=pltpu.VMEM),
        ],
        out_specs=(
            pl.BlockSpec(memory_space=pltpu.VMEM),
            pl.BlockSpec(memory_space=pltpu.VMEM),
        ),
        scratch_shapes=[
            pltpu.VMEM((WBLOCKS, C, C), BF16),
            pltpu.VMEM((9, C, POS), BF16),
            pltpu.VMEM((9, C, POS), BF16),
            pltpu.VMEM((9, POS, C), BF16),
        ],
        compiler_params=pltpu.CompilerParams(vmem_limit_bytes=48 * 1024 * 1024),
    )(core, received, other)


def time_features(timesteps):
    half_dim = TEMB // 2
    rates = jnp.exp(-math.log(10000.0) * jnp.arange(half_dim, dtype=F32) / (half_dim - 1))
    angles = timesteps.astype(F32)[:, None] * rates[None, :]
    return jnp.concatenate([jnp.sin(angles), jnp.cos(angles)], axis=1)


def halves(values):
    rows, images, positions = values.shape
    cut = values.reshape(rows, images, 2, HALF).transpose(1, 2, 0, 3)
    return cut.reshape(images, 2 * rows, HALF)


def whole(blocks):
    images = blocks.shape[0]
    cut = blocks.reshape(images, 2, ROWS, HALF).transpose(2, 0, 1, 3)
    return cut.reshape(ROWS, images, POS)


def bf16_part(values):
    return lax.reduce_precision(values, exponent_bits=8, mantissa_bits=7)


def on_device(
    inputs,
    timesteps,
    keep_mask,
    norm_gain,
    norm_bias,
    conv_weight,
    conv_bias,
    temb_weight,
    temb_bias,
    qkv_weight,
    qv_bias,
    out_weight,
    out_bias,
    cotangent,
):
    member = lax.axis_index("img")
    core = member % 2
    core_pairs = [(m, m ^ 1) for m in range(4)]
    plane_pairs = [(m, m ^ 2) for m in range(4)]
    highest = lax.Precision.HIGHEST

    features = time_features(timesteps)
    swished = features * jax.nn.sigmoid(features)
    offsets = jnp.dot(swished, temb_weight.astype(F32), precision=highest) + temb_bias[None, :]

    shard = jnp.concatenate(
        [
            conv_weight.reshape(18 * ROWS, C),
            qkv_weight.reshape(3 * ROWS, C),
            out_weight.reshape(ROWS, C),
        ],
        axis=0,
    )
    shard = lax.dynamic_slice_in_dim(shard, core * HALF, HALF, 1)
    fixed = jnp.stack(
        [*norm_gain, *norm_bias, *conv_bias, *qv_bias, out_bias], axis=-1
    )
    params = jnp.concatenate(
        [offsets[:, :, None], jnp.broadcast_to(fixed[None], (SHARDS,) + fixed.shape)], axis=2
    )
    params = jnp.pad(params, ((0, 0), (0, 0), (0, PART - params.shape[2])))
    high = bf16_part(params)
    mid = bf16_part(params - high)
    low = params - high - mid
    params = jnp.pad(
        jnp.concatenate([high, mid, low], axis=2), ((0, 0), (0, 0), (0, HALF - 3 * PART))
    ).astype(BF16)
    sent = jnp.concatenate(
        [
            jnp.broadcast_to(shard[None], (SHARDS,) + shard.shape),
            halves(inputs),
            halves(keep_mask.astype(BF16)),
            halves(cotangent),
            params,
        ],
        axis=1,
    )
    received = lax.all_to_all(sent, "ch", split_axis=0, concat_axis=0, tiled=True)
    other = lax.ppermute(received, "img", core_pairs)

    send, swap = run_block(core.reshape(1), received, other)

    swapped = lax.ppermute(swap, "img", core_pairs)
    send = send + jnp.pad(swapped, ((0, 0), (0, OUT_ROWS - WROWS), (0, 0)))
    back = lax.all_to_all(send, "ch", split_axis=0, concat_axis=0, tiled=True)

    outputs = whole(back[:, WROWS : WROWS + 16])
    input_grad = whole(back[:, WROWS + 16 : WROWS + 32])
    weight_sums = jnp.sum(back[:, :WROWS].astype(F32), axis=0)
    small = back[:, WROWS + 32 :].astype(F32)
    small = small[:, :, :PART] + small[:, :, PART : 2 * PART]
    offsets_grad = small[:, :, D_CONV_BIAS]
    temb_grad = lax.dot_general(
        offsets_grad, swished, (((0,), (0,)), ((), ())), precision=highest,
        preferred_element_type=F32,
    )
    small_sums = jnp.pad(jnp.sum(small, axis=0), ((0, 0), (0, HALF - PART)))
    sums = jnp.concatenate(
        [weight_sums, small_sums, temb_grad.reshape(TEMB * ROWS // HALF, HALF)], axis=0
    )
    sums = sums + lax.ppermute(sums, "img", plane_pairs)
    theirs = lax.ppermute(sums, "img", core_pairs)

    mine_w, their_w = sums[:WROWS], theirs[:WROWS]
    weight_grads = jnp.where(
        core == 0,
        jnp.concatenate([mine_w, their_w], axis=1),
        jnp.concatenate([their_w, mine_w], axis=1),
    )
    shared = sums[WROWS:] + theirs[WROWS:]
    table = shared[:ROWS].T
    temb_weight_grad = shared[ROWS:].reshape(ROWS, TEMB).T
    return (
        outputs,
        input_grad,
        table[D_GAINS : D_GAINS + 3],
        table[D_BIASES : D_BIASES + 3],
        weight_grads[: 18 * ROWS].reshape(2, 9, ROWS, C),
        table[D_CONV_BIAS : D_CONV_BIAS + 2],
        temb_weight_grad,
        table[D_CONV_BIAS],
        weight_grads[18 * ROWS : 21 * ROWS].reshape(3, ROWS, C),
        table[D_QV_BIAS : D_QV_BIAS + 2],
        weight_grads[21 * ROWS :],
        table[D_OUT_BIAS],
    )


def solution(mesh):
    placed = (
        P("ch", "img", None),
        P("img"),
        P("ch", "img", None),
        P(None, "ch"),
        P(None, "ch"),
        P(None, None, "ch", None),
        P(None, "ch"),
        P(None, "ch"),
        P("ch"),
        P(None, "ch", None),
        P(None, "ch"),
        P("ch", None),
        P("ch"),
        P("ch", "img", None),
    )
    return jax.shard_map(
        on_device,
        mesh=mesh,
        in_specs=placed,
        out_specs=(
            P("ch", "img", None),
            P("ch", "img", None),
            P(None, "ch"),
            P(None, "ch"),
            P(None, None, "ch", None),
            P(None, "ch"),
            P(None, "ch"),
            P("ch"),
            P(None, "ch", None),
            P(None, "ch"),
            P("ch", None),
            P("ch"),
        ),
        check_vma=False,
    )
```

time: 3030 us -> 106 us (0.03)
  waiting for transfers between devices: 2550 us -> 9.22 us
  matrix products: 181 us -> 0.33 us
  local copies, waits for them, and re-layouts: 163 us -> 11.2 us
  other arithmetic: 104 us -> 2.04 us
  blocking collectives: 10.4 us -> 65.9 us
    reduce_scatter x9 -> x0, waiting for transfers between devices: 1490 us -> none  [the longest x4 681 us: one_block(): lax.psum_scatter(partial_scores, 'ch', scatter_dimension=1, tiled=True)]
    all_gather x10 -> x0, waiting for transfers between devices: 837 us -> none  [the longest x4 319 us: project_forward(): shard_piece = lax.all_gather(local_acts, 'ch', axis=0, tiled=True)]
    dot_general x76 -> x2, matrix products: 181 us -> 0.33 us  [the longest x1 0.18 us: on_device(): lax.dot_general(offsets_grad, swished, (((0,), (0,)), ((), ())), precisio...]
    unnamed x10 -> x0, waiting for transfers between devices: 163 us -> none
    unnamed x198 -> x30, local copies, waits for them, and re-layouts: 120 us -> 4.59 us
    all_to_all x0 -> x2, blocking collectives: none -> 65.9 us  [the longest x1 37 us: on_device(): lax.all_to_all(sent, 'ch', split_axis=0, concat_axis=0, tiled=True)]
    mul x2 -> x0, other arithmetic: 65.7 us -> none  [shift_cells(): return moved * valid]
    psum x1 -> x0, waiting for transfers between devices: 54.9 us -> none  [on_device(): lax.psum(grads[2].astype(jnp.bfloat16), 'img').astype(jnp.float32)]
  transfers between devices with their start and end apart: 21 -> 4, of which waited for: 21 -> 3; matrix products, arithmetic and copies ran while one was open for 5% -> 2% of each run, Pallas kernels for 0% -> 0%
where the time goes in v1:
time: 106 us
  blocking collectives  65.9 us (62%)
  local copies, waits for them, and re-layouts  11.2 us (11%)
  waiting for transfers between devices  9.22 us (9%)
  Pallas kernels  9.02 us (9%)
  starting transfers between devices  7.14 us (7%)
  other arithmetic  2.04 us (2%)
    all_to_all x1, blocking collectives, on_device(): lax.all_to_all(sent, 'ch', split_axis=0, concat_axis=0, tiled=True)  37 us
    all_to_all x1, blocking collectives, on_device(): back = lax.all_to_all(send, 'ch', split_axis=0, concat_axis=0, tiled=True)  28.9 us
    pallas_call x1, Pallas kernels, run_block(): pl.pallas_call(block_kernel, out_shape=(jax.ShapeDtypeStruct((SHARDS, OUT...  9.02 us
    unnamed x30, local copies, waits for them, and re-layouts  4.59 us
    ppermute x1, waiting for transfers between devices, on_device(): other = lax.ppermute(received, 'img', core_pairs)  3.51 us
    ppermute x1, starting transfers between devices, on_device(): theirs = lax.ppermute(sums, 'img', core_pairs)  3.39 us
    ppermute x1, waiting for transfers between devices, on_device(): sums = sums + lax.ppermute(sums, 'img', plane_pairs)  2.86 us
    ppermute x1, waiting for transfers between devices, on_device(): swapped = lax.ppermute(swap, 'img', core_pairs)  2.85 us
  transfers between devices with their start and end apart: 4, of which 3 were waited for; matrix products, arithmetic and copies ran while one was open for 2% of the time, Pallas kernels for 0%

profile of v1, /device:TPU:1, one launch (start us, length us, event | category | flops | bytes accessed | tf_op | source)
XLA Modules:
  0.0 105.8 jit_solution(416967786007219579)
XLA Ops:
  0.8 0.9 fusion.11
  1.7 0.2 broadcast_dynamic-update-slice_fusion
  1.9 0.9 reshape.87
  3.0 0.2 multiply_sine_fusion
  3.7 0.2 bitcast_dynamic-update-slice_fusion.2
  3.9 0.2 bitcast_dynamic-update-slice_fusion.1
  4.1 0.2 bitcast_dynamic-update-slice_fusion
  4.4 37.0 %all_to_all.10.recv_ref = bf16[32,232,128]{2,1,0:T(8,128)(2,1)S(1)} all-to-all(bf16[32,232,128]{2,1,0:T(8,128)(2,1)S(1)} %fusion.9), channel_id=1, replica_groups=mesh['ch'=32,'img'=4] {'ch'}, dimensions={0} | all-to-all | bytes 3801088 | tf_op jit(solution)/shard_map/all_to_all | solution.py:359
  41.4 2.5 %collective-permute-start = (bf16[32,232,128]{2,1,0:T(8,128)(2,1)S(1)}, bf16[32,232,128]{2,1,0:T(8,128)(2,1)S(1)}, u32[]{:S(2)}, u32[]{:S(2)}) collective-permute-start(bf16[32,232,128]{2,1,0:T(8,128)(2,1)S(1)} %all_to_all.10.recv_ref), channel_id=1, source_target_pairs={{0,1},{1,0},{2,3},{3,2},{4,5},{5,4},{6,7},{7,6},{8,9},{9,8},{10,11... | collective-permute-start | bytes 5701640 | tf_op jit(solution)/shard_map/ppermute | solution.py:360
  43.9 3.5 %collective-permute-done.other_ref = bf16[32,232,128]{2,1,0:T(8,128)(2,1)S(1)} collective-permute-done((bf16[32,232,128]{2,1,0:T(8,128)(2,1)S(1)}, bf16[32,232,128]{2,1,0:T(8,128)(2,1)S(1)}, u32[]{:S(2)}, u32[]{:S(2)}) %collective-permute-start) | collective-permute-done | bytes 1900576 | tf_op jit(solution)/shard_map/ppermute | solution.py:360
  47.4 1.3 %copy-done.1 = bf16[32,232,128]{2,1,0:T(8,128)(2,1)} copy-done((bf16[32,232,128]{2,1,0:T(8,128)(2,1)}, bf16[32,232,128]{2,1,0:T(8,128)(2,1)S(1)}, u32[]{:S(2)}) %copy-start.1) | copy-done | bytes 1900568
  48.7 9.0 %shard_map.229 = (bf16[32,216,128]{2,1,0:T(8,128)(2,1)S(1)}, bf16[32,176,128]{2,1,0:T(8,128)(2,1)S(1)}) custom-call(s32[1]{0:T(128)} %bitcast.core_ref, bf16[32,232,128]{2,1,0:T(8,128)(2,1)S(1)} %all_to_all.10.recv_ref, bf16[32,232,128]{2,1,0:T(8,128)(2,1)} %copy-done.1), custom_call_target="tpu_custom_call" | custom-call | tf_op jit(solution)/shard_map/pallas_call | solution.py:253
  57.7 0.5 collective-permute-start.1
  58.2 2.9 %collective-permute-done.1 = bf16[32,176,128]{2,1,0:T(8,128)(2,1)S(1)} collective-permute-done((bf16[32,176,128]{2,1,0:T(8,128)(2,1)S(1)}, bf16[32,176,128]{2,1,0:T(8,128)(2,1)S(1)}, u32[]{:S(2)}, u32[]{:S(2)}) %collective-permute-start.1) | collective-permute-done | bytes 1441824 | tf_op jit(solution)/shard_map/ppermute | solution.py:364
  61.0 0.4 pad_add_fusion
  61.4 28.9 %all_to_all.11 = bf16[32,216,128]{2,1,0:T(8,128)(2,1)S(1)} all-to-all(bf16[32,216,128]{2,1,0:T(8,128)(2,1)S(1)} %pad_add_fusion), channel_id=1, replica_groups=mesh['ch'=32,'img'=4] {'ch'}, dimensions={0} | all-to-all | bytes 3538944 | tf_op jit(solution)/shard_map/all_to_all | solution.py:366
  90.6 0.2 fusion.12
  90.8 0.2 convert_reduce_fusion
  91.0 0.8 collective-permute-start.2
  91.8 2.9 %collective-permute-done.2 = f32[216,128]{1,0:T(8,128)S(1)} collective-permute-done((f32[216,128]{1,0:T(8,128)S(1)}, f32[216,128]{1,0:T(8,128)S(1)}, u32[]{:S(2)}, u32[]{:S(2)}) %collective-permute-start.2) | collective-permute-done | bytes 110624 | tf_op jit(solution)/shard_map/ppermute | solution.py:382
  94.7 3.4 %collective-permute-start.3 = (f32[216,128]{1,0:T(8,128)S(1)}, f32[216,128]{1,0:T(8,128)S(1)}, u32[]{:S(2)}, u32[]{:S(2)}) collective-permute-start(f32[216,128]{1,0:T(8,128)S(1)} %fusion.14), channel_id=1, source_target_pairs={{0,1},{1,0},{2,3},{3,2},{4,5},{5,4},{6,7},{7,6},{8,9},{9,8},{10,11... | collective-permute-start | bytes 331784 | tf_op jit(solution)/shard_map/ppermute | solution.py:383
  98.2 0.7 reshape.94
  99.1 0.7 reshape.96
  99.9 0.7 slice.100
  100.6 0.6 slice_bitcast_fusion.2
  101.2 0.6 slice.103
  101.9 0.7 slice_reduce_fusion
  102.7 0.6 reshape.99
  103.3 0.7 copy.67
  103.9 0.7 copy.68
  104.6 0.6 copy.69
  105.2 0.6 copy.70
  (54 shorter events, 1.6 us)
Async XLA Ops:
  0.6 2.6 %copy-start = (bf16[512,8]{0,1:T(8,128)(2,1)S(1)}, bf16[512,8]{0,1:T(8,128)(2,1)}, u32[]{:S(2)}) copy-start(bf16[512,8]{0,1:T(8,128)(2,1)} %param.21) | copy-start | bytes 24580
  0.7 2.1 %copy-start.2 = (s32[8,32,256]{2,1,0:T(8,128)S(1)}, s32[8,32,256]{2,1,0:T(8,128)}, u32[]{:S(2)}) copy-start(s32[8,32,256]{2,1,0:T(8,128)} %param.16) | copy-start | bytes 786436
  0.7 2.2 %copy-start.3 = (bf16[8,32,256]{2,1,0:T(8,128)(2,1)S(1)}, bf16[8,32,256]{2,1,0:T(8,128)(2,1)}, u32[]{:S(2)}) copy-start(bf16[8,32,256]{2,1,0:T(8,128)(2,1)} %param.27) | copy-start | bytes 393220
  0.7 2.2 %copy-start.9 = (s32[32]{0:T(128)S(1)}, s32[32]{0:T(128)}, u32[]{:S(2)}) copy-start(s32[32]{0:T(128)} %param.15) | copy-start | bytes 388
  0.7 2.3 %copy-start.5 = (f32[3,8]{1,0:T(4,128)S(1)}, f32[3,8]{1,0:T(4,128)}, u32[]{:S(2)}) copy-start(f32[3,8]{1,0:T(4,128)} %param.17) | copy-start | bytes 292
  0.7 2.3 %copy-start.4 = (f32[3,8]{1,0:T(4,128)S(1)}, f32[3,8]{1,0:T(4,128)}, u32[]{:S(2)}) copy-start(f32[3,8]{1,0:T(4,128)} %param.18) | copy-start | bytes 292
  0.7 2.3 %copy-start.7 = (f32[2,8]{1,0:T(2,128)S(1)}, f32[2,8]{1,0:T(2,128)}, u32[]{:S(2)}) copy-start(f32[2,8]{1,0:T(2,128)} %param.20) | copy-start | bytes 196
  0.7 2.3 %copy-start.6 = (f32[2,8]{1,0:T(2,128)S(1)}, f32[2,8]{1,0:T(2,128)}, u32[]{:S(2)}) copy-start(f32[2,8]{1,0:T(2,128)} %param.24) | copy-start | bytes 196
  0.7 2.5 %copy-start.10 = (f32[8]{0:T(128)S(1)}, f32[8]{0:T(128)}, u32[]{:S(2)}) copy-start(f32[8]{0:T(128)} %param.22) | copy-start | bytes 100
  0.7 2.6 %copy-start.8 = (f32[8]{0:T(128)S(1)}, f32[8]{0:T(128)}, u32[]{:S(2)}) copy-start(f32[8]{0:T(128)} %param.26) | copy-start | bytes 100
  41.4 6.0 %collective-permute-start = (bf16[32,232,128]{2,1,0:T(8,128)(2,1)S(1)}, bf16[32,232,128]{2,1,0:T(8,128)(2,1)S(1)}, u32[]{:S(2)}, u32[]{:S(2)}) collective-permute-start(bf16[32,232,128]{2,1,0:T(8,128)(2,1)S(1)} %all_to_all.10.recv_ref), channel_id=1, source_target_pairs={{0,1},{1,0},{2,3},{3,2},{4,5},{5,4},{6,7},{7,6},{8,9},{9,8},{10,11... | collective-permute-start | bytes 5701640 | tf_op jit(solution)/shard_map/ppermute | solution.py:360
  47.4 1.3 %copy-start.1 = (bf16[32,232,128]{2,1,0:T(8,128)(2,1)}, bf16[32,232,128]{2,1,0:T(8,128)(2,1)S(1)}, u32[]{:S(2)}) copy-start(bf16[32,232,128]{2,1,0:T(8,128)(2,1)S(1)} %collective-permute-done.other_ref) | copy-start | bytes 5701636
  57.7 3.3 %collective-permute-start.1 = (bf16[32,176,128]{2,1,0:T(8,128)(2,1)S(1)}, bf16[32,176,128]{2,1,0:T(8,128)(2,1)S(1)}, u32[]{:S(2)}, u32[]{:S(2)}) collective-permute-start(bf16[32,176,128]{2,1,0:T(8,128)(2,1)S(1)} %get-tuple-element.15), channel_id=1, source_target_pairs={{0,1},{1,0},{2,3},{3,2},{4,5},{5,4},{6,7},{7,6},{8,9},{9,8},{10,11... | collective-permute-start | bytes 4325384 | tf_op jit(solution)/shard_map/ppermute | solution.py:364
  91.0 3.7 %collective-permute-start.2 = (f32[216,128]{1,0:T(8,128)S(1)}, f32[216,128]{1,0:T(8,128)S(1)}, u32[]{:S(2)}, u32[]{:S(2)}) collective-permute-start(f32[216,128]{1,0:T(8,128)S(1)} %fusion.5), channel_id=1, source_target_pairs={{0,2},{1,3},{2,0},{3,1},{4,6},{5,7},{6,4},{7,5},{8,10},{9,11},{10,... | collective-permute-start | bytes 331784 | tf_op jit(solution)/shard_map/ppermute | solution.py:382
  94.7 5.1 %collective-permute-start.3 = (f32[216,128]{1,0:T(8,128)S(1)}, f32[216,128]{1,0:T(8,128)S(1)}, u32[]{:S(2)}, u32[]{:S(2)}) collective-permute-start(f32[216,128]{1,0:T(8,128)S(1)} %fusion.14), channel_id=1, source_target_pairs={{0,1},{1,0},{2,3},{3,2},{4,5},{5,4},{6,7},{7,6},{8,9},{9,8},{10,11... | collective-permute-start | bytes 331784 | tf_op jit(solution)/shard_map/ppermute | solution.py:383

commit v2 on v1

--- a/solution.py
+++ b/solution.py
@@ -22,7 +22,7 @@
 F32 = jnp.float32
 BF16 = jnp.bfloat16
 
-OFFSETS, GAINS, BIASES, CONV_BIAS, QV_BIAS, OUT_BIAS = 0, 1, 4, 7, 9, 11
+OFFSETS, GAINS, BIASES, CONV_BIAS, QV_BIAS, OUT_BIAS, TEMB_BIAS = 0, 1, 4, 7, 9, 11, 12
 D_GAINS, D_BIASES, D_CONV_BIAS, D_QV_BIAS, D_OUT_BIAS = 0, 3, 6, 8, 10
 PART = 16
 
@@ -271,31 +271,177 @@
             pltpu.VMEM((9, C, POS), BF16),
             pltpu.VMEM((9, POS, C), BF16),
         ],
-        compiler_params=pltpu.CompilerParams(vmem_limit_bytes=48 * 1024 * 1024),
+        compiler_params=pltpu.CompilerParams(vmem_limit_bytes=24 * 1024 * 1024),
     )(core, received, other)
 
 
-def time_features(timesteps):
+def finish_kernel(core_ref, mine_ref, theirs_ref, *refs):
+    results, scratch, sems = refs[:10], refs[10:20], refs[20]
+    first_core = core_ref[0] == 0
+    (gain, bias, conv_w, conv_b, temb_w, temb_b, qkv_w, qv_b, out_w, out_b) = scratch
+
+    def weight_grad(block):
+        rows = slice(ROWS * block, ROWS * block + ROWS)
+        mine, theirs = mine_ref[rows, :], theirs_ref[rows, :]
+        return jnp.concatenate(
+            [jnp.where(first_core, mine, theirs), jnp.where(first_core, theirs, mine)], axis=1
+        )
+
+    copies = [pltpu.make_async_copy(scratch[k], results[k], sems.at[k]) for k in range(10)]
+    for block in range(18):
+        conv_w[block // 9, block % 9, :, :] = weight_grad(block)
+    copies[2].start()
+    for k in range(3):
+        qkv_w[k, :, :] = weight_grad(18 + k)
+    copies[6].start()
+    out_w[...] = weight_grad(21)
+    copies[8].start()
+    shared = mine_ref[WROWS:, :] + theirs_ref[WROWS:, :]
+    for part in range(TEMB // HALF):
+        rows = slice(ROWS + ROWS * part, 2 * ROWS + ROWS * part)
+        temb_w[:, HALF * part : HALF * part + HALF] = shared[rows, :]
+    copies[4].start()
+    padded = jnp.concatenate([shared[:ROWS, :], jnp.zeros((HALF - ROWS, HALF), F32)], axis=0)
+    table = padded.T[:PART, :ROWS]
+    gain[...] = table[D_GAINS : D_GAINS + 3]
+    bias[...] = table[D_BIASES : D_BIASES + 3]
+    conv_b[...] = table[D_CONV_BIAS : D_CONV_BIAS + 2]
+    temb_b[...] = table[D_CONV_BIAS : D_CONV_BIAS + 1]
+    qv_b[...] = table[D_QV_BIAS : D_QV_BIAS + 2]
+    out_b[...] = table[D_OUT_BIAS : D_OUT_BIAS + 1]
+    for k in (0, 1, 3, 5, 7, 9):
+        copies[k].start()
+    for copy in copies:
+        copy.wait()
+
+
+def finish(core, mine, theirs):
+    shapes = [
+        (3, ROWS), (3, ROWS), (2, 9, ROWS, C), (2, ROWS), (ROWS, TEMB), (1, ROWS),
+        (3, ROWS, C), (2, ROWS), (ROWS, C), (1, ROWS),
+    ]
+    return pl.pallas_call(
+        finish_kernel,
+        out_shape=[jax.ShapeDtypeStruct(shape, F32) for shape in shapes],
+        in_specs=[
+            pl.BlockSpec(memory_space=pltpu.SMEM),
+            pl.BlockSpec(memory_space=pltpu.VMEM),
+            pl.BlockSpec(memory_space=pltpu.VMEM),
+        ],
+        out_specs=[pl.BlockSpec(memory_space=pltpu.HBM) for _ in shapes],
+        scratch_shapes=[pltpu.VMEM(shape, F32) for shape in shapes]
+        + [pltpu.SemaphoreType.DMA((10,))],
+        compiler_params=pltpu.CompilerParams(vmem_limit_bytes=8 * 1024 * 1024),
+    )(core, mine, theirs)
+
+
+def prepare_kernel(core_ref, *refs):
+    count = PREPARE_ARRAYS
+    arrays, (send_ref, swished_ref) = refs[:count], refs[count : count + 2]
+    held, (angles, sems) = refs[count + 2 : 2 * count + 2], refs[2 * count + 2 :]
+    (
+        steps_ref, gain_ref, bias_ref, conv_bias_ref, qv_ref, out_bias_ref, temb_bias_ref,
+        temb_ref, conv_ref, qkv_ref, out_ref, inputs_ref, mask_ref, cotangent_ref,
+    ) = held
+    copies = [pltpu.make_async_copy(arrays[k], held[k], sems.at[k]) for k in range(count)]
+    for copy in copies:
+        copy.start()
+    first_core = core_ref[0] == 0
+    for copy in copies[:8]:
+        copy.wait()
+
     half_dim = TEMB // 2
-    rates = jnp.exp(-math.log(10000.0) * jnp.arange(half_dim, dtype=F32) / (half_dim - 1))
-    angles = timesteps.astype(F32)[:, None] * rates[None, :]
-    return jnp.concatenate([jnp.sin(angles), jnp.cos(angles)], axis=1)
-
-
-def halves(values):
-    rows, images, positions = values.shape
-    cut = values.reshape(rows, images, 2, HALF).transpose(1, 2, 0, 3)
-    return cut.reshape(images, 2 * rows, HALF)
+    index = lax.broadcasted_iota(jnp.int32, (1, half_dim), 1).astype(F32)
+    rates = jnp.exp(-math.log(10000.0) * index / (half_dim - 1))
+    for image in range(SHARDS):
+        angles[image : image + 1, :] = rates * steps_ref[image].astype(F32)
+    features = jnp.concatenate([jnp.sin(angles[...]), jnp.cos(angles[...])], axis=1)
+    swished = features * sigmoid(features)
+    swished_ref[...] = swished
+    offsets = None
+    rest = swished
+    for _ in range(3):
+        part = rest.astype(BF16)
+        rest = rest - part.astype(F32)
+        product = dot_nt(temb_ref[...], part)
+        offsets = product if offsets is None else offsets + product
+
+    rows = jnp.concatenate(
+        [
+            jnp.zeros((1, ROWS), F32), gain_ref[...], bias_ref[...], conv_bias_ref[...],
+            qv_ref[...], out_bias_ref[...], temb_bias_ref[...], jnp.zeros((3, ROWS), F32),
+        ],
+        axis=0,
+    )
+    square = jnp.concatenate([rows] * (HALF // PART), axis=0)
+    square = jnp.concatenate([square, jnp.zeros((HALF, HALF - ROWS), F32)], axis=1)
+    columns = square.T[:ROWS, :]
+    lane = lax.broadcasted_iota(jnp.int32, (ROWS, HALF), 1)
+    offset_lane = (lane & (PART - 1)) == OFFSETS
+    offsets = offsets + columns[:, TEMB_BIAS : TEMB_BIAS + 1]
+    for image in range(SHARDS):
+        values = jnp.where(offset_lane, offsets[:, image : image + 1], columns)
+        high = values.astype(BF16).astype(F32)
+        mid = (values - high).astype(BF16).astype(F32)
+        low = values - high - mid
+        parts = jnp.where(
+            lane < PART,
+            high,
+            jnp.where(lane < 2 * PART, mid, jnp.where(lane < 3 * PART, low, 0.0)),
+        )
+        send_ref[image, WROWS + 48 : WROWS + 56, :] = parts.astype(BF16)
+
+    for copy in copies[8:]:
+        copy.wait()
+
+    def half(values):
+        values = values.astype(F32)
+        return jnp.where(first_core, values[:, :HALF], values[:, HALF:])
+
+    shard = jnp.concatenate(
+        [
+            half(conv_ref[...].reshape(18 * ROWS, C)),
+            half(qkv_ref[...].reshape(3 * ROWS, C)),
+            half(out_ref[...]),
+        ],
+        axis=0,
+    ).astype(BF16)
+    send_ref[:, :WROWS, :] = jnp.broadcast_to(shard[None], (SHARDS, WROWS, HALF))
+
+    def put(at, values):
+        turned = jnp.swapaxes(values.astype(F32), 0, 1)
+        cut = jnp.concatenate([turned[:, :, :HALF], turned[:, :, HALF:]], axis=1)
+        send_ref[:, at : at + 16, :] = cut.astype(BF16)
+
+    put(WROWS, inputs_ref[...])
+    put(WROWS + 16, mask_ref[...])
+    put(WROWS + 32, cotangent_ref[...])
+
+
+PREPARE_ARRAYS = 14
+
+
+def prepare(core, timesteps, *arrays):
+    held = [pltpu.SMEM((SHARDS,), jnp.int32)]
+    held += [pltpu.VMEM(array.shape, array.dtype) for array in arrays]
+    return pl.pallas_call(
+        prepare_kernel,
+        out_shape=(
+            jax.ShapeDtypeStruct((SHARDS, IN_ROWS, HALF), BF16),
+            jax.ShapeDtypeStruct((SHARDS, TEMB), F32),
+        ),
+        in_specs=[pl.BlockSpec(memory_space=pltpu.SMEM)]
+        + [pl.BlockSpec(memory_space=pltpu.HBM)] * PREPARE_ARRAYS,
+        out_specs=(pl.BlockSpec(memory_space=pltpu.VMEM), pl.BlockSpec(memory_space=pltpu.VMEM)),
+        scratch_shapes=held
+        + [pltpu.VMEM((SHARDS, TEMB // 2), F32), pltpu.SemaphoreType.DMA((PREPARE_ARRAYS,))],
+        compiler_params=pltpu.CompilerParams(vmem_limit_bytes=16 * 1024 * 1024),
+    )(core, *[pltpu.with_memory_space_constraint(a, pltpu.HBM) for a in (timesteps, *arrays)])
 
 
 def whole(blocks):
-    images = blocks.shape[0]
-    cut = blocks.reshape(images, 2, ROWS, HALF).transpose(2, 0, 1, 3)
-    return cut.reshape(ROWS, images, POS)
-
-
-def bf16_part(values):
-    return lax.reduce_precision(values, exponent_bits=8, mantissa_bits=7)
+    turned = blocks.transpose(1, 0, 2)
+    return jnp.concatenate([turned[:ROWS], turned[ROWS:]], axis=2)
 
 
 def on_device(
@@ -320,41 +466,22 @@
     plane_pairs = [(m, m ^ 2) for m in range(4)]
     highest = lax.Precision.HIGHEST
 
-    features = time_features(timesteps)
-    swished = features * jax.nn.sigmoid(features)
-    offsets = jnp.dot(swished, temb_weight.astype(F32), precision=highest) + temb_bias[None, :]
-
-    shard = jnp.concatenate(
-        [
-            conv_weight.reshape(18 * ROWS, C),
-            qkv_weight.reshape(3 * ROWS, C),
-            out_weight.reshape(ROWS, C),
-        ],
-        axis=0,
-    )
-    shard = lax.dynamic_slice_in_dim(shard, core * HALF, HALF, 1)
-    fixed = jnp.stack(
-        [*norm_gain, *norm_bias, *conv_bias, *qv_bias, out_bias], axis=-1
-    )
-    params = jnp.concatenate(
-        [offsets[:, :, None], jnp.broadcast_to(fixed[None], (SHARDS,) + fixed.shape)], axis=2
-    )
-    params = jnp.pad(params, ((0, 0), (0, 0), (0, PART - params.shape[2])))
-    high = bf16_part(params)
-    mid = bf16_part(params - high)
-    low = params - high - mid
-    params = jnp.pad(
-        jnp.concatenate([high, mid, low], axis=2), ((0, 0), (0, 0), (0, HALF - 3 * PART))
-    ).astype(BF16)
-    sent = jnp.concatenate(
-        [
-            jnp.broadcast_to(shard[None], (SHARDS,) + shard.shape),
-            halves(inputs),
-            halves(keep_mask.astype(BF16)),
-            halves(cotangent),
-            params,
-        ],
-        axis=1,
+    sent, swished = prepare(
+        core.reshape(1),
+        timesteps,
+        norm_gain,
+        norm_bias,
+        conv_bias,
+        qv_bias,
+        out_bias.reshape(1, ROWS),
+        temb_bias.reshape(1, ROWS),
+        temb_weight.T,
+        conv_weight,
+        qkv_weight,
+        out_weight,
+        inputs,
+        keep_mask,
+        cotangent,
     )
     received = lax.all_to_all(sent, "ch", split_axis=0, concat_axis=0, tiled=True)
     other = lax.ppermute(received, "img", core_pairs)
@@ -376,34 +503,28 @@
         preferred_element_type=F32,
     )
     small_sums = jnp.pad(jnp.sum(small, axis=0), ((0, 0), (0, HALF - PART)))
-    sums = jnp.concatenate(
-        [weight_sums, small_sums, temb_grad.reshape(TEMB * ROWS // HALF, HALF)], axis=0
-    )
-    sums = sums + lax.ppermute(sums, "img", plane_pairs)
+    temb_rows = [temb_grad[:, HALF * k : HALF * k + HALF] for k in range(TEMB // HALF)]
+    sums = jnp.concatenate([weight_sums, small_sums, *temb_rows], axis=0)
+    plane = lax.ppermute(sums, "img", plane_pairs)
+    plane, outputs, input_grad = lax.optimization_barrier((plane, outputs, input_grad))
+    sums = sums + plane
     theirs = lax.ppermute(sums, "img", core_pairs)
-
-    mine_w, their_w = sums[:WROWS], theirs[:WROWS]
-    weight_grads = jnp.where(
-        core == 0,
-        jnp.concatenate([mine_w, their_w], axis=1),
-        jnp.concatenate([their_w, mine_w], axis=1),
-    )
-    shared = sums[WROWS:] + theirs[WROWS:]
-    table = shared[:ROWS].T
-    temb_weight_grad = shared[ROWS:].reshape(ROWS, TEMB).T
+    (gain, bias, conv_w, conv_b, temb_w, temb_b, qkv_w, qv_b, out_w, out_b) = finish(
+        core.reshape(1), sums, theirs
+    )
     return (
         outputs,
         input_grad,
-        table[D_GAINS : D_GAINS + 3],
-        table[D_BIASES : D_BIASES + 3],
-        weight_grads[: 18 * ROWS].reshape(2, 9, ROWS, C),
-        table[D_CONV_BIAS : D_CONV_BIAS + 2],
-        temb_weight_grad,
-        table[D_CONV_BIAS],
-        weight_grads[18 * ROWS : 21 * ROWS].reshape(3, ROWS, C),
-        table[D_QV_BIAS : D_QV_BIAS + 2],
-        weight_grads[21 * ROWS :],
-        table[D_OUT_BIAS],
+        gain,
+        bias,
+        conv_w,
+        conv_b,
+        temb_w.T,
+        temb_b[0],
+        qkv_w,
+        qv_b,
+        out_w,
+        out_b[0],
     )
 
 

time: 106 us -> 95.6 us (0.902)
  local copies, waits for them, and re-layouts: 11.2 us -> 1.67 us
  other arithmetic: 2.04 us -> 0.75 us
    reshape x8 -> x0, local copies, waits for them, and re-layouts: 3.73 us -> none  [the longest x2 1.49 us: whole(): return cut.reshape(ROWS, images, POS)]
    unnamed x30 -> x7, local copies, waits for them, and re-layouts: 4.59 us -> 1.38 us
    pallas_call x0 -> x2, Pallas kernels: none -> 2.47 us  [the longest x1 1.69 us: prepare(): pl.pallas_call(prepare_kernel, out_shape=(jax.ShapeDtypeStruct((SHARDS, I...]
    slice x8 -> x1, local copies, waits for them, and re-layouts: 2.17 us -> 0.05 us  [whole(): return jnp.concatenate([turned[:ROWS], turned[ROWS:]], axis=2)]
    pallas_call x1, Pallas kernels: 9.02 us -> 7.5 us  [run_block(): pl.pallas_call(block_kernel, out_shape=(jax.ShapeDtypeStruct((SHARDS, OUT...]
where the time goes in v2:
time: 95.6 us; the launch traced here: 95.4 us
  blocking collectives  65.9 us (69%)
  Pallas kernels  9.97 us (10%)
  waiting for transfers between devices  9.11 us (10%)
  starting transfers between devices  7.12 us (7%)
  local copies, waits for them, and re-layouts  1.67 us (2%)
    all_to_all x1, blocking collectives, on_device(): lax.all_to_all(sent, 'ch', split_axis=0, concat_axis=0, tiled=True)  37 us
    all_to_all x1, blocking collectives, on_device(): back = lax.all_to_all(send, 'ch', split_axis=0, concat_axis=0, tiled=True)  28.9 us
    pallas_call x1, Pallas kernels, run_block(): pl.pallas_call(block_kernel, out_shape=(jax.ShapeDtypeStruct((SHARDS, OUT...  7.5 us
    ppermute x1, waiting for transfers between devices, on_device(): other = lax.ppermute(received, 'img', core_pairs)  3.51 us
    ppermute x1, starting transfers between devices, on_device(): theirs = lax.ppermute(sums, 'img', core_pairs)  3.39 us
    ppermute x1, waiting for transfers between devices, on_device(): swapped = lax.ppermute(swap, 'img', core_pairs)  2.87 us
    ppermute x1, waiting for transfers between devices, on_device(): plane = lax.ppermute(sums, 'img', plane_pairs)  2.73 us
    ppermute x1, starting transfers between devices, on_device(): other = lax.ppermute(received, 'img', core_pairs)  2.48 us
  transfers between devices with their start and end apart: 4, of which 3 were waited for; matrix products, arithmetic and copies ran while one was open for 2% of the time, Pallas kernels for 0%

profile of v2, /device:TPU:1, one launch (start us, length us, event | category | flops | bytes accessed | tf_op | source)
XLA Modules:
  0.0 95.4 jit_solution(10496445456075792010)
XLA Ops:
  0.7 1.7 %shard_map.229 = (bf16[32,232,128]{2,1,0:T(8,128)(2,1)S(1)}, f32[32,512]{1,0:T(8,128)S(1)}) custom-call(s32[1]{0:T(128)} %bitcast.core_ref, s32[32]{0:T(128)} %refs_0_.1, f32[3,8]{1,0:T(4,128)} %refs_1_.1, f32[3,8]{1,0:T(4,128)} %refs_2_.1, f32[2,8]{1,0:T(2,128)} %refs_3_.1, f32[2,8]{1,0:T(2,128)} %refs_4_.1, f32[1,8]{1,0:T(1,128)} %bitcast.16, ...), custom_call_target="tpu_custom_call" | custom-call | tf_op jit(solution)/shard_map/pallas_call | solution.py:427
  2.4 37.0 %all_to_all.10.recv_ref = bf16[32,232,128]{2,1,0:T(8,128)(2,1)S(1)} all-to-all(bf16[32,232,128]{2,1,0:T(8,128)(2,1)S(1)} %get-tuple-element.29), channel_id=1, replica_groups=mesh['ch'=32,'img'=4] {'ch'}, dimensions={0} | all-to-all | bytes 3801088 | tf_op jit(solution)/shard_map/all_to_all | solution.py:486
  39.4 2.5 %collective-permute-start = (bf16[32,232,128]{2,1,0:T(8,128)(2,1)S(1)}, bf16[32,232,128]{2,1,0:T(8,128)(2,1)S(1)}, u32[]{:S(2)}, u32[]{:S(2)}) collective-permute-start(bf16[32,232,128]{2,1,0:T(8,128)(2,1)S(1)} %all_to_all.10.recv_ref), channel_id=1, source_target_pairs={{0,1},{1,0},{2,3},{3,2},{4,5},{5,4},{6,7},{7,6},{8,9},{9,8},{10,11... | collective-permute-start | bytes 5701640 | tf_op jit(solution)/shard_map/ppermute | solution.py:487
  41.9 3.5 %collective-permute-done.other_ref = bf16[32,232,128]{2,1,0:T(8,128)(2,1)S(1)} collective-permute-done((bf16[32,232,128]{2,1,0:T(8,128)(2,1)S(1)}, bf16[32,232,128]{2,1,0:T(8,128)(2,1)S(1)}, u32[]{:S(2)}, u32[]{:S(2)}) %collective-permute-start) | collective-permute-done | bytes 1900576 | tf_op jit(solution)/shard_map/ppermute | solution.py:487
  45.4 7.5 %shard_map.230 = (bf16[32,216,128]{2,1,0:T(8,128)(2,1)S(1)}, bf16[32,176,128]{2,1,0:T(8,128)(2,1)S(1)}) custom-call(s32[1]{0:T(128)} %bitcast.core_ref, bf16[32,232,128]{2,1,0:T(8,128)(2,1)S(1)} %all_to_all.10.recv_ref, bf16[32,232,128]{2,1,0:T(8,128)(2,1)S(1)} %collective-permute-done.other_ref), custom_call_target="tpu_custom_call" | custom-call | tf_op jit(solution)/shard_map/pallas_call | solution.py:253
  52.9 0.4 collective-permute-start.1
  53.3 2.9 %collective-permute-done.1 = bf16[32,176,128]{2,1,0:T(8,128)(2,1)S(1)} collective-permute-done((bf16[32,176,128]{2,1,0:T(8,128)(2,1)S(1)}, bf16[32,176,128]{2,1,0:T(8,128)(2,1)S(1)}, u32[]{:S(2)}, u32[]{:S(2)}) %collective-permute-start.1) | collective-permute-done | bytes 1441824 | tf_op jit(solution)/shard_map/ppermute | solution.py:491
  56.2 0.4 pad_add_fusion
  56.6 28.9 %all_to_all.11 = bf16[32,216,128]{2,1,0:T(8,128)(2,1)S(1)} all-to-all(bf16[32,216,128]{2,1,0:T(8,128)(2,1)S(1)} %pad_add_fusion), channel_id=1, replica_groups=mesh['ch'=32,'img'=4] {'ch'}, dimensions={0} | all-to-all | bytes 3538944 | tf_op jit(solution)/shard_map/all_to_all | solution.py:493
  85.4 0.2 convert_reduce_fusion
  85.7 0.1 fusion.2
  85.8 0.1 slice.64
  85.9 0.1 copy.28
  86.0 0.2 fusion
  86.2 0.8 collective-permute-start.2
  87.2 2.7 %collective-permute-done.2 = f32[216,128]{1,0:T(8,128)S(1)} collective-permute-done((f32[216,128]{1,0:T(8,128)S(1)}, f32[216,128]{1,0:T(8,128)S(1)}, u32[]{:S(2)}, u32[]{:S(2)}) %collective-permute-start.2) | collective-permute-done | bytes 110624 | tf_op jit(solution)/shard_map/ppermute | solution.py:508
  89.9 3.4 %collective-permute-start.3 = (f32[216,128]{1,0:T(8,128)S(1)}, f32[216,128]{1,0:T(8,128)S(1)}, u32[]{:S(2)}, u32[]{:S(2)}) collective-permute-start(f32[216,128]{1,0:T(8,128)S(1)} %add.20.mine_ref), channel_id=1, source_target_pairs={{0,1},{1,0},{2,3},{3,2},{4,5},{5,4},{6,7},{7,6},{8,9},{9,8},{10,11... | collective-permute-start | bytes 331784 | tf_op jit(solution)/shard_map/ppermute | solution.py:511
  93.3 0.7 copy.29
  94.0 0.7 copy.30
  94.6 0.0 collective-permute-done.3.theirs_ref
  94.7 0.8 shard_map.231
  (12 shorter events, 0.1 us)
Async XLA Ops:
  39.4 6.0 %collective-permute-start = (bf16[32,232,128]{2,1,0:T(8,128)(2,1)S(1)}, bf16[32,232,128]{2,1,0:T(8,128)(2,1)S(1)}, u32[]{:S(2)}, u32[]{:S(2)}) collective-permute-start(bf16[32,232,128]{2,1,0:T(8,128)(2,1)S(1)} %all_to_all.10.recv_ref), channel_id=1, source_target_pairs={{0,1},{1,0},{2,3},{3,2},{4,5},{5,4},{6,7},{7,6},{8,9},{9,8},{10,11... | collective-permute-start | bytes 5701640 | tf_op jit(solution)/shard_map/ppermute | solution.py:487
  52.9 3.3 %collective-permute-start.1 = (bf16[32,176,128]{2,1,0:T(8,128)(2,1)S(1)}, bf16[32,176,128]{2,1,0:T(8,128)(2,1)S(1)}, u32[]{:S(2)}, u32[]{:S(2)}) collective-permute-start(bf16[32,176,128]{2,1,0:T(8,128)(2,1)S(1)} %get-tuple-element.31), channel_id=1, source_target_pairs={{0,1},{1,0},{2,3},{3,2},{4,5},{5,4},{6,7},{7,6},{8,9},{9,8},{10,11... | collective-permute-start | bytes 4325384 | tf_op jit(solution)/shard_map/ppermute | solution.py:491
  86.2 3.7 %collective-permute-start.2 = (f32[216,128]{1,0:T(8,128)S(1)}, f32[216,128]{1,0:T(8,128)S(1)}, u32[]{:S(2)}, u32[]{:S(2)}) collective-permute-start(f32[216,128]{1,0:T(8,128)S(1)} %constant_dynamic-update-slice_fusion), channel_id=1, source_target_pairs={{0,2},{1,3},{2,0},{3,1},{4,6},{5,7},{6,4},{7,5},{8,10},{9,11},{10,... | collective-permute-start | bytes 331784 | tf_op jit(solution)/shard_map/ppermute | solution.py:508
  89.9 4.8 %collective-permute-start.3 = (f32[216,128]{1,0:T(8,128)S(1)}, f32[216,128]{1,0:T(8,128)S(1)}, u32[]{:S(2)}, u32[]{:S(2)}) collective-permute-start(f32[216,128]{1,0:T(8,128)S(1)} %add.20.mine_ref), channel_id=1, source_target_pairs={{0,1},{1,0},{2,3},{3,2},{4,5},{5,4},{6,7},{7,6},{8,9},{9,8},{10,11... | collective-permute-start | bytes 331784 | tf_op jit(solution)/shard_map/ppermute | solution.py:511

commit v3 on v2

--- a/solution.py
+++ b/solution.py
@@ -92,14 +92,11 @@
     return moved * valid.astype(F32)
 
 
-def block_kernel(
-    core_ref, recv_ref, other_ref, send_ref, swap_ref, weights, taps_one, taps_two, back
-):
-    first_core = core_ref[0] == 0
-
-    for pair in range(WBLOCKS // 2):
-        mine = recv_ref[:, 16 * pair : 16 * pair + 16, :].astype(F32)
-        theirs = other_ref[:, 16 * pair : 16 * pair + 16, :].astype(F32)
+def load_weights(mine_ref, theirs_ref, first_row, blocks, first_core, weights):
+    for pair in range(blocks // 2):
+        rows = slice(first_row + 16 * pair, first_row + 16 * pair + 16)
+        mine = mine_ref[:, rows, :].astype(F32)
+        theirs = theirs_ref[:, 16 * pair : 16 * pair + 16, :].astype(F32)
         for part in range(2):
             rows = slice(ROWS * part, ROWS * part + ROWS)
             a = mine[:, rows, :].reshape(C, HALF)
@@ -107,172 +104,324 @@
             weights[2 * pair + part, :, 0:HALF] = jnp.where(first_core, a, b).astype(BF16)
             weights[2 * pair + part, :, HALF:C] = jnp.where(first_core, b, a).astype(BF16)
 
-    def image(at):
-        block = recv_ref[:, at : at + 16, :].astype(F32)
-        left = block[:, 0:ROWS, :].reshape(C, HALF)
-        right = block[:, ROWS : 2 * ROWS, :].reshape(C, HALF)
-        return jnp.concatenate([left, right], axis=1)
-
-    source = image(WROWS)
-    keep = image(WROWS + 16) * (1.0 / 0.9)
-    cotangent = image(WROWS + 32)
-    columns = recv_ref[:, WROWS + 48 : WROWS + 56, :].astype(F32).reshape(C, HALF)
-
-    def param(lane):
-        high = columns[:, lane : lane + 1]
-        middle_part = columns[:, PART + lane : PART + lane + 1]
-        low = columns[:, 2 * PART + lane : 2 * PART + lane + 1]
-        return high + middle_part + low
-
-    gains = [param(GAINS + j) for j in range(3)]
-    biases = [param(BIASES + j) for j in range(3)]
-
-    def store_taps(target, values):
-        for tap in range(9):
-            row_step, col_step = tap_steps(tap)
-            target[tap, :, :] = shifted(values, row_step, col_step, 1).astype(BF16)
-
-    def convolve(first_block, taps):
-        total = None
-        for tap in range(9):
-            product = dot_nn(weights[first_block + tap], taps[tap])
-            total = product if total is None else total + product
-        return total
-
-    hat_one, inverse_one = norm_hat(source)
-    pre_one = hat_one * gains[0] + biases[0]
-    first_act = (pre_one * sigmoid(pre_one)).astype(BF16).astype(F32)
-    store_taps(taps_one, first_act)
-    middle = convolve(0, taps_one) + (param(CONV_BIAS) + param(OFFSETS))
-    hat_two, inverse_two = norm_hat(middle)
-    pre_two = hat_two * gains[1] + biases[1]
-    second_act = (pre_two * sigmoid(pre_two) * keep).astype(BF16).astype(F32)
-    store_taps(taps_two, second_act)
-    residual = source + convolve(9, taps_two) + param(CONV_BIAS + 1)
-    hat_three, inverse_three = norm_hat(residual)
-    normed = (hat_three * gains[2] + biases[2]).astype(BF16)
-    queries = (dot_nn(weights[18], normed) + param(QV_BIAS)).astype(BF16)
-    keys = dot_nn(weights[19], normed).astype(BF16)
-    vals = (dot_nn(weights[20], normed) + param(QV_BIAS + 1)).astype(BF16)
+
+def load_image(ref, at):
+    block = ref[:, at : at + 16, :].astype(F32)
+    left = block[:, 0:ROWS, :].reshape(C, HALF)
+    right = block[:, ROWS : 2 * ROWS, :].reshape(C, HALF)
+    return jnp.concatenate([left, right], axis=1)
+
+
+def image_rows(values):
+    left = values[:, 0:HALF].reshape(SHARDS, ROWS, HALF)
+    right = values[:, HALF:C].reshape(SHARDS, ROWS, HALF)
+    return jnp.concatenate([left, right], axis=1).astype(BF16)
+
+
+def store_taps(target, values):
+    for tap in range(9):
+        row_step, col_step = tap_steps(tap)
+        target[tap, :, :] = shifted(values, row_step, col_step, 1).astype(BF16)
+
+
+def convolve(weights, taps):
+    total = None
+    for tap in range(9):
+        product = dot_nn(weights[tap], taps[tap])
+        total = product if total is None else total + product
+    return total
+
+
+def convolve_back(weights, low):
+    turned = low.astype(F32).T
+    total = None
+    for tap in range(9):
+        row_step, col_step = tap_steps(tap)
+        moved = shifted(turned, -row_step, -col_step, 0).astype(BF16)
+        product = dot_nn(moved, weights[tap])
+        total = product if total is None else total + product
+    return total.T
+
+
+def store_weight_grads(own_ref, swap_ref, pair, first_core, grads):
+    low = [v[:, 0:HALF].reshape(SHARDS, ROWS, HALF) for v in grads]
+    high = [v[:, HALF:C].reshape(SHARDS, ROWS, HALF) for v in grads]
+    low, high = jnp.concatenate(low, axis=1), jnp.concatenate(high, axis=1)
+    rows = slice(16 * pair, 16 * pair + 16)
+    own_ref[:, rows, :] = jnp.where(first_core, low, high).astype(BF16)
+    swap_ref[:, rows, :] = jnp.where(first_core, high, low).astype(BF16)
+
+
+def columns_of(listed):
+    lane = lax.broadcasted_iota(jnp.int32, (C, HALF), 1)
+    table = jnp.zeros((C, HALF), F32)
+    for k, column in enumerate(listed):
+        table = jnp.where(lane == k, column, table)
+    return table
+
+
+def column(ref, lane):
+    return ref[:, lane : lane + 1]
+
+
+def row_sum(values):
+    return jnp.sum(values, axis=1, keepdims=True)
+
+
+def slope(values):
+    sigma = sigmoid(values)
+    return sigma * (1.0 + values * (1.0 - sigma))
+
+
+def first_kernel(recv_ref, taps_ref, hat_ref, params_ref, stats_ref):
+    columns = recv_ref[:, AT_PARAMS : AT_PARAMS + ROWS, :].astype(F32).reshape(C, HALF)
+    columns = (
+        columns
+        + pltpu.roll(columns, HALF - PART, 1)
+        + pltpu.roll(columns, HALF - 2 * PART, 1)
+    )
+    params_ref[...] = columns
+    hat, inverse = norm_hat(load_image(recv_ref, AT_SOURCE))
+    hat_ref[...] = hat
+    stats_ref[...] = jnp.broadcast_to(inverse, (C, HALF))
+    pre = hat * columns[:, GAINS : GAINS + 1] + columns[:, BIASES : BIASES + 1]
+    store_taps(taps_ref, (pre * sigmoid(pre)).astype(BF16).astype(F32))
+
+
+def middle_kernel(
+    core_ref, recv_ref, other_ref, taps_one, params, weights, taps_ref, hat_ref, stats_ref
+):
+    load_weights(recv_ref, other_ref, 0, FIRST_BLOCKS, core_ref[0] == 0, weights)
+    middle = convolve(weights, taps_one) + (column(params, CONV_BIAS) + column(params, OFFSETS))
+    hat, inverse = norm_hat(middle)
+    hat_ref[...] = hat
+    stats_ref[...] = jnp.broadcast_to(inverse, (C, HALF))
+    pre = hat * column(params, GAINS + 1) + column(params, BIASES + 1)
+    keep = load_image(recv_ref, AT_KEEP) * (1.0 / 0.9)
+    store_taps(taps_ref, (pre * sigmoid(pre) * keep).astype(BF16).astype(F32))
+
+
+def attention_kernel(
+    core_ref, recv_ref, other_ref, taps_two, params, out_weight,
+    own_ref, swap_ref, weights, outputs_ref, attended_ref, grad_ref, sums_ref,
+):
+    first_core = core_ref[0] == 0
+    load_weights(recv_ref, other_ref, FIRST_ROWS, SECOND_BLOCKS, first_core, weights)
+    source = load_image(recv_ref, AT_SOURCE)
+    residual = source + convolve(weights, taps_two) + column(params, CONV_BIAS + 1)
+    hat, inverse = norm_hat(residual)
+    normed = (hat * column(params, GAINS + 2) + column(params, BIASES + 2)).astype(BF16)
+    queries = (dot_nn(weights[9], normed) + column(params, QV_BIAS)).astype(BF16)
+    keys = dot_nn(weights[10], normed).astype(BF16)
+    vals = (dot_nn(weights[11], normed) + column(params, QV_BIAS + 1)).astype(BF16)
     scale = C ** (-0.5)
     scores = dot_tn(queries, keys) * scale
     exps = jnp.exp(scores - jnp.max(scores, axis=1, keepdims=True))
-    probs = exps / jnp.sum(exps, axis=1, keepdims=True)
+    probs = exps / row_sum(exps)
     probs_low = probs.astype(BF16)
     attended = dot_nt(vals, probs_low).astype(BF16)
-    outputs = residual + dot_nn(weights[21], attended) + param(OUT_BIAS)
-
-    def put_image(at, values):
-        left = values[:, 0:HALF].reshape(SHARDS, ROWS, HALF)
-        right = values[:, HALF:C].reshape(SHARDS, ROWS, HALF)
-        send_ref[:, at : at + 16, :] = jnp.concatenate([left, right], axis=1).astype(BF16)
-
-    put_image(WROWS, outputs)
-
-    pending = {}
-
-    def put_weight_grad(block, values):
-        pending[block] = values
-        pair = block // 2
-        if 2 * pair in pending and 2 * pair + 1 in pending:
-            a, b = pending.pop(2 * pair), pending.pop(2 * pair + 1)
-            low = [v[:, 0:HALF].reshape(SHARDS, ROWS, HALF) for v in (a, b)]
-            high = [v[:, HALF:C].reshape(SHARDS, ROWS, HALF) for v in (a, b)]
-            low, high = jnp.concatenate(low, axis=1), jnp.concatenate(high, axis=1)
-            rows = slice(16 * pair, 16 * pair + 16)
-            send_ref[:, rows, :] = jnp.where(first_core, low, high).astype(BF16)
-            swap_ref[:, rows, :] = jnp.where(first_core, high, low).astype(BF16)
-
+    attended_ref[...] = attended
+    outputs = residual + dot_nn(out_weight[FIRST_BLOCKS - 1], attended) + column(params, OUT_BIAS)
+    outputs_ref[...] = image_rows(outputs)
+
+    cotangent = load_image(recv_ref, AT_COTANGENT)
     cot_low = cotangent.astype(BF16)
-    out_bias_grad = jnp.sum(cotangent, axis=1, keepdims=True)
-    put_weight_grad(21, dot_nt(cot_low, attended))
-    attended_grad = dot_tn(weights[21], cot_low).astype(BF16)
+    attended_grad = dot_tn(out_weight[FIRST_BLOCKS - 1], cot_low).astype(BF16)
     dprobs = dot_tn(attended_grad, vals)
-    row_dot = jnp.sum(probs * dprobs, axis=1, keepdims=True)
-    dscores = (probs * (dprobs - row_dot)).astype(BF16)
+    dscores = (probs * (dprobs - row_sum(probs * dprobs))).astype(BF16)
     query_grad = (dot_nt(keys, dscores) * scale).astype(BF16)
     key_grad = (dot_nn(queries, dscores) * scale).astype(BF16)
     value_grad = dot_nn(attended_grad, probs_low).astype(BF16)
-    query_bias_grad = jnp.sum(query_grad.astype(F32), axis=1, keepdims=True)
-    value_bias_grad = jnp.sum(value_grad.astype(F32), axis=1, keepdims=True)
     normed_grad = None
     for k, gradient in enumerate((query_grad, key_grad, value_grad)):
-        put_weight_grad(18 + k, dot_nt(gradient, normed))
-        product = dot_tn(weights[18 + k], gradient)
+        product = dot_tn(weights[9 + k], gradient)
         normed_grad = product if normed_grad is None else normed_grad + product
-    branch_three, gain_three, bias_three = norm_back(
-        hat_three, inverse_three, normed_grad, gains[2]
-    )
-    residual_grad = cotangent + branch_three
-    conv_two_bias = jnp.sum(residual_grad, axis=1, keepdims=True)
-
-    def conv_back(first_block, gradient, taps):
-        low = gradient.astype(BF16)
-        for tap in range(9):
-            put_weight_grad(first_block + tap, dot_nt(low, taps[tap]))
-        turned = low.astype(F32).T
-        total = None
-        for tap in range(9):
-            row_step, col_step = tap_steps(tap)
-            moved = shifted(turned, -row_step, -col_step, 0).astype(BF16)
-            product = dot_nn(moved, weights[first_block + tap])
-            total = product if total is None else total + product
-        return total.T
-
-    def slope(values):
-        sigma = sigmoid(values)
-        return sigma * (1.0 + values * (1.0 - sigma))
-
-    second_grad = conv_back(9, residual_grad, taps_two)
-    pre_two_grad = second_grad * keep * slope(pre_two)
-    middle_grad, gain_two, bias_two = norm_back(hat_two, inverse_two, pre_two_grad, gains[1])
-    conv_one_bias = jnp.sum(middle_grad, axis=1, keepdims=True)
-    first_grad = conv_back(0, middle_grad, taps_one)
-    pre_one_grad = first_grad * slope(pre_one)
-    branch_one, gain_one, bias_one = norm_back(hat_one, inverse_one, pre_one_grad, gains[0])
-    put_image(WROWS + 16, residual_grad + branch_one)
-
+    branch, gain_grad, bias_grad = norm_back(hat, inverse, normed_grad, column(params, GAINS + 2))
+    residual_grad = cotangent + branch
+    grad_ref[...] = residual_grad
+    low = residual_grad.astype(BF16)
+    grads = [dot_nt(low, taps_two[tap]) for tap in range(9)]
+    grads += [dot_nt(gradient, normed) for gradient in (query_grad, key_grad, value_grad)]
+    for pair in range(SECOND_BLOCKS // 2):
+        store_weight_grads(own_ref, swap_ref, pair, first_core, grads[2 * pair : 2 * pair + 2])
+    listed = {
+        D_GAINS + 2: gain_grad,
+        D_BIASES + 2: bias_grad,
+        D_CONV_BIAS + 1: row_sum(residual_grad),
+        D_QV_BIAS: row_sum(query_grad.astype(F32)),
+        D_QV_BIAS + 1: row_sum(value_grad.astype(F32)),
+        D_OUT_BIAS: row_sum(cotangent),
+    }
+    zero = jnp.zeros((C, 1), F32)
+    sums_ref[...] = columns_of([listed.get(k, zero) for k in range(PART)])
+
+
+def middle_back_kernel(
+    core_ref, recv_ref, weights, taps_one, hat_ref, stats, params, attended, grad_ref, sums,
+    own_ref, swap_ref, low_ref, sums_ref,
+):
+    second_grad = convolve_back(weights, grad_ref[...].astype(BF16))
+    hat = hat_ref[...]
+    gain = column(params, GAINS + 1)
+    pre = hat * gain + column(params, BIASES + 1)
+    keep = load_image(recv_ref, AT_KEEP) * (1.0 / 0.9)
+    pre_grad = second_grad * keep * slope(pre)
+    middle_grad, gain_grad, bias_grad = norm_back(hat, column(stats, 0), pre_grad, gain)
+    low = middle_grad.astype(BF16)
+    low_ref[...] = low
+    grads = [dot_nt(low, taps_one[tap]) for tap in range(9)]
+    grads += [dot_nt(load_image(recv_ref, AT_COTANGENT).astype(BF16), attended[...])]
+    for pair in range(FIRST_BLOCKS // 2):
+        store_weight_grads(
+            own_ref, swap_ref, pair, core_ref[0] == 0, grads[2 * pair : 2 * pair + 2]
+        )
+    listed = {D_GAINS + 1: gain_grad, D_BIASES + 1: bias_grad, D_CONV_BIAS: row_sum(middle_grad)}
+    zero = jnp.zeros((C, 1), F32)
+    sums_ref[...] = sums[...] + columns_of([listed.get(k, zero) for k in range(PART)])
+
+
+def first_back_kernel(
+    weights, hat_ref, stats, params, low_ref, grad_ref, sums, outputs, own, swapped, send_ref
+):
+    first_grad = convolve_back(weights, low_ref[...])
+    hat = hat_ref[...]
+    gain = column(params, GAINS)
+    pre = hat * gain + column(params, BIASES)
+    branch, gain_grad, bias_grad = norm_back(hat, column(stats, 0), first_grad * slope(pre), gain)
+    for pair in range(SECOND_BLOCKS // 2):
+        rows = slice(16 * pair, 16 * pair + 16)
+        both = own[:, rows, :].astype(F32) + swapped[:, rows, :].astype(F32)
+        to = FIRST_ROWS + 16 * pair
+        send_ref[:, to : to + 16, :] = both.astype(BF16)
+    send_ref[:, WROWS : WROWS + 16, :] = outputs[...]
+    send_ref[:, WROWS + 16 : WROWS + 32, :] = image_rows(grad_ref[...] + branch)
+
+    zero = jnp.zeros((C, 1), F32)
+    listed = {D_GAINS: gain_grad, D_BIASES: bias_grad}
+    table = sums[...] + columns_of([listed.get(k, zero) for k in range(PART)])
+    high = table.astype(BF16).astype(F32)
+    low = pltpu.roll(table - high, PART, 1)
     lane = lax.broadcasted_iota(jnp.int32, (C, HALF), 1)
-    table = jnp.zeros((C, HALF), F32)
-    listed = (
-        gain_one, gain_two, gain_three, bias_one, bias_two, bias_three,
-        conv_one_bias, conv_two_bias, query_bias_grad, value_bias_grad, out_bias_grad,
-    )
-    for k, column in enumerate(listed):
-        table = jnp.where((lane & (PART - 1)) == k, column, table)
-    high = table.astype(BF16).astype(F32)
-    table = jnp.where(lane < PART, high, jnp.where(lane < 2 * PART, table - high, 0.0))
+    table = jnp.where(lane < PART, high, low)
     send_ref[:, WROWS + 32 : WROWS + 40, :] = table.reshape(SHARDS, ROWS, HALF).astype(BF16)
 
 
+AT_SOURCE, AT_KEEP, AT_COTANGENT, AT_PARAMS = WROWS, WROWS + 16, WROWS + 32, WROWS + 48
 IN_ROWS = WROWS + 56
 OUT_ROWS = WROWS + 40
-
-
-def run_block(core, received, other):
+FIRST_BLOCKS, SECOND_BLOCKS = 10, 12
+FIRST_ROWS, SECOND_ROWS = FIRST_BLOCKS * ROWS, SECOND_BLOCKS * ROWS
+
+
+def local_call(kernel, core, *operands, out):
+    in_specs = [pl.BlockSpec(memory_space=pltpu.VMEM) for _ in operands]
+    if core is not None:
+        in_specs = [pl.BlockSpec(memory_space=pltpu.SMEM)] + in_specs
+        operands = (core, *operands)
+    shapes = tuple(jax.ShapeDtypeStruct(shape, dtype) for shape, dtype in out)
     return pl.pallas_call(
-        block_kernel,
-        out_shape=(
-            jax.ShapeDtypeStruct((SHARDS, OUT_ROWS, HALF), BF16),
-            jax.ShapeDtypeStruct((SHARDS, WROWS, HALF), BF16),
-        ),
-        in_specs=[
-            pl.BlockSpec(memory_space=pltpu.SMEM),
-            pl.BlockSpec(memory_space=pltpu.VMEM),
-            pl.BlockSpec(memory_space=pltpu.VMEM),
-        ],
-        out_specs=(
-            pl.BlockSpec(memory_space=pltpu.VMEM),
-            pl.BlockSpec(memory_space=pltpu.VMEM),
-        ),
-        scratch_shapes=[
-            pltpu.VMEM((WBLOCKS, C, C), BF16),
-            pltpu.VMEM((9, C, POS), BF16),
-            pltpu.VMEM((9, C, POS), BF16),
-            pltpu.VMEM((9, POS, C), BF16),
-        ],
-        compiler_params=pltpu.CompilerParams(vmem_limit_bytes=24 * 1024 * 1024),
-    )(core, received, other)
+        kernel,
+        out_shape=shapes,
+        in_specs=in_specs,
+        out_specs=tuple(pl.BlockSpec(memory_space=pltpu.VMEM) for _ in out),
+        compiler_params=pltpu.CompilerParams(vmem_limit_bytes=VMEM_LIMIT),
+    )(*operands)
+
+
+VMEM_LIMIT = 24 * 1024 * 1024
+
+
+def run_block(core, received, swap):
+    other_one = swap(received[:, :FIRST_ROWS])
+    other_two = swap(received[:, FIRST_ROWS:WROWS])
+    image, table = ((C, POS), F32), ((C, HALF), F32)
+    taps, low = ((9, C, POS), BF16), ((C, POS), BF16)
+
+    taps_one, hat_one, params, stats_one = local_call(
+        first_kernel, None, received, out=(taps, image, table, table)
+    )
+    weights_one, taps_two, hat_two, stats_two = local_call(
+        middle_kernel, core, received, other_one, taps_one, params,
+        out=(((FIRST_BLOCKS, C, C), BF16), taps, image, table),
+    )
+    second = ((SHARDS, SECOND_ROWS, HALF), BF16)
+    rows = ((SHARDS, 16, HALF), BF16)
+    own_two, swap_two, weights_two, outputs, attended, residual_grad, sums = local_call(
+        attention_kernel, core, received, other_two, taps_two, params, weights_one,
+        out=(second, second, ((SECOND_BLOCKS, C, C), BF16), rows, low, image, table),
+    )
+    swapped_two = swap(swap_two)
+    first = ((SHARDS, FIRST_ROWS, HALF), BF16)
+    own_one, swap_one, middle_low, sums = local_call(
+        middle_back_kernel, core, received, weights_two, taps_one, hat_two, stats_two, params,
+        attended, residual_grad, sums, out=(first, first, low, table),
+    )
+    swapped_one = swap(swap_one)
+    (send,) = local_call(
+        first_back_kernel, None, weights_one, hat_one, stats_one, params, middle_low,
+        residual_grad, sums, outputs, own_two, swapped_two,
+        out=(((SHARDS, OUT_ROWS, HALF), BF16),),
+    )
+    both = (own_one.astype(F32) + swapped_one.astype(F32)).astype(BF16)
+    return lax.dynamic_update_slice(send, both, (0, 0, 0))
+
+
+def collect_kernel(back_ref, swished_ref, sums_ref):
+    for pair in range(WROWS // 16):
+        rows = slice(16 * pair, 16 * pair + 16)
+        total = back_ref[0, rows, :].astype(F32)
+        for image in range(1, SHARDS):
+            total = total + back_ref[image, rows, :].astype(F32)
+        sums_ref[rows, :] = total.astype(BF16)
+    small = back_ref[:, WROWS + 32 : WROWS + 40, :].astype(F32)
+    table = jnp.zeros((ROWS, HALF), F32)
+    temb = jnp.zeros((ROWS, TEMB), F32)
+    for image in range(SHARDS):
+        values = small[image] + pltpu.roll(small[image], HALF - PART, 1)
+        table = table + values
+        offsets_grad = values[:, D_CONV_BIAS : D_CONV_BIAS + 1]
+        temb = temb + offsets_grad * swished_ref[image : image + 1, :]
+    lane = lax.broadcasted_iota(jnp.int32, (ROWS, HALF), 1)
+    high = table.astype(BF16).astype(F32)
+    low = pltpu.roll(table - high, PART, 1)
+    parts = jnp.where(lane < PART, high, jnp.where(lane < 2 * PART, low, 0.0))
+    blocks = [parts] + [temb[:, HALF * k : HALF * k + HALF] for k in range(TEMB // HALF)]
+    blocks = blocks + [jnp.zeros((ROWS, HALF), F32)]
+    for pair in range(len(blocks) // 2):
+        rows = slice(WROWS + 16 * pair, WROWS + 16 * pair + 16)
+        both = jnp.concatenate(blocks[2 * pair : 2 * pair + 2], axis=0)
+        sums_ref[rows, :] = both.astype(BF16)
+
+
+SUM_ROWS = WROWS + ROWS + TEMB * ROWS // HALF + ROWS
+
+
+def collect(back, swished):
+    return pl.pallas_call(
+        collect_kernel,
+        out_shape=jax.ShapeDtypeStruct((SUM_ROWS, HALF), BF16),
+        in_specs=[pl.BlockSpec(memory_space=pltpu.VMEM)] * 2,
+        out_specs=pl.BlockSpec(memory_space=pltpu.VMEM),
+        compiler_params=pltpu.CompilerParams(vmem_limit_bytes=8 * 1024 * 1024),
+    )(back, swished)
+
+
+def images_kernel(back_ref, outputs_ref, grad_ref):
+    for at, target in ((WROWS, outputs_ref), (WROWS + 16, grad_ref)):
+        block = back_ref[:, at : at + 16, :].astype(F32)
+        cut = jnp.concatenate([block[:, :ROWS, :], block[:, ROWS:, :]], axis=2)
+        target[...] = jnp.swapaxes(cut, 0, 1).astype(BF16)
+
+
+def images(back):
+    shape = jax.ShapeDtypeStruct((ROWS, SHARDS, POS), BF16)
+    return pl.pallas_call(
+        images_kernel,
+        out_shape=(shape, shape),
+        in_specs=[pl.BlockSpec(memory_space=pltpu.VMEM)],
+        out_specs=(pl.BlockSpec(memory_space=pltpu.VMEM), pl.BlockSpec(memory_space=pltpu.VMEM)),
+        compiler_params=pltpu.CompilerParams(vmem_limit_bytes=8 * 1024 * 1024),
+    )(back)
 
 
 def finish_kernel(core_ref, mine_ref, theirs_ref, *refs):
@@ -288,20 +437,22 @@
         )
 
     copies = [pltpu.make_async_copy(scratch[k], results[k], sems.at[k]) for k in range(10)]
-    for block in range(18):
-        conv_w[block // 9, block % 9, :, :] = weight_grad(block)
+    for conv in range(2):
+        for tap in range(9):
+            conv_w[conv, tap, :, :] = weight_grad(FIRST_BLOCKS * conv + tap)
     copies[2].start()
     for k in range(3):
-        qkv_w[k, :, :] = weight_grad(18 + k)
+        qkv_w[k, :, :] = weight_grad(FIRST_BLOCKS + 9 + k)
     copies[6].start()
-    out_w[...] = weight_grad(21)
+    out_w[...] = weight_grad(FIRST_BLOCKS - 1)
     copies[8].start()
     shared = mine_ref[WROWS:, :] + theirs_ref[WROWS:, :]
+    small = shared[:ROWS, :] + pltpu.roll(shared[:ROWS, :], HALF - PART, 1)
     for part in range(TEMB // HALF):
         rows = slice(ROWS + ROWS * part, 2 * ROWS + ROWS * part)
         temb_w[:, HALF * part : HALF * part + HALF] = shared[rows, :]
     copies[4].start()
-    padded = jnp.concatenate([shared[:ROWS, :], jnp.zeros((HALF - ROWS, HALF), F32)], axis=0)
+    padded = jnp.concatenate([small, jnp.zeros((HALF - ROWS, HALF), F32)], axis=0)
     table = padded.T[:PART, :ROWS]
     gain[...] = table[D_GAINS : D_GAINS + 3]
     bias[...] = table[D_BIASES : D_BIASES + 3]
@@ -400,9 +551,10 @@
 
     shard = jnp.concatenate(
         [
-            half(conv_ref[...].reshape(18 * ROWS, C)),
+            half(conv_ref[0].reshape(9 * ROWS, C)),
+            half(out_ref[...]),
+            half(conv_ref[1].reshape(9 * ROWS, C)),
             half(qkv_ref[...].reshape(3 * ROWS, C)),
-            half(out_ref[...]),
         ],
         axis=0,
     ).astype(BF16)
@@ -437,11 +589,6 @@
         + [pltpu.VMEM((SHARDS, TEMB // 2), F32), pltpu.SemaphoreType.DMA((PREPARE_ARRAYS,))],
         compiler_params=pltpu.CompilerParams(vmem_limit_bytes=16 * 1024 * 1024),
     )(core, *[pltpu.with_memory_space_constraint(a, pltpu.HBM) for a in (timesteps, *arrays)])
-
-
-def whole(blocks):
-    turned = blocks.transpose(1, 0, 2)
-    return jnp.concatenate([turned[:ROWS], turned[ROWS:]], axis=2)
 
 
 def on_device(
@@ -464,8 +611,6 @@
     core = member % 2
     core_pairs = [(m, m ^ 1) for m in range(4)]
     plane_pairs = [(m, m ^ 2) for m in range(4)]
-    highest = lax.Precision.HIGHEST
-
     sent, swished = prepare(
         core.reshape(1),
         timesteps,
@@ -484,30 +629,16 @@
         cotangent,
     )
     received = lax.all_to_all(sent, "ch", split_axis=0, concat_axis=0, tiled=True)
-    other = lax.ppermute(received, "img", core_pairs)
-
-    send, swap = run_block(core.reshape(1), received, other)
-
-    swapped = lax.ppermute(swap, "img", core_pairs)
-    send = send + jnp.pad(swapped, ((0, 0), (0, OUT_ROWS - WROWS), (0, 0)))
+    send = run_block(
+        core.reshape(1), received, lambda values: lax.ppermute(values, "img", core_pairs)
+    )
     back = lax.all_to_all(send, "ch", split_axis=0, concat_axis=0, tiled=True)
 
-    outputs = whole(back[:, WROWS : WROWS + 16])
-    input_grad = whole(back[:, WROWS + 16 : WROWS + 32])
-    weight_sums = jnp.sum(back[:, :WROWS].astype(F32), axis=0)
-    small = back[:, WROWS + 32 :].astype(F32)
-    small = small[:, :, :PART] + small[:, :, PART : 2 * PART]
-    offsets_grad = small[:, :, D_CONV_BIAS]
-    temb_grad = lax.dot_general(
-        offsets_grad, swished, (((0,), (0,)), ((), ())), precision=highest,
-        preferred_element_type=F32,
-    )
-    small_sums = jnp.pad(jnp.sum(small, axis=0), ((0, 0), (0, HALF - PART)))
-    temb_rows = [temb_grad[:, HALF * k : HALF * k + HALF] for k in range(TEMB // HALF)]
-    sums = jnp.concatenate([weight_sums, small_sums, *temb_rows], axis=0)
+    sums = collect(back, swished)
     plane = lax.ppermute(sums, "img", plane_pairs)
+    outputs, input_grad = images(back)
     plane, outputs, input_grad = lax.optimization_barrier((plane, outputs, input_grad))
-    sums = sums + plane
+    sums = sums.astype(F32) + plane.astype(F32)
     theirs = lax.ppermute(sums, "img", core_pairs)
     (gain, bias, conv_w, conv_b, temb_w, temb_b, qkv_w, qv_b, out_w, out_b) = finish(
         core.reshape(1), sums, theirs

time: 95.6 us -> 91.9 us (0.961)
  waiting for transfers between devices: 9.11 us -> 5.14 us
  Pallas kernels: 9.97 us -> 12.3 us
  local copies, waits for them, and re-layouts: 1.67 us -> 0.09 us
    ppermute x2 -> x4, waiting for transfers between devices: 6.37 us -> 2.71 us  [on_device(): lax.ppermute(values, 'img', core_pairs)]
    pallas_call x1 -> x7, Pallas kernels: 7.5 us -> 9.76 us  [the longest x5 8.66 us: local_call(): pl.pallas_call(kernel, out_shape=shapes, in_specs=in_specs, out_specs=tup...]
    unnamed x7 -> x0, local copies, waits for them, and re-layouts: 1.38 us -> none
    ppermute x1, waiting for transfers between devices: 2.73 us -> 1.47 us  [on_device(): plane = lax.ppermute(sums, 'img', plane_pairs)]
    ppermute x1, waiting for transfers between devices: 0.01 us -> 0.97 us  [on_device(): theirs = lax.ppermute(sums, 'img', core_pairs)]
    ppermute x2 -> x4, starting transfers between devices: 2.91 us -> 3.32 us  [on_device(): lax.ppermute(values, 'img', core_pairs)]
  transfers between devices with their start and end apart: 4 -> 6, of which waited for: 3 -> 4; matrix products, arithmetic and copies ran while one was open for 2% -> 0% of each run, Pallas kernels for 0% -> 6%
where the time goes in v3:
time: 91.9 us; the launch traced here: 91.7 us
  blocking collectives  66.1 us (72%)
  Pallas kernels  12.3 us (13%)
  starting transfers between devices  7.12 us (8%)
  waiting for transfers between devices  5.14 us (6%)
    all_to_all x1, blocking collectives, on_device(): lax.all_to_all(sent, 'ch', split_axis=0, concat_axis=0, tiled=True)  37 us
    all_to_all x1, blocking collectives, on_device(): back = lax.all_to_all(send, 'ch', split_axis=0, concat_axis=0, tiled=True)  29.1 us
    pallas_call x5, Pallas kernels, local_call(): pl.pallas_call(kernel, out_shape=shapes, in_specs=in_specs, out_specs=tup...  8.66 us
    ppermute x4, starting transfers between devices, on_device(): lax.ppermute(values, 'img', core_pairs)  3.32 us
    ppermute x1, starting transfers between devices, on_device(): theirs = lax.ppermute(sums, 'img', core_pairs)  2.95 us
    ppermute x4, waiting for transfers between devices, on_device(): lax.ppermute(values, 'img', core_pairs)  2.71 us
  transfers between devices with their start and end apart: 6, of which 4 were waited for; matrix products, arithmetic and copies ran while one was open for 0% of the time, Pallas kernels for 6%

profile of v3, /device:TPU:1, one launch (start us, length us, event | category | flops | bytes accessed | tf_op | source)
XLA Modules:
  0.0 91.7 jit_solution(9035363426035755858)
XLA Ops:
  0.7 1.7 %shard_map.229 = (bf16[32,232,128]{2,1,0:T(8,128)(2,1)S(1)}, f32[32,512]{1,0:T(8,128)S(1)}) custom-call(s32[1]{0:T(128)} %bitcast.core_ref, s32[32]{0:T(128)} %refs_0_.1, f32[3,8]{1,0:T(4,128)} %refs_1_.1, f32[3,8]{1,0:T(4,128)} %refs_2_.1, f32[2,8]{1,0:T(2,128)} %refs_3_.1, f32[2,8]{1,0:T(2,128)} %refs_4_.1, f32[1,8]{1,0:T(1,128)} %bitcast.8, ...), custom_call_target="tpu_custom_call" | custom-call | tf_op jit(solution)/shard_map/pallas_call | solution.py:579
  2.4 37.0 %all_to_all.10.recv_ref = bf16[32,232,128]{2,1,0:T(8,128)(2,1)S(1)} all-to-all(bf16[32,232,128]{2,1,0:T(8,128)(2,1)S(1)} %get-tuple-element.48), channel_id=1, replica_groups=mesh['ch'=32,'img'=4] {'ch'}, dimensions={0} | all-to-all | bytes 3801088 | tf_op jit(solution)/shard_map/all_to_all | solution.py:631
  39.4 0.1 slice.9
  39.5 2.6 %collective-permute-start.1 = (bf16[32,96,128]{2,1,0:T(8,128)(2,1)S(1)}, bf16[32,96,128]{2,1,0:T(8,128)(2,1)S(1)}, u32[]{:S(2)}, u32[]{:S(2)}) collective-permute-start(bf16[32,96,128]{2,1,0:T(8,128)(2,1)S(1)} %slice.9), channel_id=1, source_target_pairs={{0,1},{1,0},{2,3},{3,2},{4,5},{5,4},{6,7},{7,6},{8,9},{9,8},{10,11... | collective-permute-start | bytes 2359304 | tf_op jit(solution)/shard_map/ppermute | solution.py:633
  42.1 0.1 collective-permute-start
  42.2 0.7 shard_map.230
  42.9 1.9 %collective-permute-done.other_ref = bf16[32,80,128]{2,1,0:T(8,128)(2,1)S(1)} collective-permute-done((bf16[32,80,128]{2,1,0:T(8,128)(2,1)S(1)}, bf16[32,80,128]{2,1,0:T(8,128)(2,1)S(1)}, u32[]{:S(2)}, u32[]{:S(2)}) %collective-permute-start) | collective-permute-done | bytes 655392 | tf_op jit(solution)/shard_map/ppermute | solution.py:633
  44.9 1.0 %shard_map.231 = (bf16[10,256,256]{2,1,0:T(8,128)(2,1)S(1)}, bf16[9,256,256]{2,1,0:T(8,128)(2,1)S(1)}, f32[256,256]{1,0:T(8,128)S(1)}, f32[256,128]{1,0:T(8,128)S(1)}) custom-call(s32[1]{0:T(128)} %bitcast.core_ref, bf16[32,232,128]{2,1,0:T(8,128)(2,1)S(1)} %all_to_all.10.recv_ref, bf16[32,80,128]{2,1,0:T(8,128)(2,1)S(1)} %collective-permute-done.other_ref, ...), custom_call_target="tpu_custom_call" | custom-call | tf_op jit(solution)/shard_map/pallas_call | solution.py:322
  45.9 0.0 collective-permute-done.1.other_ref
  45.9 3.8 %shard_map.232 = (bf16[32,96,128]{2,1,0:T(8,128)(2,1)S(1)}, bf16[32,96,128]{2,1,0:T(8,128)(2,1)S(1)}, bf16[12,256,256]{2,1,0:T(8,128)(2,1)S(1)}, bf16[32,16,128]...) custom-call(s32[1]{0:T(128)} %bitcast.core_ref, ...), custom_call_target="tpu_custom_call" | custom-call | tf_op jit(solution)/shard_map/pallas_call | solution.py:322
  49.7 0.5 collective-permute-start.2
  50.2 1.9 %shard_map.233 = (bf16[32,80,128]{2,1,0:T(8,128)(2,1)S(1)}, bf16[32,80,128]{2,1,0:T(8,128)(2,1)S(1)}, bf16[256,256]{1,0:T(8,128)(2,1)S(1)}, f32[256,128]{1,0:T(8,128)S(1)}) custom-call(s32[1]{0:T(128)} %bitcast.core_ref, bf16[32,232,128]{2,1,0:T(8,128)(2,1)S(1)} %all_to_all.10.recv_ref, bf16[12,256,256]{2,1,0:T(8,128)(2,1)S(1)} %get-tuple-element.55.weights, ...), custom_call_target="tpu_custom_call" | custom-call | tf_op jit(solution)/shard_map/pallas_call | solution.py:322
  52.1 0.2 collective-permute-start.3
  52.3 0.0 collective-permute-done.2.swapped
  52.3 1.2 %shard_map.234 = bf16[32,216,128]{2,1,0:T(8,128)(2,1)S(1)} custom-call(bf16[10,256,256]{2,1,0:T(8,128)(2,1)S(1)} %get-tuple-element.51.out_weight.weights, f32[256,256]{1,0:T(8,128)S(1)} %get-tuple-element.52.hat_ref, f32[256,128]{1,0:T(8,128)S(1)} %get-tuple-element.53.stats, f32[256,128]{1,0:T(8,128)S(1)} %get-tuple-element.50.params, ...), custom_call_target="tpu_custom_call" | custom-call | tf_op jit(solution)/shard_map/pallas_call | solution.py:322
  53.5 0.8 collective-permute-done.3
  54.2 0.2 fusion
  54.4 29.1 %all_to_all.11.back_ref = bf16[32,216,128]{2,1,0:T(8,128)(2,1)S(1)} all-to-all(bf16[32,216,128]{2,1,0:T(8,128)(2,1)S(1)} %fusion), channel_id=1, replica_groups=mesh['ch'=32,'img'=4] {'ch'}, dimensions={0} | all-to-all | bytes 3538944 | tf_op jit(solution)/shard_map/all_to_all | solution.py:635
  83.5 0.3 shard_map.235
  83.8 0.8 collective-permute-start.4
  84.7 0.8 shard_map.236
  85.5 1.5 %collective-permute-done.4 = bf16[224,128]{1,0:T(8,128)(2,1)S(1)} collective-permute-done((bf16[224,128]{1,0:T(8,128)(2,1)S(1)}, bf16[224,128]{1,0:T(8,128)(2,1)S(1)}, u32[]{:S(2)}, u32[]{:S(2)}) %collective-permute-start.4) | collective-permute-done | bytes 57376 | tf_op jit(solution)/shard_map/ppermute | solution.py:638
  87.0 2.9 %collective-permute-start.5 = (f32[224,128]{1,0:T(8,128)S(1)}, f32[224,128]{1,0:T(8,128)S(1)}, u32[]{:S(2)}, u32[]{:S(2)}) collective-permute-start(f32[224,128]{1,0:T(8,128)S(1)} %convert_add_fusion.mine_ref), channel_id=1, source_target_pairs={{0,1},{1,0},{2,3},{3,2},{4,5},{5,4},{6,7},{7,6},{8,9},{9,8},{10,11... | collective-permute-start | bytes 344072 | tf_op jit(solution)/shard_map/ppermute | solution.py:642
  89.9 1.0 %collective-permute-done.5.theirs_ref = f32[224,128]{1,0:T(8,128)S(1)} collective-permute-done((f32[224,128]{1,0:T(8,128)S(1)}, f32[224,128]{1,0:T(8,128)S(1)}, u32[]{:S(2)}, u32[]{:S(2)}) %collective-permute-start.5) | collective-permute-done | bytes 114720 | tf_op jit(solution)/shard_map/ppermute | solution.py:642
  90.9 0.8 shard_map.237
  (2 shorter events, 0.1 us)
Async XLA Ops:
  39.5 6.5 %collective-permute-start.1 = (bf16[32,96,128]{2,1,0:T(8,128)(2,1)S(1)}, bf16[32,96,128]{2,1,0:T(8,128)(2,1)S(1)}, u32[]{:S(2)}, u32[]{:S(2)}) collective-permute-start(bf16[32,96,128]{2,1,0:T(8,128)(2,1)S(1)} %slice.9), channel_id=1, source_target_pairs={{0,1},{1,0},{2,3},{3,2},{4,5},{5,4},{6,7},{7,6},{8,9},{9,8},{10,11... | collective-permute-start | bytes 2359304 | tf_op jit(solution)/shard_map/ppermute | solution.py:633
  42.1 2.8 %collective-permute-start = (bf16[32,80,128]{2,1,0:T(8,128)(2,1)S(1)}, bf16[32,80,128]{2,1,0:T(8,128)(2,1)S(1)}, u32[]{:S(2)}, u32[]{:S(2)}) collective-permute-start(bf16[32,80,128]{2,1,0:T(8,128)(2,1)S(1)} %slice.8), channel_id=1, source_target_pairs={{0,1},{1,0},{2,3},{3,2},{4,5},{5,4},{6,7},{7,6},{8,9},{9,8},{10,11... | collective-permute-start | bytes 1966088 | tf_op jit(solution)/shard_map/ppermute | solution.py:633
  49.7 2.6 %collective-permute-start.2 = (bf16[32,96,128]{2,1,0:T(8,128)(2,1)S(1)}, bf16[32,96,128]{2,1,0:T(8,128)(2,1)S(1)}, u32[]{:S(2)}, u32[]{:S(2)}) collective-permute-start(bf16[32,96,128]{2,1,0:T(8,128)(2,1)S(1)} %get-tuple-element.65), channel_id=1, source_target_pairs={{0,1},{1,0},{2,3},{3,2},{4,5},{5,4},{6,7},{7,6},{8,9},{9,8},{10,11... | collective-permute-start | bytes 2359304 | tf_op jit(solution)/shard_map/ppermute | solution.py:633
  52.1 2.2 %collective-permute-start.3 = (bf16[32,80,128]{2,1,0:T(8,128)(2,1)S(1)}, bf16[32,80,128]{2,1,0:T(8,128)(2,1)S(1)}, u32[]{:S(2)}, u32[]{:S(2)}) collective-permute-start(bf16[32,80,128]{2,1,0:T(8,128)(2,1)S(1)} %get-tuple-element.67), channel_id=1, source_target_pairs={{0,1},{1,0},{2,3},{3,2},{4,5},{5,4},{6,7},{7,6},{8,9},{9,8},{10,11... | collective-permute-start | bytes 1966088 | tf_op jit(solution)/shard_map/ppermute | solution.py:633
  83.8 3.1 %collective-permute-start.4 = (bf16[224,128]{1,0:T(8,128)(2,1)S(1)}, bf16[224,128]{1,0:T(8,128)(2,1)S(1)}, u32[]{:S(2)}, u32[]{:S(2)}) collective-permute-start(bf16[224,128]{1,0:T(8,128)(2,1)S(1)} %shard_map.235), channel_id=1, source_target_pairs={{0,2},{1,3},{2,0},{3,1},{4,6},{5,7},{6,4},{7,5},{8,10},{9,11},{10,... | collective-permute-start | bytes 172040 | tf_op jit(solution)/shard_map/ppermute | solution.py:638
  87.0 3.9 %collective-permute-start.5 = (f32[224,128]{1,0:T(8,128)S(1)}, f32[224,128]{1,0:T(8,128)S(1)}, u32[]{:S(2)}, u32[]{:S(2)}) collective-permute-start(f32[224,128]{1,0:T(8,128)S(1)} %convert_add_fusion.mine_ref), channel_id=1, source_target_pairs={{0,1},{1,0},{2,3},{3,2},{4,5},{5,4},{6,7},{7,6},{8,9},{9,8},{10,11... | collective-permute-start | bytes 344072 | tf_op jit(solution)/shard_map/ppermute | solution.py:642

commit v4 on v3

--- a/solution.py
+++ b/solution.py
@@ -71,25 +71,21 @@
     return 1.0 / (1.0 + jnp.exp(-values))
 
 
-def tap_steps(tap):
-    return tap // 3 - 1, tap % 3 - 1
-
-
-def shifted(values, row_step, col_step, axis):
-    if row_step == 0 and col_step == 0:
-        return values
-    moved = pltpu.roll(values, (-(row_step * SIDE + col_step)) % POS, axis)
+def rolled(values, steps, axis):
+    return pltpu.roll(values, steps % POS, axis)
+
+
+def column_shifted(values, step, axis):
     shape = (1, POS) if axis == 1 else (POS, POS)
-    cell = lax.broadcasted_iota(jnp.int32, shape, axis)
-    valid = None
-    if col_step:
-        column = (cell & (SIDE - 1)) + col_step
-        valid = (column >= 0) & (column < SIDE)
-    if row_step:
-        row = cell + row_step * SIDE
-        inside = (row >= 0) & (row < POS)
-        valid = inside if valid is None else valid & inside
-    return moved * valid.astype(F32)
+    cell = (lax.broadcasted_iota(jnp.int32, shape, axis) & (SIDE - 1)) + step
+    valid = (cell >= 0) & (cell < SIDE)
+    return rolled(values, -step, axis) * valid.astype(F32)
+
+
+def row_shifted(values, step):
+    cell = lax.broadcasted_iota(jnp.int32, (1, POS), 1) + step * SIDE
+    valid = (cell >= 0) & (cell < POS)
+    return rolled(values, -step * SIDE, 1) * valid.astype(F32)
 
 
 def load_weights(mine_ref, theirs_ref, first_row, blocks, first_core, weights):
@@ -118,38 +114,71 @@
     return jnp.concatenate([left, right], axis=1).astype(BF16)
 
 
-def store_taps(target, values):
-    for tap in range(9):
-        row_step, col_step = tap_steps(tap)
-        target[tap, :, :] = shifted(values, row_step, col_step, 1).astype(BF16)
-
-
-def convolve(weights, taps):
+def store_shifts(target, values):
+    for step in (-1, 0, 1):
+        moved = (column_shifted(values, step, 1) if step else values).astype(BF16)
+        target[0, step + 1, :, :] = moved[:HALF]
+        target[1, step + 1, :, :] = moved[HALF:]
+
+
+def convolve(weights, shifts):
+    stacked = jnp.concatenate([shifts[k % 2, k // 2] for k in range(6)], axis=0)
     total = None
-    for tap in range(9):
-        product = dot_nn(weights[tap], taps[tap])
-        total = product if total is None else total + product
+    for row in (0, -1, 1):
+        matrix = jnp.concatenate([weights[3 * row + 3 + k] for k in range(3)], axis=1)
+        product = dot_nn(matrix, stacked)
+        total = product if row == 0 else total + row_shifted(product, row)
     return total
 
 
 def convolve_back(weights, low):
-    turned = low.astype(F32).T
+    turned = low.astype(F32).T.astype(BF16)
+    edge = jnp.zeros((SIDE, C), BF16)
+    stacked = jnp.concatenate(
+        [
+            jnp.concatenate([turned[SIDE:], edge], axis=0),
+            turned,
+            jnp.concatenate([edge, turned[:-SIDE]], axis=0),
+        ],
+        axis=1,
+    )
     total = None
-    for tap in range(9):
-        row_step, col_step = tap_steps(tap)
-        moved = shifted(turned, -row_step, -col_step, 0).astype(BF16)
-        product = dot_nn(moved, weights[tap])
-        total = product if total is None else total + product
+    for step in (0, -1, 1):
+        matrix = jnp.concatenate([weights[3 * k + step + 1] for k in range(3)], axis=0)
+        product = dot_nn(stacked, matrix)
+        total = product if step == 0 else total + column_shifted(product, -step, 0)
     return total.T
 
 
-def store_weight_grads(own_ref, swap_ref, pair, first_core, grads):
-    low = [v[:, 0:HALF].reshape(SHARDS, ROWS, HALF) for v in grads]
-    high = [v[:, HALF:C].reshape(SHARDS, ROWS, HALF) for v in grads]
-    low, high = jnp.concatenate(low, axis=1), jnp.concatenate(high, axis=1)
-    rows = slice(16 * pair, 16 * pair + 16)
-    own_ref[:, rows, :] = jnp.where(first_core, low, high).astype(BF16)
-    swap_ref[:, rows, :] = jnp.where(first_core, high, low).astype(BF16)
+def own_first(ref, core):
+    count = math.prod(ref.shape[1:-1])
+    halves = [ref[core].reshape(count, POS), ref[1 - core].reshape(count, POS)]
+    return jnp.concatenate(halves, axis=0)
+
+
+def store_weight_grads(own_ref, swap_ref, first_block, products):
+    for target, at in ((own_ref, 0), (swap_ref, 1)):
+        blocks = []
+        for product in products:
+            lanes = product.shape[1] // 2
+            for k in range(lanes // HALF):
+                start = at * lanes + k * HALF
+                blocks.append(product[:, start : start + HALF].reshape(SHARDS, ROWS, HALF))
+        for pair in range(len(blocks) // 2):
+            rows = slice((first_block + 2 * pair) * ROWS, (first_block + 2 * pair + 2) * ROWS)
+            target[:, rows, :] = jnp.concatenate(
+                blocks[2 * pair : 2 * pair + 2], axis=1
+            ).astype(BF16)
+
+
+def conv_weight_grads(low, shifts, core):
+    wide = low.astype(F32)
+    operand = own_first(shifts, core)
+    grads = []
+    for row in (-1, 0, 1):
+        moved = row_shifted(wide, -row).astype(BF16) if row else low
+        grads.append(dot_nt(moved, operand))
+    return grads
 
 
 def columns_of(listed):
@@ -185,65 +214,67 @@
     hat_ref[...] = hat
     stats_ref[...] = jnp.broadcast_to(inverse, (C, HALF))
     pre = hat * columns[:, GAINS : GAINS + 1] + columns[:, BIASES : BIASES + 1]
-    store_taps(taps_ref, (pre * sigmoid(pre)).astype(BF16).astype(F32))
+    store_shifts(taps_ref, (pre * sigmoid(pre)).astype(BF16).astype(F32))
 
 
 def middle_kernel(
     core_ref, recv_ref, other_ref, taps_one, params, weights, taps_ref, hat_ref, stats_ref
 ):
-    load_weights(recv_ref, other_ref, 0, FIRST_BLOCKS, core_ref[0] == 0, weights)
+    load_weights(recv_ref, other_ref, 0, IN_CUT, core_ref[0] == 0, weights)
     middle = convolve(weights, taps_one) + (column(params, CONV_BIAS) + column(params, OFFSETS))
     hat, inverse = norm_hat(middle)
     hat_ref[...] = hat
     stats_ref[...] = jnp.broadcast_to(inverse, (C, HALF))
     pre = hat * column(params, GAINS + 1) + column(params, BIASES + 1)
     keep = load_image(recv_ref, AT_KEEP) * (1.0 / 0.9)
-    store_taps(taps_ref, (pre * sigmoid(pre) * keep).astype(BF16).astype(F32))
+    store_shifts(taps_ref, (pre * sigmoid(pre) * keep).astype(BF16).astype(F32))
 
 
 def attention_kernel(
-    core_ref, recv_ref, other_ref, taps_two, params, out_weight,
-    own_ref, swap_ref, weights, outputs_ref, attended_ref, grad_ref, sums_ref,
+    core_ref, recv_ref, other_ref, taps_two, params, first_weights,
+    own_ref, swap_ref, weights, outputs_ref, attended_ref, grad_ref, sums_ref, normed_ref,
 ):
     first_core = core_ref[0] == 0
-    load_weights(recv_ref, other_ref, FIRST_ROWS, SECOND_BLOCKS, first_core, weights)
+    load_weights(recv_ref, other_ref, IN_CUT_ROWS, WBLOCKS - IN_CUT, first_core, weights)
+    cotangent = load_image(recv_ref, AT_COTANGENT)
+    cot_low = cotangent.astype(BF16)
+    attended_grad = dot_tn(first_weights[OUT_BLOCK], cot_low).astype(BF16)
     source = load_image(recv_ref, AT_SOURCE)
     residual = source + convolve(weights, taps_two) + column(params, CONV_BIAS + 1)
     hat, inverse = norm_hat(residual)
     normed = (hat * column(params, GAINS + 2) + column(params, BIASES + 2)).astype(BF16)
-    queries = (dot_nn(weights[9], normed) + column(params, QV_BIAS)).astype(BF16)
-    keys = dot_nn(weights[10], normed).astype(BF16)
-    vals = (dot_nn(weights[11], normed) + column(params, QV_BIAS + 1)).astype(BF16)
     scale = C ** (-0.5)
+    queries = (dot_nn(first_weights[QUERY_BLOCK], normed) + column(params, QV_BIAS)).astype(BF16)
+    keys = dot_nn(first_weights[KEY_BLOCK], normed).astype(BF16)
+    vals = (dot_nn(weights[VALUE_BLOCK - IN_CUT], normed) + column(params, QV_BIAS + 1)).astype(BF16)
     scores = dot_tn(queries, keys) * scale
+    dprobs = dot_tn(attended_grad, vals)
     exps = jnp.exp(scores - jnp.max(scores, axis=1, keepdims=True))
     probs = exps / row_sum(exps)
     probs_low = probs.astype(BF16)
-    attended = dot_nt(vals, probs_low).astype(BF16)
-    attended_ref[...] = attended
-    outputs = residual + dot_nn(out_weight[FIRST_BLOCKS - 1], attended) + column(params, OUT_BIAS)
-    outputs_ref[...] = image_rows(outputs)
-
-    cotangent = load_image(recv_ref, AT_COTANGENT)
-    cot_low = cotangent.astype(BF16)
-    attended_grad = dot_tn(out_weight[FIRST_BLOCKS - 1], cot_low).astype(BF16)
-    dprobs = dot_tn(attended_grad, vals)
     dscores = (probs * (dprobs - row_sum(probs * dprobs))).astype(BF16)
     query_grad = (dot_nt(keys, dscores) * scale).astype(BF16)
     key_grad = (dot_nn(queries, dscores) * scale).astype(BF16)
     value_grad = dot_nn(attended_grad, probs_low).astype(BF16)
-    normed_grad = None
-    for k, gradient in enumerate((query_grad, key_grad, value_grad)):
-        product = dot_tn(weights[9 + k], gradient)
-        normed_grad = product if normed_grad is None else normed_grad + product
+    matrices = [first_weights[QUERY_BLOCK], first_weights[KEY_BLOCK], weights[VALUE_BLOCK - IN_CUT]]
+    normed_grad = dot_tn(
+        jnp.concatenate(matrices, axis=0),
+        jnp.concatenate([query_grad, key_grad, value_grad], axis=0),
+    )
+    normed_ref[0] = normed[:HALF]
+    normed_ref[1] = normed[HALF:]
+    operand = own_first(normed_ref, core_ref[0])
+    dqkv = [dot_nt(gradient, operand) for gradient in (query_grad, key_grad, value_grad)]
+    attended = dot_nt(vals, probs_low).astype(BF16)
+    attended_ref[0] = attended[:HALF]
+    attended_ref[1] = attended[HALF:]
+    outputs = residual + dot_nn(first_weights[OUT_BLOCK], attended) + column(params, OUT_BIAS)
+    outputs_ref[...] = image_rows(outputs)
     branch, gain_grad, bias_grad = norm_back(hat, inverse, normed_grad, column(params, GAINS + 2))
     residual_grad = cotangent + branch
     grad_ref[...] = residual_grad
     low = residual_grad.astype(BF16)
-    grads = [dot_nt(low, taps_two[tap]) for tap in range(9)]
-    grads += [dot_nt(gradient, normed) for gradient in (query_grad, key_grad, value_grad)]
-    for pair in range(SECOND_BLOCKS // 2):
-        store_weight_grads(own_ref, swap_ref, pair, first_core, grads[2 * pair : 2 * pair + 2])
+    store_weight_grads(own_ref, swap_ref, 0, dqkv[:2] + conv_weight_grads(low, taps_two, core_ref[0]) + dqkv[2:])
     listed = {
         D_GAINS + 2: gain_grad,
         D_BIASES + 2: bias_grad,
@@ -260,21 +291,20 @@
     core_ref, recv_ref, weights, taps_one, hat_ref, stats, params, attended, grad_ref, sums,
     own_ref, swap_ref, low_ref, sums_ref,
 ):
-    second_grad = convolve_back(weights, grad_ref[...].astype(BF16))
     hat = hat_ref[...]
     gain = column(params, GAINS + 1)
     pre = hat * gain + column(params, BIASES + 1)
     keep = load_image(recv_ref, AT_KEEP) * (1.0 / 0.9)
-    pre_grad = second_grad * keep * slope(pre)
+    factor = keep * slope(pre)
+    cot_low = load_image(recv_ref, AT_COTANGENT).astype(BF16)
+    out_grad = dot_nt(cot_low, own_first(attended, core_ref[0]))
+    second_grad = convolve_back(weights, grad_ref[...].astype(BF16))
+    pre_grad = second_grad * factor
     middle_grad, gain_grad, bias_grad = norm_back(hat, column(stats, 0), pre_grad, gain)
     low = middle_grad.astype(BF16)
     low_ref[...] = low
-    grads = [dot_nt(low, taps_one[tap]) for tap in range(9)]
-    grads += [dot_nt(load_image(recv_ref, AT_COTANGENT).astype(BF16), attended[...])]
-    for pair in range(FIRST_BLOCKS // 2):
-        store_weight_grads(
-            own_ref, swap_ref, pair, core_ref[0] == 0, grads[2 * pair : 2 * pair + 2]
-        )
+    grads = conv_weight_grads(low, taps_one, core_ref[0]) + [out_grad]
+    store_weight_grads(own_ref, swap_ref, 0, grads)
     listed = {D_GAINS + 1: gain_grad, D_BIASES + 1: bias_grad, D_CONV_BIAS: row_sum(middle_grad)}
     zero = jnp.zeros((C, 1), F32)
     sums_ref[...] = sums[...] + columns_of([listed.get(k, zero) for k in range(PART)])
@@ -283,15 +313,16 @@
 def first_back_kernel(
     weights, hat_ref, stats, params, low_ref, grad_ref, sums, outputs, own, swapped, send_ref
 ):
-    first_grad = convolve_back(weights, low_ref[...])
     hat = hat_ref[...]
     gain = column(params, GAINS)
     pre = hat * gain + column(params, BIASES)
-    branch, gain_grad, bias_grad = norm_back(hat, column(stats, 0), first_grad * slope(pre), gain)
-    for pair in range(SECOND_BLOCKS // 2):
+    factor = slope(pre)
+    first_grad = convolve_back(weights, low_ref[...])
+    branch, gain_grad, bias_grad = norm_back(hat, column(stats, 0), first_grad * factor, gain)
+    for pair in range((WBLOCKS - OUT_CUT) // 2):
         rows = slice(16 * pair, 16 * pair + 16)
         both = own[:, rows, :].astype(F32) + swapped[:, rows, :].astype(F32)
-        to = FIRST_ROWS + 16 * pair
+        to = OUT_CUT_ROWS + 16 * pair
         send_ref[:, to : to + 16, :] = both.astype(BF16)
     send_ref[:, WROWS : WROWS + 16, :] = outputs[...]
     send_ref[:, WROWS + 16 : WROWS + 32, :] = image_rows(grad_ref[...] + branch)
@@ -309,8 +340,9 @@
 AT_SOURCE, AT_KEEP, AT_COTANGENT, AT_PARAMS = WROWS, WROWS + 16, WROWS + 32, WROWS + 48
 IN_ROWS = WROWS + 56
 OUT_ROWS = WROWS + 40
-FIRST_BLOCKS, SECOND_BLOCKS = 10, 12
-FIRST_ROWS, SECOND_ROWS = FIRST_BLOCKS * ROWS, SECOND_BLOCKS * ROWS
+OUT_BLOCK, QUERY_BLOCK, KEY_BLOCK, SECOND_CONV, VALUE_BLOCK = 9, 10, 11, 12, 21
+IN_CUT, OUT_CUT = 12, 10
+IN_CUT_ROWS, OUT_CUT_ROWS = IN_CUT * ROWS, OUT_CUT * ROWS
 
 
 def local_call(kernel, core, *operands, out):
@@ -332,26 +364,27 @@
 
 
 def run_block(core, received, swap):
-    other_one = swap(received[:, :FIRST_ROWS])
-    other_two = swap(received[:, FIRST_ROWS:WROWS])
+    other_one = swap(received[:, :IN_CUT_ROWS])
+    other_two = swap(received[:, IN_CUT_ROWS:WROWS])
     image, table = ((C, POS), F32), ((C, HALF), F32)
-    taps, low = ((9, C, POS), BF16), ((C, POS), BF16)
+    taps, low = ((2, 3, HALF, POS), BF16), ((C, POS), BF16)
+    halves = ((2, HALF, POS), BF16)
 
     taps_one, hat_one, params, stats_one = local_call(
         first_kernel, None, received, out=(taps, image, table, table)
     )
     weights_one, taps_two, hat_two, stats_two = local_call(
         middle_kernel, core, received, other_one, taps_one, params,
-        out=(((FIRST_BLOCKS, C, C), BF16), taps, image, table),
-    )
-    second = ((SHARDS, SECOND_ROWS, HALF), BF16)
+        out=(((IN_CUT, C, C), BF16), taps, image, table),
+    )
+    second = ((SHARDS, WROWS - OUT_CUT_ROWS, HALF), BF16)
     rows = ((SHARDS, 16, HALF), BF16)
-    own_two, swap_two, weights_two, outputs, attended, residual_grad, sums = local_call(
+    own_two, swap_two, weights_two, outputs, attended, residual_grad, sums, _ = local_call(
         attention_kernel, core, received, other_two, taps_two, params, weights_one,
-        out=(second, second, ((SECOND_BLOCKS, C, C), BF16), rows, low, image, table),
+        out=(second, second, ((WBLOCKS - IN_CUT, C, C), BF16), rows, halves, image, table, halves),
     )
     swapped_two = swap(swap_two)
-    first = ((SHARDS, FIRST_ROWS, HALF), BF16)
+    first = ((SHARDS, OUT_CUT_ROWS, HALF), BF16)
     own_one, swap_one, middle_low, sums = local_call(
         middle_back_kernel, core, received, weights_two, taps_one, hat_two, stats_two, params,
         attended, residual_grad, sums, out=(first, first, low, table),
@@ -439,12 +472,12 @@
     copies = [pltpu.make_async_copy(scratch[k], results[k], sems.at[k]) for k in range(10)]
     for conv in range(2):
         for tap in range(9):
-            conv_w[conv, tap, :, :] = weight_grad(FIRST_BLOCKS * conv + tap)
+            conv_w[conv, tap, :, :] = weight_grad(SECOND_CONV * conv + tap)
     copies[2].start()
     for k in range(3):
-        qkv_w[k, :, :] = weight_grad(FIRST_BLOCKS + 9 + k)
+        qkv_w[k, :, :] = weight_grad((QUERY_BLOCK, KEY_BLOCK, VALUE_BLOCK)[k])
     copies[6].start()
-    out_w[...] = weight_grad(FIRST_BLOCKS - 1)
+    out_w[...] = weight_grad(OUT_BLOCK)
     copies[8].start()
     shared = mine_ref[WROWS:, :] + theirs_ref[WROWS:, :]
     small = shared[:ROWS, :] + pltpu.roll(shared[:ROWS, :], HALF - PART, 1)
@@ -553,8 +586,10 @@
         [
             half(conv_ref[0].reshape(9 * ROWS, C)),
             half(out_ref[...]),
+            half(qkv_ref[0]),
+            half(qkv_ref[1]),
             half(conv_ref[1].reshape(9 * ROWS, C)),
-            half(qkv_ref[...].reshape(3 * ROWS, C)),
+            half(qkv_ref[2]),
         ],
         axis=0,
     ).astype(BF16)

time: 91.9 us -> 89.9 us (0.978)
  Pallas kernels: 12.3 us -> 11.1 us
    pallas_call x5, Pallas kernels: 8.66 us -> 7.49 us  [local_call(): pl.pallas_call(kernel, out_shape=shapes, in_specs=in_specs, out_specs=tup...]
  transfers between devices with their start and end apart: 6 -> 6, of which waited for: 4 -> 5; matrix products, arithmetic and copies ran while one was open for 0% -> 0% of each run, Pallas kernels for 6% -> 6%
where the time goes in v4:
time: 89.9 us; the launch traced here: 89.7 us
  blocking collectives  66.1 us (74%)
  Pallas kernels  11.1 us (12%)
  starting transfers between devices  7 us (8%)
  waiting for transfers between devices  4.43 us (5%)
    all_to_all x1, blocking collectives, on_device(): lax.all_to_all(sent, 'ch', split_axis=0, concat_axis=0, tiled=True)  37 us
    all_to_all x1, blocking collectives, on_device(): back = lax.all_to_all(send, 'ch', split_axis=0, concat_axis=0, tiled=True)  29.1 us
    pallas_call x5, Pallas kernels, local_call(): pl.pallas_call(kernel, out_shape=shapes, in_specs=in_specs, out_specs=tup...  7.49 us
    ppermute x4, starting transfers between devices, on_device(): lax.ppermute(values, 'img', core_pairs)  3.26 us
    ppermute x1, starting transfers between devices, on_device(): theirs = lax.ppermute(sums, 'img', core_pairs)  2.92 us
    ppermute x4, waiting for transfers between devices, on_device(): lax.ppermute(values, 'img', core_pairs)  1.97 us
  transfers between devices with their start and end apart: 6, of which 5 were waited for; matrix products, arithmetic and copies ran while one was open for 0% of the time, Pallas kernels for 6%

profile of v4, /device:TPU:1, one launch (start us, length us, event | category | flops | bytes accessed | tf_op | source)
XLA Modules:
  0.0 89.7 jit_solution(10245048999417924120)
XLA Ops:
  0.7 1.7 %shard_map.229 = (bf16[32,232,128]{2,1,0:T(8,128)(2,1)S(1)}, f32[32,512]{1,0:T(8,128)S(1)}) custom-call(s32[1]{0:T(128)} %bitcast.core_ref, s32[32]{0:T(128)} %refs_0_.1, f32[3,8]{1,0:T(4,128)} %refs_1_.1, f32[3,8]{1,0:T(4,128)} %refs_2_.1, f32[2,8]{1,0:T(2,128)} %refs_3_.1, f32[2,8]{1,0:T(2,128)} %refs_4_.1, f32[1,8]{1,0:T(1,128)} %bitcast.8, ...), custom_call_target="tpu_custom_call" | custom-call | tf_op jit(solution)/shard_map/pallas_call | solution.py:614
  2.4 37.0 %all_to_all.10.recv_ref = bf16[32,232,128]{2,1,0:T(8,128)(2,1)S(1)} all-to-all(bf16[32,232,128]{2,1,0:T(8,128)(2,1)S(1)} %get-tuple-element.48), channel_id=1, replica_groups=mesh['ch'=32,'img'=4] {'ch'}, dimensions={0} | all-to-all | bytes 3801088 | tf_op jit(solution)/shard_map/all_to_all | solution.py:666
  39.4 0.1 slice.8
  39.5 2.6 %collective-permute-start = (bf16[32,96,128]{2,1,0:T(8,128)(2,1)S(1)}, bf16[32,96,128]{2,1,0:T(8,128)(2,1)S(1)}, u32[]{:S(2)}, u32[]{:S(2)}) collective-permute-start(bf16[32,96,128]{2,1,0:T(8,128)(2,1)S(1)} %slice.8), channel_id=1, source_target_pairs={{0,1},{1,0},{2,3},{3,2},{4,5},{5,4},{6,7},{7,6},{8,9},{9,8},{10,11... | collective-permute-start | bytes 2359304 | tf_op jit(solution)/shard_map/ppermute | solution.py:668
  42.1 0.1 collective-permute-start.1
  42.2 0.5 shard_map.230
  42.7 1.2 %collective-permute-done.other_ref = bf16[32,96,128]{2,1,0:T(8,128)(2,1)S(1)} collective-permute-done((bf16[32,96,128]{2,1,0:T(8,128)(2,1)S(1)}, bf16[32,96,128]{2,1,0:T(8,128)(2,1)S(1)}, u32[]{:S(2)}, u32[]{:S(2)}) %collective-permute-start) | collective-permute-done | bytes 786464 | tf_op jit(solution)/shard_map/ppermute | solution.py:668
  43.9 1.1 %shard_map.231 = (bf16[12,256,256]{2,1,0:T(8,128)(2,1)S(1)}, bf16[2,3,128,256]{3,2,1,0:T(8,128)(2,1)S(1)}, f32[256,256]{1,0:T(8,128)S(1)}, f32[256,128]{1,0:T(8,128)S(1)}) custom-call(s32[1]{0:T(128)} %bitcast.core_ref, bf16[32,232,128]{2,1,0:T(8,128)(2,1)S(1)} %all_to_all.10.recv_ref, bf16[32,96,128]{2,1,0:T(8,128)(2,1)S(1)} %collective-permute-done.other_ref, ...), custom_call_target="tpu_custom_call" | custom-call | tf_op jit(solution)/shard_map/pallas_call | solution.py:354
  45.0 0.0 collective-permute-done.1.other_ref
  45.0 3.1 %shard_map.232 = (bf16[32,96,128]{2,1,0:T(8,128)(2,1)S(1)}, bf16[32,96,128]{2,1,0:T(8,128)(2,1)S(1)}, bf16[10,256,256]{2,1,0:T(8,128)(2,1)S(1)}, bf16[32,16,128]...) custom-call(s32[1]{0:T(128)} %bitcast.core_ref, ...), custom_call_target="tpu_custom_call" | custom-call | tf_op jit(solution)/shard_map/pallas_call | solution.py:354
  48.1 0.4 collective-permute-start.2
  48.5 1.6 %shard_map.233 = (bf16[32,80,128]{2,1,0:T(8,128)(2,1)S(1)}, bf16[32,80,128]{2,1,0:T(8,128)(2,1)S(1)}, bf16[256,256]{1,0:T(8,128)(2,1)S(1)}, f32[256,128]{1,0:T(8,128)S(1)}) custom-call(s32[1]{0:T(128)} %bitcast.core_ref, bf16[32,232,128]{2,1,0:T(8,128)(2,1)S(1)} %all_to_all.10.recv_ref, bf16[10,256,256]{2,1,0:T(8,128)(2,1)S(1)} %get-tuple-element.55.weights, ...), custom_call_target="tpu_custom_call" | custom-call | tf_op jit(solution)/shard_map/pallas_call | solution.py:354
  50.1 0.2 collective-permute-start.3
  50.3 0.1 collective-permute-done.2.swapped
  50.4 1.2 %shard_map.234 = bf16[32,216,128]{2,1,0:T(8,128)(2,1)S(1)} custom-call(bf16[12,256,256]{2,1,0:T(8,128)(2,1)S(1)} %get-tuple-element.51.first_weights.weights, f32[256,256]{1,0:T(8,128)S(1)} %get-tuple-element.52.hat_ref, f32[256,128]{1,0:T(8,128)S(1)} %get-tuple-element.53.stats, f32[256,128]{1,0:T(8,128)S(1)} %get-tuple-element.50.params, ...), custom_call_target="tpu_custom_call" | custom-call | tf_op jit(solution)/shard_map/pallas_call | solution.py:354
  51.6 0.6 collective-permute-done.3
  52.3 0.2 fusion
  52.5 29.1 %all_to_all.11.back_ref = bf16[32,216,128]{2,1,0:T(8,128)(2,1)S(1)} all-to-all(bf16[32,216,128]{2,1,0:T(8,128)(2,1)S(1)} %fusion), channel_id=1, replica_groups=mesh['ch'=32,'img'=4] {'ch'}, dimensions={0} | all-to-all | bytes 3538944 | tf_op jit(solution)/shard_map/all_to_all | solution.py:670
  81.6 0.3 shard_map.235
  81.9 0.8 collective-permute-start.4
  82.7 0.8 shard_map.236
  83.5 1.5 %collective-permute-done.4 = bf16[224,128]{1,0:T(8,128)(2,1)S(1)} collective-permute-done((bf16[224,128]{1,0:T(8,128)(2,1)S(1)}, bf16[224,128]{1,0:T(8,128)(2,1)S(1)}, u32[]{:S(2)}, u32[]{:S(2)}) %collective-permute-start.4) | collective-permute-done | bytes 57376 | tf_op jit(solution)/shard_map/ppermute | solution.py:673
  85.0 2.9 %collective-permute-start.5 = (f32[224,128]{1,0:T(8,128)S(1)}, f32[224,128]{1,0:T(8,128)S(1)}, u32[]{:S(2)}, u32[]{:S(2)}) collective-permute-start(f32[224,128]{1,0:T(8,128)S(1)} %convert_add_fusion.mine_ref), channel_id=1, source_target_pairs={{0,1},{1,0},{2,3},{3,2},{4,5},{5,4},{6,7},{7,6},{8,9},{9,8},{10,11... | collective-permute-start | bytes 344072 | tf_op jit(solution)/shard_map/ppermute | solution.py:677
  87.9 1.0 %collective-permute-done.5.theirs_ref = f32[224,128]{1,0:T(8,128)S(1)} collective-permute-done((f32[224,128]{1,0:T(8,128)S(1)}, f32[224,128]{1,0:T(8,128)S(1)}, u32[]{:S(2)}, u32[]{:S(2)}) %collective-permute-start.5) | collective-permute-done | bytes 114720 | tf_op jit(solution)/shard_map/ppermute | solution.py:677
  88.9 0.8 shard_map.237
  (2 shorter events, 0.1 us)
Async XLA Ops:
  39.5 4.5 %collective-permute-start = (bf16[32,96,128]{2,1,0:T(8,128)(2,1)S(1)}, bf16[32,96,128]{2,1,0:T(8,128)(2,1)S(1)}, u32[]{:S(2)}, u32[]{:S(2)}) collective-permute-start(bf16[32,96,128]{2,1,0:T(8,128)(2,1)S(1)} %slice.8), channel_id=1, source_target_pairs={{0,1},{1,0},{2,3},{3,2},{4,5},{5,4},{6,7},{7,6},{8,9},{9,8},{10,11... | collective-permute-start | bytes 2359304 | tf_op jit(solution)/shard_map/ppermute | solution.py:668
  42.1 2.9 %collective-permute-start.1 = (bf16[32,80,128]{2,1,0:T(8,128)(2,1)S(1)}, bf16[32,80,128]{2,1,0:T(8,128)(2,1)S(1)}, u32[]{:S(2)}, u32[]{:S(2)}) collective-permute-start(bf16[32,80,128]{2,1,0:T(8,128)(2,1)S(1)} %slice.9), channel_id=1, source_target_pairs={{0,1},{1,0},{2,3},{3,2},{4,5},{5,4},{6,7},{7,6},{8,9},{9,8},{10,11... | collective-permute-start | bytes 1966088 | tf_op jit(solution)/shard_map/ppermute | solution.py:668
  48.1 2.3 %collective-permute-start.2 = (bf16[32,96,128]{2,1,0:T(8,128)(2,1)S(1)}, bf16[32,96,128]{2,1,0:T(8,128)(2,1)S(1)}, u32[]{:S(2)}, u32[]{:S(2)}) collective-permute-start(bf16[32,96,128]{2,1,0:T(8,128)(2,1)S(1)} %get-tuple-element.65), channel_id=1, source_target_pairs={{0,1},{1,0},{2,3},{3,2},{4,5},{5,4},{6,7},{7,6},{8,9},{9,8},{10,11... | collective-permute-start | bytes 2359304 | tf_op jit(solution)/shard_map/ppermute | solution.py:668
  50.1 2.2 %collective-permute-start.3 = (bf16[32,80,128]{2,1,0:T(8,128)(2,1)S(1)}, bf16[32,80,128]{2,1,0:T(8,128)(2,1)S(1)}, u32[]{:S(2)}, u32[]{:S(2)}) collective-permute-start(bf16[32,80,128]{2,1,0:T(8,128)(2,1)S(1)} %get-tuple-element.67), channel_id=1, source_target_pairs={{0,1},{1,0},{2,3},{3,2},{4,5},{5,4},{6,7},{7,6},{8,9},{9,8},{10,11... | collective-permute-start | bytes 1966088 | tf_op jit(solution)/shard_map/ppermute | solution.py:668
  81.9 3.1 %collective-permute-start.4 = (bf16[224,128]{1,0:T(8,128)(2,1)S(1)}, bf16[224,128]{1,0:T(8,128)(2,1)S(1)}, u32[]{:S(2)}, u32[]{:S(2)}) collective-permute-start(bf16[224,128]{1,0:T(8,128)(2,1)S(1)} %shard_map.235), channel_id=1, source_target_pairs={{0,2},{1,3},{2,0},{3,1},{4,6},{5,7},{6,4},{7,5},{8,10},{9,11},{10,... | collective-permute-start | bytes 172040 | tf_op jit(solution)/shard_map/ppermute | solution.py:673
  85.0 3.9 %collective-permute-start.5 = (f32[224,128]{1,0:T(8,128)S(1)}, f32[224,128]{1,0:T(8,128)S(1)}, u32[]{:S(2)}, u32[]{:S(2)}) collective-permute-start(f32[224,128]{1,0:T(8,128)S(1)} %convert_add_fusion.mine_ref), channel_id=1, source_target_pairs={{0,1},{1,0},{2,3},{3,2},{4,5},{5,4},{6,7},{7,6},{8,9},{9,8},{10,11... | collective-permute-start | bytes 344072 | tf_op jit(solution)/shard_map/ppermute | solution.py:677

commit v5 on v4

--- a/solution.py
+++ b/solution.py
@@ -68,7 +68,7 @@
 
 
 def sigmoid(values):
-    return 1.0 / (1.0 + jnp.exp(-values))
+    return 0.5 + 0.5 * jnp.tanh(0.5 * values)
 
 
 def rolled(values, steps, axis):
@@ -83,9 +83,13 @@
 
 
 def row_shifted(values, step):
-    cell = lax.broadcasted_iota(jnp.int32, (1, POS), 1) + step * SIDE
-    valid = (cell >= 0) & (cell < POS)
-    return rolled(values, -step * SIDE, 1) * valid.astype(F32)
+    moved = rolled(values, -step * SIDE, 1)
+    lane = lax.broadcasted_iota(jnp.int32, (1, HALF), 1)
+    if step > 0:
+        edge = jnp.where(lane < HALF - SIDE, moved[:, HALF:], 0.0)
+        return jnp.concatenate([moved[:, :HALF], edge], axis=1)
+    edge = jnp.where(lane >= SIDE, moved[:, :HALF], 0.0)
+    return jnp.concatenate([edge, moved[:, HALF:]], axis=1)
 
 
 def load_weights(mine_ref, theirs_ref, first_row, blocks, first_core, weights):
@@ -156,19 +160,24 @@
     return jnp.concatenate(halves, axis=0)
 
 
-def store_weight_grads(own_ref, swap_ref, first_block, products):
+def lane_blocks(product):
+    count = product.shape[1] // HALF
+    cut = [product[:, HALF * k : HALF * k + HALF] for k in range(count)]
+    return [values.reshape(SHARDS, ROWS, HALF) for values in cut]
+
+
+def store_weight_grads(own_ref, swap_ref, products):
+    blocks = [lane_blocks(product) for product in products]
     for target, at in ((own_ref, 0), (swap_ref, 1)):
-        blocks = []
-        for product in products:
-            lanes = product.shape[1] // 2
-            for k in range(lanes // HALF):
-                start = at * lanes + k * HALF
-                blocks.append(product[:, start : start + HALF].reshape(SHARDS, ROWS, HALF))
-        for pair in range(len(blocks) // 2):
-            rows = slice((first_block + 2 * pair) * ROWS, (first_block + 2 * pair + 2) * ROWS)
-            target[:, rows, :] = jnp.concatenate(
-                blocks[2 * pair : 2 * pair + 2], axis=1
-            ).astype(BF16)
+        listed = []
+        for cut in blocks:
+            listed += cut[: len(cut) // 2] if at == 0 else cut[len(cut) // 2 :]
+        if len(listed) % 2:
+            listed.append(jnp.zeros_like(listed[0]))
+        for pair in range(len(listed) // 2):
+            both = jnp.concatenate(listed[2 * pair : 2 * pair + 2], axis=1)
+            rows = slice(PAIR_ROWS * pair, PAIR_ROWS * pair + PAIR_ROWS)
+            target[rows, :] = both.reshape(PAIR_ROWS, HALF).astype(BF16)
 
 
 def conv_weight_grads(low, shifts, core):
@@ -181,10 +190,9 @@
     return grads
 
 
-def columns_of(listed):
+def columns_of(listed, table):
     lane = lax.broadcasted_iota(jnp.int32, (C, HALF), 1)
-    table = jnp.zeros((C, HALF), F32)
-    for k, column in enumerate(listed):
+    for k, column in listed.items():
         table = jnp.where(lane == k, column, table)
     return table
 
@@ -232,7 +240,7 @@
 
 def attention_kernel(
     core_ref, recv_ref, other_ref, taps_two, params, first_weights,
-    own_ref, swap_ref, weights, outputs_ref, attended_ref, grad_ref, sums_ref, normed_ref,
+    weights, outputs_ref, grad_ref, sums_ref, normed_ref, halves_ref, grads_ref,
 ):
     first_core = core_ref[0] == 0
     load_weights(recv_ref, other_ref, IN_CUT_ROWS, WBLOCKS - IN_CUT, first_core, weights)
@@ -263,18 +271,16 @@
     )
     normed_ref[0] = normed[:HALF]
     normed_ref[1] = normed[HALF:]
-    operand = own_first(normed_ref, core_ref[0])
-    dqkv = [dot_nt(gradient, operand) for gradient in (query_grad, key_grad, value_grad)]
+    for k, gradient in enumerate((query_grad, key_grad, value_grad)):
+        grads_ref[k, :, :] = gradient
     attended = dot_nt(vals, probs_low).astype(BF16)
-    attended_ref[0] = attended[:HALF]
-    attended_ref[1] = attended[HALF:]
+    halves_ref[0] = attended[:HALF]
+    halves_ref[1] = attended[HALF:]
     outputs = residual + dot_nn(first_weights[OUT_BLOCK], attended) + column(params, OUT_BIAS)
     outputs_ref[...] = image_rows(outputs)
     branch, gain_grad, bias_grad = norm_back(hat, inverse, normed_grad, column(params, GAINS + 2))
     residual_grad = cotangent + branch
     grad_ref[...] = residual_grad
-    low = residual_grad.astype(BF16)
-    store_weight_grads(own_ref, swap_ref, 0, dqkv[:2] + conv_weight_grads(low, taps_two, core_ref[0]) + dqkv[2:])
     listed = {
         D_GAINS + 2: gain_grad,
         D_BIASES + 2: bias_grad,
@@ -283,58 +289,84 @@
         D_QV_BIAS + 1: row_sum(value_grad.astype(F32)),
         D_OUT_BIAS: row_sum(cotangent),
     }
-    zero = jnp.zeros((C, 1), F32)
-    sums_ref[...] = columns_of([listed.get(k, zero) for k in range(PART)])
+    sums_ref[...] = columns_of(listed, jnp.zeros((C, HALF), F32))
+
+
+def early_grads_kernel(
+    core_ref, recv_ref, taps_one, taps_two, grad_ref, normed_ref, halves_ref, grads_ref,
+    own_ref, swap_ref,
+):
+    core = core_ref[0]
+    other_half = taps_one[1 - core].reshape(3 * HALF, POS)
+    swap_ref[EARLY_ROWS : EARLY_ROWS + 3 * HALF, :] = other_half[:, :HALF]
+    swap_ref[EARLY_ROWS + 3 * HALF :, :] = other_half[:, HALF:]
+    operand = own_first(normed_ref, core)
+    dqkv = [dot_nt(grads_ref[k], operand) for k in range(3)]
+    cot_low = load_image(recv_ref, AT_COTANGENT).astype(BF16)
+    out_grad = dot_nt(cot_low, own_first(halves_ref, core))
+    low = grad_ref[...].astype(BF16)
+    grads = dqkv[:2] + conv_weight_grads(low, taps_two, core) + [dqkv[2], out_grad]
+    store_weight_grads(own_ref, swap_ref, grads)
 
 
 def middle_back_kernel(
-    core_ref, recv_ref, weights, taps_one, hat_ref, stats, params, attended, grad_ref, sums,
-    own_ref, swap_ref, low_ref, sums_ref,
+    recv_ref, weights, hat_ref, stats, params, grad_ref, sums, low_ref, sums_ref
 ):
     hat = hat_ref[...]
     gain = column(params, GAINS + 1)
     pre = hat * gain + column(params, BIASES + 1)
     keep = load_image(recv_ref, AT_KEEP) * (1.0 / 0.9)
     factor = keep * slope(pre)
-    cot_low = load_image(recv_ref, AT_COTANGENT).astype(BF16)
-    out_grad = dot_nt(cot_low, own_first(attended, core_ref[0]))
     second_grad = convolve_back(weights, grad_ref[...].astype(BF16))
     pre_grad = second_grad * factor
     middle_grad, gain_grad, bias_grad = norm_back(hat, column(stats, 0), pre_grad, gain)
-    low = middle_grad.astype(BF16)
-    low_ref[...] = low
-    grads = conv_weight_grads(low, taps_one, core_ref[0]) + [out_grad]
-    store_weight_grads(own_ref, swap_ref, 0, grads)
+    low_ref[...] = middle_grad.astype(BF16)
     listed = {D_GAINS + 1: gain_grad, D_BIASES + 1: bias_grad, D_CONV_BIAS: row_sum(middle_grad)}
-    zero = jnp.zeros((C, 1), F32)
-    sums_ref[...] = sums[...] + columns_of([listed.get(k, zero) for k in range(PART)])
-
-
-def first_back_kernel(
-    weights, hat_ref, stats, params, low_ref, grad_ref, sums, outputs, own, swapped, send_ref
-):
+    sums_ref[...] = columns_of(listed, sums[...])
+
+
+def first_back_kernel(weights, hat_ref, stats, params, low_ref, grad_ref, sums, tail_ref):
     hat = hat_ref[...]
     gain = column(params, GAINS)
     pre = hat * gain + column(params, BIASES)
     factor = slope(pre)
     first_grad = convolve_back(weights, low_ref[...])
     branch, gain_grad, bias_grad = norm_back(hat, column(stats, 0), first_grad * factor, gain)
-    for pair in range((WBLOCKS - OUT_CUT) // 2):
-        rows = slice(16 * pair, 16 * pair + 16)
-        both = own[:, rows, :].astype(F32) + swapped[:, rows, :].astype(F32)
-        to = OUT_CUT_ROWS + 16 * pair
-        send_ref[:, to : to + 16, :] = both.astype(BF16)
-    send_ref[:, WROWS : WROWS + 16, :] = outputs[...]
-    send_ref[:, WROWS + 16 : WROWS + 32, :] = image_rows(grad_ref[...] + branch)
-
-    zero = jnp.zeros((C, 1), F32)
-    listed = {D_GAINS: gain_grad, D_BIASES: bias_grad}
-    table = sums[...] + columns_of([listed.get(k, zero) for k in range(PART)])
+    tail_ref[:, :16, :] = image_rows(grad_ref[...] + branch)
+
+    table = columns_of({D_GAINS: gain_grad, D_BIASES: bias_grad}, sums[...])
     high = table.astype(BF16).astype(F32)
     low = pltpu.roll(table - high, PART, 1)
     lane = lax.broadcasted_iota(jnp.int32, (C, HALF), 1)
-    table = jnp.where(lane < PART, high, low)
-    send_ref[:, WROWS + 32 : WROWS + 40, :] = table.reshape(SHARDS, ROWS, HALF).astype(BF16)
+    table = jnp.where(lane < PART, high, low).reshape(SHARDS, ROWS, HALF)
+    tail_ref[:, 16:, :] = jnp.concatenate([table, jnp.zeros_like(table)], axis=1).astype(BF16)
+
+
+def gather_kernel(core_ref, shifts, low_ref, their_low, own, swapped, outputs, tail, send_ref):
+    mine = shifts[core_ref[0]].reshape(3 * HALF, POS)
+    left = swapped[EARLY_ROWS : EARLY_ROWS + 3 * HALF, :]
+    right = swapped[EARLY_ROWS + 3 * HALF :, :]
+    operand = jnp.concatenate([mine, left, right], axis=1)
+    wide = [low_ref[...].astype(F32), their_low[...].astype(F32)]
+    blocks = []
+    for row in (-1, 0, 1):
+        moved = [row_shifted(values, -row) if row else values for values in wide]
+        blocks += lane_blocks(dot_nt(jnp.concatenate(moved, axis=1).astype(BF16), operand))
+
+    def early(pair):
+        rows = slice(PAIR_ROWS * pair, PAIR_ROWS * pair + PAIR_ROWS)
+        both = own[rows, :].astype(F32) + swapped[rows, :].astype(F32)
+        return both.reshape(SHARDS, 16, HALF)
+
+    blocks.append(early(EARLY_PAIRS - 1)[:, :ROWS, :])
+    for pair in range(len(blocks) // 2):
+        rows = jnp.concatenate(blocks[2 * pair : 2 * pair + 2], axis=1)
+        send_ref[:, 16 * pair : 16 * pair + 16, :] = rows.astype(BF16)
+    for pair in range(EARLY_PAIRS - 1):
+        to = OUT_CUT_ROWS + 16 * pair
+        send_ref[:, to : to + 16, :] = early(pair).astype(BF16)
+    send_ref[:, WROWS : WROWS + 16, :] = outputs[...]
+    send_ref[:, WROWS + 16 : WROWS + 40, :] = tail[:, :24, :]
 
 
 AT_SOURCE, AT_KEEP, AT_COTANGENT, AT_PARAMS = WROWS, WROWS + 16, WROWS + 32, WROWS + 48
@@ -343,6 +375,8 @@
 OUT_BLOCK, QUERY_BLOCK, KEY_BLOCK, SECOND_CONV, VALUE_BLOCK = 9, 10, 11, 12, 21
 IN_CUT, OUT_CUT = 12, 10
 IN_CUT_ROWS, OUT_CUT_ROWS = IN_CUT * ROWS, OUT_CUT * ROWS
+EARLY_PAIRS, PAIR_ROWS = (WBLOCKS - OUT_CUT) // 2 + 1, 16 * SHARDS
+EARLY_ROWS = EARLY_PAIRS * PAIR_ROWS
 
 
 def local_call(kernel, core, *operands, out):
@@ -377,26 +411,31 @@
         middle_kernel, core, received, other_one, taps_one, params,
         out=(((IN_CUT, C, C), BF16), taps, image, table),
     )
-    second = ((SHARDS, WROWS - OUT_CUT_ROWS, HALF), BF16)
     rows = ((SHARDS, 16, HALF), BF16)
-    own_two, swap_two, weights_two, outputs, attended, residual_grad, sums, _ = local_call(
+    weights_two, outputs, residual_grad, sums, normed, attended, gradients = local_call(
         attention_kernel, core, received, other_two, taps_two, params, weights_one,
-        out=(second, second, ((WBLOCKS - IN_CUT, C, C), BF16), rows, halves, image, table, halves),
-    )
-    swapped_two = swap(swap_two)
-    first = ((SHARDS, OUT_CUT_ROWS, HALF), BF16)
-    own_one, swap_one, middle_low, sums = local_call(
-        middle_back_kernel, core, received, weights_two, taps_one, hat_two, stats_two, params,
-        attended, residual_grad, sums, out=(first, first, low, table),
-    )
-    swapped_one = swap(swap_one)
+        out=(((WBLOCKS - IN_CUT, C, C), BF16), rows, image, table, halves, halves, ((3, C, POS), BF16)),
+    )
+    own, swap_early = local_call(
+        early_grads_kernel, core, received, taps_one, taps_two, residual_grad, normed, attended,
+        gradients,
+        out=(((EARLY_ROWS, HALF), BF16), ((EARLY_ROWS + 6 * HALF, HALF), BF16)),
+    )
+    swapped = swap(swap_early)
+    low_one, sums = local_call(
+        middle_back_kernel, None, received, weights_two, hat_two, stats_two, params,
+        residual_grad, sums, out=(low, table),
+    )
+    their_low = swap(low_one)
+    (tail,) = local_call(
+        first_back_kernel, None, weights_one, hat_one, stats_one, params, low_one,
+        residual_grad, sums, out=(((SHARDS, 32, HALF), BF16),),
+    )
     (send,) = local_call(
-        first_back_kernel, None, weights_one, hat_one, stats_one, params, middle_low,
-        residual_grad, sums, outputs, own_two, swapped_two,
+        gather_kernel, core, taps_one, low_one, their_low, own, swapped, outputs, tail,
         out=(((SHARDS, OUT_ROWS, HALF), BF16),),
     )
-    both = (own_one.astype(F32) + swapped_one.astype(F32)).astype(BF16)
-    return lax.dynamic_update_slice(send, both, (0, 0, 0))
+    return send
 
 
 def collect_kernel(back_ref, swished_ref, sums_ref):

time: 89.9 us -> 89.6 us (level)
    pallas_call x5 -> x7, Pallas kernels: 7.49 us -> 7.29 us  [local_call(): pl.pallas_call(kernel, out_shape=shapes, in_specs=in_specs, out_specs=tup...]
  transfers between devices with their start and end apart: 6 -> 6, of which waited for: 5 -> 4; matrix products, arithmetic and copies ran while one was open for 0% -> 0% of each run, Pallas kernels for 6% -> 5%
where the time goes in v5:
time: 89.6 us; the launch traced here: 89.4 us
  blocking collectives  65.9 us (74%)
  Pallas kernels  10.9 us (12%)
  starting transfers between devices  7.47 us (8%)
  waiting for transfers between devices  4.3 us (5%)
    all_to_all x1, blocking collectives, on_device(): lax.all_to_all(sent, 'ch', split_axis=0, concat_axis=0, tiled=True)  37 us
    all_to_all x1, blocking collectives, on_device(): back = lax.all_to_all(send, 'ch', split_axis=0, concat_axis=0, tiled=True)  28.9 us
    pallas_call x7, Pallas kernels, local_call(): pl.pallas_call(kernel, out_shape=shapes, in_specs=in_specs, out_specs=tup...  7.29 us
    ppermute x1, starting transfers between devices, on_device(): theirs = lax.ppermute(sums, 'img', core_pairs)  3.34 us
    ppermute x4, starting transfers between devices, on_device(): lax.ppermute(values, 'img', core_pairs)  3.32 us
    ppermute x4, waiting for transfers between devices, on_device(): lax.ppermute(values, 'img', core_pairs)  1.83 us
  transfers between devices with their start and end apart: 6, of which 4 were waited for; matrix products, arithmetic and copies ran while one was open for 0% of the time, Pallas kernels for 5%

profile of v5, /device:TPU:1, one launch (start us, length us, event | category | flops | bytes accessed | tf_op | source)
XLA Modules:
  0.0 89.4 jit_solution(3884104257534977126)
XLA Ops:
  0.7 1.7 %shard_map.229 = (bf16[32,232,128]{2,1,0:T(8,128)(2,1)S(1)}, f32[32,512]{1,0:T(8,128)S(1)}) custom-call(s32[1]{0:T(128)} %bitcast.core_ref, s32[32]{0:T(128)} %refs_0_.1, f32[3,8]{1,0:T(4,128)} %refs_1_.1, f32[3,8]{1,0:T(4,128)} %refs_2_.1, f32[2,8]{1,0:T(2,128)} %refs_3_.1, f32[2,8]{1,0:T(2,128)} %refs_4_.1, f32[1,8]{1,0:T(1,128)} %bitcast.8, ...), custom_call_target="tpu_custom_call" | custom-call | tf_op jit(solution)/shard_map/pallas_call | solution.py:653
  2.4 37.0 %all_to_all.10.recv_ref = bf16[32,232,128]{2,1,0:T(8,128)(2,1)S(1)} all-to-all(bf16[32,232,128]{2,1,0:T(8,128)(2,1)S(1)} %get-tuple-element.48), channel_id=1, replica_groups=mesh['ch'=32,'img'=4] {'ch'}, dimensions={0} | all-to-all | bytes 3801088 | tf_op jit(solution)/shard_map/all_to_all | solution.py:705
  39.4 0.1 slice.9
  39.4 2.6 %collective-permute-start.1 = (bf16[32,96,128]{2,1,0:T(8,128)(2,1)S(1)}, bf16[32,96,128]{2,1,0:T(8,128)(2,1)S(1)}, u32[]{:S(2)}, u32[]{:S(2)}) collective-permute-start(bf16[32,96,128]{2,1,0:T(8,128)(2,1)S(1)} %slice.9), channel_id=1, source_target_pairs={{0,1},{1,0},{2,3},{3,2},{4,5},{5,4},{6,7},{7,6},{8,9},{9,8},{10,11... | collective-permute-start | bytes 2359304 | tf_op jit(solution)/shard_map/ppermute | solution.py:707
  42.1 0.1 collective-permute-start
  42.1 0.5 shard_map.230
  42.7 1.3 %collective-permute-done.1.other_ref = bf16[32,96,128]{2,1,0:T(8,128)(2,1)S(1)} collective-permute-done((bf16[32,96,128]{2,1,0:T(8,128)(2,1)S(1)}, bf16[32,96,128]{2,1,0:T(8,128)(2,1)S(1)}, u32[]{:S(2)}, u32[]{:S(2)}) %collective-permute-start.1) | collective-permute-done | bytes 786464 | tf_op jit(solution)/shard_map/ppermute | solution.py:707
  43.9 1.0 %shard_map.231 = (bf16[12,256,256]{2,1,0:T(8,128)(2,1)S(1)}, bf16[2,3,128,256]{3,2,1,0:T(8,128)(2,1)S(1)}, f32[256,256]{1,0:T(8,128)S(1)}, f32[256,128]{1,0:T(8,128)S(1)}) custom-call(s32[1]{0:T(128)} %bitcast.core_ref, bf16[32,232,128]{2,1,0:T(8,128)(2,1)S(1)} %all_to_all.10.recv_ref, bf16[32,96,128]{2,1,0:T(8,128)(2,1)S(1)} %collective-permute-done.1.other_ref, ...), custom_call_target="tpu_custom_call" | custom-call | tf_op jit(solution)/shard_map/pallas_call | solution.py:388
  45.0 0.0 collective-permute-done.other_ref
  45.0 2.5 %shard_map.232 = (bf16[10,256,256]{2,1,0:T(8,128)(2,1)S(1)}, bf16[32,16,128]{2,1,0:T(8,128)(2,1)S(1)}, f32[256,256]{1,0:T(8,128)S(1)}, f32[256,128]{1,0:T(8,128)...) custom-call(s32[1]{0:T(128)} %bitcast.core_ref, ...), custom_call_target="tpu_custom_call" | custom-call | tf_op jit(solution)/shard_map/pallas_call | solution.py:388
  47.4 0.7 shard_map.234
  48.1 0.5 collective-permute-start.3
  48.6 0.9 %shard_map.233 = (bf16[256,256]{1,0:T(8,128)(2,1)S(1)}, f32[256,128]{1,0:T(8,128)S(1)}) custom-call(bf16[32,232,128]{2,1,0:T(8,128)(2,1)S(1)} %all_to_all.10.recv_ref, bf16[10,256,256]{2,1,0:T(8,128)(2,1)S(1)} %get-tuple-element.53.weights, f32[256,256]{1,0:T(8,128)S(1)} %get-tuple-element.54.hat_ref, f32[256,128]{1,0:T(8,128)S(1)} %get-tuple-element.55.stats, ...), custom_call_target="tpu_custom_call" | custom-call | tf_op jit(solution)/shard_map/pallas_call | solution.py:388
  49.5 0.2 collective-permute-start.2
  49.7 0.9 shard_map.235.tail
  50.6 0.6 collective-permute-done.2.their_low
  51.1 0.0 collective-permute-done.3.swapped
  51.1 0.8 shard_map.236
  52.0 28.9 %all_to_all.11.back_ref = bf16[32,216,128]{2,1,0:T(8,128)(2,1)S(1)} all-to-all(bf16[32,216,128]{2,1,0:T(8,128)(2,1)S(1)} %shard_map.236), channel_id=1, replica_groups=mesh['ch'=32,'img'=4] {'ch'}, dimensions={0} | all-to-all | bytes 3538944 | tf_op jit(solution)/shard_map/all_to_all | solution.py:709
  80.8 0.3 shard_map.237
  81.1 0.8 collective-permute-start.4
  82.0 0.8 shard_map.238
  82.7 1.5 %collective-permute-done.4 = bf16[224,128]{1,0:T(8,128)(2,1)S(1)} collective-permute-done((bf16[224,128]{1,0:T(8,128)(2,1)S(1)}, bf16[224,128]{1,0:T(8,128)(2,1)S(1)}, u32[]{:S(2)}, u32[]{:S(2)}) %collective-permute-start.4) | collective-permute-done | bytes 57376 | tf_op jit(solution)/shard_map/ppermute | solution.py:712
  84.3 3.3 %collective-permute-start.5 = (f32[224,128]{1,0:T(8,128)S(1)}, f32[224,128]{1,0:T(8,128)S(1)}, u32[]{:S(2)}, u32[]{:S(2)}) collective-permute-start(f32[224,128]{1,0:T(8,128)S(1)} %convert_add_fusion.mine_ref), channel_id=1, source_target_pairs={{0,1},{1,0},{2,3},{3,2},{4,5},{5,4},{6,7},{7,6},{8,9},{9,8},{10,11... | collective-permute-start | bytes 344072 | tf_op jit(solution)/shard_map/ppermute | solution.py:716
  87.6 1.0 %collective-permute-done.5.theirs_ref = f32[224,128]{1,0:T(8,128)S(1)} collective-permute-done((f32[224,128]{1,0:T(8,128)S(1)}, f32[224,128]{1,0:T(8,128)S(1)}, u32[]{:S(2)}, u32[]{:S(2)}) %collective-permute-start.5) | collective-permute-done | bytes 114720 | tf_op jit(solution)/shard_map/ppermute | solution.py:716
  88.6 0.8 shard_map.239
  (2 shorter events, 0.1 us)
Async XLA Ops:
  39.4 4.5 %collective-permute-start.1 = (bf16[32,96,128]{2,1,0:T(8,128)(2,1)S(1)}, bf16[32,96,128]{2,1,0:T(8,128)(2,1)S(1)}, u32[]{:S(2)}, u32[]{:S(2)}) collective-permute-start(bf16[32,96,128]{2,1,0:T(8,128)(2,1)S(1)} %slice.9), channel_id=1, source_target_pairs={{0,1},{1,0},{2,3},{3,2},{4,5},{5,4},{6,7},{7,6},{8,9},{9,8},{10,11... | collective-permute-start | bytes 2359304 | tf_op jit(solution)/shard_map/ppermute | solution.py:707
  42.1 2.9 %collective-permute-start = (bf16[32,80,128]{2,1,0:T(8,128)(2,1)S(1)}, bf16[32,80,128]{2,1,0:T(8,128)(2,1)S(1)}, u32[]{:S(2)}, u32[]{:S(2)}) collective-permute-start(bf16[32,80,128]{2,1,0:T(8,128)(2,1)S(1)} %slice.8), channel_id=1, source_target_pairs={{0,1},{1,0},{2,3},{3,2},{4,5},{5,4},{6,7},{7,6},{8,9},{9,8},{10,11... | collective-permute-start | bytes 1966088 | tf_op jit(solution)/shard_map/ppermute | solution.py:707
  48.1 3.0 %collective-permute-start.3 = (bf16[4352,128]{1,0:T(8,128)(2,1)S(1)}, bf16[4352,128]{1,0:T(8,128)(2,1)S(1)}, u32[]{:S(2)}, u32[]{:S(2)}) collective-permute-start(bf16[4352,128]{1,0:T(8,128)(2,1)S(1)} %get-tuple-element.63), channel_id=1, source_target_pairs={{0,1},{1,0},{2,3},{3,2},{4,5},{5,4},{6,7},{7,6},{8,9},{9,8},{10,11... | collective-permute-start | bytes 3342344 | tf_op jit(solution)/shard_map/ppermute | solution.py:707
  49.5 1.6 %collective-permute-start.2 = (bf16[256,256]{1,0:T(8,128)(2,1)S(1)}, bf16[256,256]{1,0:T(8,128)(2,1)S(1)}, u32[]{:S(2)}, u32[]{:S(2)}) collective-permute-start(bf16[256,256]{1,0:T(8,128)(2,1)S(1)} %get-tuple-element.58.low_ref), channel_id=1, source_target_pairs={{0,1},{1,0},{2,3},{3,2},{4,5},{5,4},{6,7},{7,6},{8,9},{9,8},{10,11... | collective-permute-start | bytes 393224 | tf_op jit(solution)/shard_map/ppermute | solution.py:707
  81.1 3.1 %collective-permute-start.4 = (bf16[224,128]{1,0:T(8,128)(2,1)S(1)}, bf16[224,128]{1,0:T(8,128)(2,1)S(1)}, u32[]{:S(2)}, u32[]{:S(2)}) collective-permute-start(bf16[224,128]{1,0:T(8,128)(2,1)S(1)} %shard_map.237), channel_id=1, source_target_pairs={{0,2},{1,3},{2,0},{3,1},{4,6},{5,7},{6,4},{7,5},{8,10},{9,11},{10,... | collective-permute-start | bytes 172040 | tf_op jit(solution)/shard_map/ppermute | solution.py:712
  84.3 4.3 %collective-permute-start.5 = (f32[224,128]{1,0:T(8,128)S(1)}, f32[224,128]{1,0:T(8,128)S(1)}, u32[]{:S(2)}, u32[]{:S(2)}) collective-permute-start(f32[224,128]{1,0:T(8,128)S(1)} %convert_add_fusion.mine_ref), channel_id=1, source_target_pairs={{0,1},{1,0},{2,3},{3,2},{4,5},{5,4},{6,7},{7,6},{8,9},{9,8},{10,11... | collective-permute-start | bytes 344072 | tf_op jit(solution)/shard_map/ppermute | solution.py:716

commit v6 on v5

--- a/solution.py
+++ b/solution.py
@@ -92,17 +92,29 @@
     return jnp.concatenate([edge, moved[:, HALF:]], axis=1)
 
 
-def load_weights(mine_ref, theirs_ref, first_row, blocks, first_core, weights):
-    for pair in range(blocks // 2):
-        rows = slice(first_row + 16 * pair, first_row + 16 * pair + 16)
-        mine = mine_ref[:, rows, :].astype(F32)
-        theirs = theirs_ref[:, 16 * pair : 16 * pair + 16, :].astype(F32)
+def store_matrices(ref, first_row, target):
+    for pair in range(target.shape[0] // 2):
+        rows = ref[:, first_row + 16 * pair : first_row + 16 * pair + 16, :].astype(F32)
         for part in range(2):
-            rows = slice(ROWS * part, ROWS * part + ROWS)
-            a = mine[:, rows, :].reshape(C, HALF)
-            b = theirs[:, rows, :].reshape(C, HALF)
-            weights[2 * pair + part, :, 0:HALF] = jnp.where(first_core, a, b).astype(BF16)
-            weights[2 * pair + part, :, HALF:C] = jnp.where(first_core, b, a).astype(BF16)
+            cut = rows[:, ROWS * part : ROWS * part + ROWS, :]
+            target[2 * pair + part, :, :] = cut.reshape(C, HALF).astype(BF16)
+
+
+def matrix(own, other, block, first_other):
+    return jnp.concatenate([own[block], other[block - first_other]], axis=1)
+
+
+def own_first(ref, core):
+    halves = [ref[core], ref[1 - core]]
+    return jnp.concatenate([half.reshape(-1, POS) for half in halves], axis=0)
+
+
+def in_order(values, core):
+    top, bottom = values[:HALF], values[HALF:]
+    first = core == 0
+    return jnp.concatenate(
+        [jnp.where(first, top, bottom), jnp.where(first, bottom, top)], axis=0
+    )
 
 
 def load_image(ref, at):
@@ -125,17 +137,26 @@
         target[1, step + 1, :, :] = moved[HALF:]
 
 
-def convolve(weights, shifts):
-    stacked = jnp.concatenate([shifts[k % 2, k // 2] for k in range(6)], axis=0)
+def half_convolve(matrices, shifts):
+    operand = shifts.reshape(3 * HALF, POS)
     total = None
     for row in (0, -1, 1):
-        matrix = jnp.concatenate([weights[3 * row + 3 + k] for k in range(3)], axis=1)
-        product = dot_nn(matrix, stacked)
+        product = dot_nn(jnp.concatenate(matrices[3 * row + 3 : 3 * row + 6], axis=1), operand)
         total = product if row == 0 else total + row_shifted(product, row)
     return total
 
 
-def convolve_back(weights, low):
+def convolve(matrices, shifts, core):
+    operand = [shifts[half, step] for step in range(3) for half in (core, 1 - core)]
+    operand = jnp.concatenate(operand, axis=0)
+    total = None
+    for row in (0, -1, 1):
+        product = dot_nn(jnp.concatenate(matrices[3 * row + 3 : 3 * row + 6], axis=1), operand)
+        total = product if row == 0 else total + row_shifted(product, row)
+    return total
+
+
+def convolve_back(matrices, low, core):
     turned = low.astype(F32).T.astype(BF16)
     edge = jnp.zeros((SIDE, C), BF16)
     stacked = jnp.concatenate(
@@ -148,16 +169,9 @@
     )
     total = None
     for step in (0, -1, 1):
-        matrix = jnp.concatenate([weights[3 * k + step + 1] for k in range(3)], axis=0)
-        product = dot_nn(stacked, matrix)
+        product = dot_nn(stacked, jnp.concatenate(matrices[step + 1 :: 3], axis=0))
         total = product if step == 0 else total + column_shifted(product, -step, 0)
-    return total.T
-
-
-def own_first(ref, core):
-    count = math.prod(ref.shape[1:-1])
-    halves = [ref[core].reshape(count, POS), ref[1 - core].reshape(count, POS)]
-    return jnp.concatenate(halves, axis=0)
+    return in_order(total.T, core)
 
 
 def lane_blocks(product):
@@ -166,28 +180,20 @@
     return [values.reshape(SHARDS, ROWS, HALF) for values in cut]
 
 
-def store_weight_grads(own_ref, swap_ref, products):
-    blocks = [lane_blocks(product) for product in products]
-    for target, at in ((own_ref, 0), (swap_ref, 1)):
-        listed = []
-        for cut in blocks:
-            listed += cut[: len(cut) // 2] if at == 0 else cut[len(cut) // 2 :]
-        if len(listed) % 2:
-            listed.append(jnp.zeros_like(listed[0]))
-        for pair in range(len(listed) // 2):
-            both = jnp.concatenate(listed[2 * pair : 2 * pair + 2], axis=1)
-            rows = slice(PAIR_ROWS * pair, PAIR_ROWS * pair + PAIR_ROWS)
-            target[rows, :] = both.reshape(PAIR_ROWS, HALF).astype(BF16)
-
-
-def conv_weight_grads(low, shifts, core):
-    wide = low.astype(F32)
-    operand = own_first(shifts, core)
-    grads = []
+def conv_weight_grads(lows, shifts):
+    operand = jnp.concatenate([part.reshape(3 * HALF, POS) for part in shifts], axis=1)
+    wide = [low.astype(F32) for low in lows]
+    blocks = []
     for row in (-1, 0, 1):
-        moved = row_shifted(wide, -row).astype(BF16) if row else low
-        grads.append(dot_nt(moved, operand))
-    return grads
+        moved = [row_shifted(values, -row) if row else values for values in wide]
+        blocks += lane_blocks(dot_nt(jnp.concatenate(moved, axis=1).astype(BF16), operand))
+    return blocks
+
+
+def store_blocks(target, blocks):
+    for pair in range(len(blocks) // 2):
+        rows = jnp.concatenate(blocks[2 * pair : 2 * pair + 2], axis=1)
+        target[:, 16 * pair : 16 * pair + 16, :] = rows.astype(BF16)
 
 
 def columns_of(listed, table):
@@ -210,7 +216,7 @@
     return sigma * (1.0 + values * (1.0 - sigma))
 
 
-def first_kernel(recv_ref, taps_ref, hat_ref, params_ref, stats_ref):
+def first_kernel(core_ref, recv_ref, taps_ref, hat_ref, params_ref, stats_ref, own_ref, partial_ref):
     columns = recv_ref[:, AT_PARAMS : AT_PARAMS + ROWS, :].astype(F32).reshape(C, HALF)
     columns = (
         columns
@@ -223,38 +229,57 @@
     stats_ref[...] = jnp.broadcast_to(inverse, (C, HALF))
     pre = hat * columns[:, GAINS : GAINS + 1] + columns[:, BIASES : BIASES + 1]
     store_shifts(taps_ref, (pre * sigmoid(pre)).astype(BF16).astype(F32))
+    store_matrices(recv_ref, 0, own_ref)
+    partial_ref[...] = half_convolve([own_ref[tap] for tap in range(9)], taps_ref[core_ref[0]])
 
 
 def middle_kernel(
-    core_ref, recv_ref, other_ref, taps_one, params, weights, taps_ref, hat_ref, stats_ref
+    core_ref, recv_ref, swapped, taps_one, params, partial,
+    other, taps_ref, hat_ref, stats_ref, halves_ref,
 ):
-    load_weights(recv_ref, other_ref, 0, IN_CUT, core_ref[0] == 0, weights)
-    middle = convolve(weights, taps_one) + (column(params, CONV_BIAS) + column(params, OFFSETS))
+    store_matrices(swapped, 0, other)
+    rest = half_convolve([other[tap] for tap in range(9)], taps_one[1 - core_ref[0]])
+    middle = partial[...] + rest
+    middle = middle + (column(params, CONV_BIAS) + column(params, OFFSETS))
     hat, inverse = norm_hat(middle)
     hat_ref[...] = hat
     stats_ref[...] = jnp.broadcast_to(inverse, (C, HALF))
     pre = hat * column(params, GAINS + 1) + column(params, BIASES + 1)
     keep = load_image(recv_ref, AT_KEEP) * (1.0 / 0.9)
     store_shifts(taps_ref, (pre * sigmoid(pre) * keep).astype(BF16).astype(F32))
+    away = 1 - core_ref[0]
+    halves_ref[0 : 3 * HALF, :] = taps_one[away].reshape(3 * HALF, POS)
+    halves_ref[3 * HALF : 6 * HALF, :] = taps_ref[away].reshape(3 * HALF, POS)
+    halves_ref[6 * HALF :, :] = load_image(recv_ref, AT_COTANGENT).astype(BF16)
 
 
 def attention_kernel(
-    core_ref, recv_ref, other_ref, taps_two, params, first_weights,
-    weights, outputs_ref, grad_ref, sums_ref, normed_ref, halves_ref, grads_ref,
+    core_ref, recv_ref, swapped, taps_two, params, own, other_one,
+    other, outputs_ref, grad_ref, sums_ref, normed_ref, halves_ref, grads_ref, swap_ref,
 ):
-    first_core = core_ref[0] == 0
-    load_weights(recv_ref, other_ref, IN_CUT_ROWS, WBLOCKS - IN_CUT, first_core, weights)
+    core = core_ref[0]
+    store_matrices(swapped, 0, other)
+    out_matrix = matrix(own, other_one, OUT_BLOCK, 0)
+    qkv = [
+        matrix(own, other_one, QUERY_BLOCK, 0),
+        matrix(own, other_one, KEY_BLOCK, 0),
+        matrix(own, other, VALUE_BLOCK, IN_CUT),
+    ]
     cotangent = load_image(recv_ref, AT_COTANGENT)
     cot_low = cotangent.astype(BF16)
-    attended_grad = dot_tn(first_weights[OUT_BLOCK], cot_low).astype(BF16)
+    attended_grad = in_order(dot_tn(out_matrix, cot_low), core).astype(BF16)
     source = load_image(recv_ref, AT_SOURCE)
-    residual = source + convolve(weights, taps_two) + column(params, CONV_BIAS + 1)
+    matrices = [matrix(own, other, SECOND_CONV + tap, IN_CUT) for tap in range(9)]
+    residual = source + convolve(matrices, taps_two, core) + column(params, CONV_BIAS + 1)
     hat, inverse = norm_hat(residual)
     normed = (hat * column(params, GAINS + 2) + column(params, BIASES + 2)).astype(BF16)
     scale = C ** (-0.5)
-    queries = (dot_nn(first_weights[QUERY_BLOCK], normed) + column(params, QV_BIAS)).astype(BF16)
-    keys = dot_nn(first_weights[KEY_BLOCK], normed).astype(BF16)
-    vals = (dot_nn(weights[VALUE_BLOCK - IN_CUT], normed) + column(params, QV_BIAS + 1)).astype(BF16)
+    normed_ref[0] = normed[:HALF]
+    normed_ref[1] = normed[HALF:]
+    operand = own_first(normed_ref, core)
+    queries = (dot_nn(qkv[0], operand) + column(params, QV_BIAS)).astype(BF16)
+    keys = dot_nn(qkv[1], operand).astype(BF16)
+    vals = (dot_nn(qkv[2], operand) + column(params, QV_BIAS + 1)).astype(BF16)
     scores = dot_tn(queries, keys) * scale
     dprobs = dot_tn(attended_grad, vals)
     exps = jnp.exp(scores - jnp.max(scores, axis=1, keepdims=True))
@@ -264,23 +289,27 @@
     query_grad = (dot_nt(keys, dscores) * scale).astype(BF16)
     key_grad = (dot_nn(queries, dscores) * scale).astype(BF16)
     value_grad = dot_nn(attended_grad, probs_low).astype(BF16)
-    matrices = [first_weights[QUERY_BLOCK], first_weights[KEY_BLOCK], weights[VALUE_BLOCK - IN_CUT]]
     normed_grad = dot_tn(
-        jnp.concatenate(matrices, axis=0),
+        jnp.concatenate(qkv, axis=0),
         jnp.concatenate([query_grad, key_grad, value_grad], axis=0),
     )
-    normed_ref[0] = normed[:HALF]
-    normed_ref[1] = normed[HALF:]
+    normed_grad = in_order(normed_grad, core)
     for k, gradient in enumerate((query_grad, key_grad, value_grad)):
         grads_ref[k, :, :] = gradient
     attended = dot_nt(vals, probs_low).astype(BF16)
     halves_ref[0] = attended[:HALF]
     halves_ref[1] = attended[HALF:]
-    outputs = residual + dot_nn(first_weights[OUT_BLOCK], attended) + column(params, OUT_BIAS)
+    product = dot_nn(out_matrix, own_first(halves_ref, core))
+    outputs = residual + product + column(params, OUT_BIAS)
     outputs_ref[...] = image_rows(outputs)
     branch, gain_grad, bias_grad = norm_back(hat, inverse, normed_grad, column(params, GAINS + 2))
     residual_grad = cotangent + branch
     grad_ref[...] = residual_grad
+    swap_ref[0:HALF, :] = normed_ref[1 - core]
+    swap_ref[HALF:C, :] = halves_ref[1 - core]
+    swap_ref[C : 2 * C, :] = residual_grad.astype(BF16)
+    for k, gradient in enumerate((query_grad, key_grad, value_grad)):
+        swap_ref[C * k + 2 * C : C * k + 3 * C, :] = gradient
     listed = {
         D_GAINS + 2: gain_grad,
         D_BIASES + 2: bias_grad,
@@ -292,32 +321,16 @@
     sums_ref[...] = columns_of(listed, jnp.zeros((C, HALF), F32))
 
 
-def early_grads_kernel(
-    core_ref, recv_ref, taps_one, taps_two, grad_ref, normed_ref, halves_ref, grads_ref,
-    own_ref, swap_ref,
-):
-    core = core_ref[0]
-    other_half = taps_one[1 - core].reshape(3 * HALF, POS)
-    swap_ref[EARLY_ROWS : EARLY_ROWS + 3 * HALF, :] = other_half[:, :HALF]
-    swap_ref[EARLY_ROWS + 3 * HALF :, :] = other_half[:, HALF:]
-    operand = own_first(normed_ref, core)
-    dqkv = [dot_nt(grads_ref[k], operand) for k in range(3)]
-    cot_low = load_image(recv_ref, AT_COTANGENT).astype(BF16)
-    out_grad = dot_nt(cot_low, own_first(halves_ref, core))
-    low = grad_ref[...].astype(BF16)
-    grads = dqkv[:2] + conv_weight_grads(low, taps_two, core) + [dqkv[2], out_grad]
-    store_weight_grads(own_ref, swap_ref, grads)
-
-
 def middle_back_kernel(
-    recv_ref, weights, hat_ref, stats, params, grad_ref, sums, low_ref, sums_ref
+    core_ref, recv_ref, own, other, hat_ref, stats, params, grad_ref, sums, low_ref, sums_ref
 ):
     hat = hat_ref[...]
     gain = column(params, GAINS + 1)
     pre = hat * gain + column(params, BIASES + 1)
     keep = load_image(recv_ref, AT_KEEP) * (1.0 / 0.9)
     factor = keep * slope(pre)
-    second_grad = convolve_back(weights, grad_ref[...].astype(BF16))
+    matrices = [matrix(own, other, SECOND_CONV + tap, IN_CUT) for tap in range(9)]
+    second_grad = convolve_back(matrices, grad_ref[...].astype(BF16), core_ref[0])
     pre_grad = second_grad * factor
     middle_grad, gain_grad, bias_grad = norm_back(hat, column(stats, 0), pre_grad, gain)
     low_ref[...] = middle_grad.astype(BF16)
@@ -325,12 +338,15 @@
     sums_ref[...] = columns_of(listed, sums[...])
 
 
-def first_back_kernel(weights, hat_ref, stats, params, low_ref, grad_ref, sums, tail_ref):
+def first_back_kernel(
+    core_ref, own, other, hat_ref, stats, params, low_ref, grad_ref, sums, tail_ref
+):
     hat = hat_ref[...]
     gain = column(params, GAINS)
     pre = hat * gain + column(params, BIASES)
     factor = slope(pre)
-    first_grad = convolve_back(weights, low_ref[...])
+    matrices = [matrix(own, other, tap, 0) for tap in range(9)]
+    first_grad = convolve_back(matrices, low_ref[...], core_ref[0])
     branch, gain_grad, bias_grad = norm_back(hat, column(stats, 0), first_grad * factor, gain)
     tail_ref[:, :16, :] = image_rows(grad_ref[...] + branch)
 
@@ -342,29 +358,36 @@
     tail_ref[:, 16:, :] = jnp.concatenate([table, jnp.zeros_like(table)], axis=1).astype(BF16)
 
 
-def gather_kernel(core_ref, shifts, low_ref, their_low, own, swapped, outputs, tail, send_ref):
-    mine = shifts[core_ref[0]].reshape(3 * HALF, POS)
-    left = swapped[EARLY_ROWS : EARLY_ROWS + 3 * HALF, :]
-    right = swapped[EARLY_ROWS + 3 * HALF :, :]
-    operand = jnp.concatenate([mine, left, right], axis=1)
-    wide = [low_ref[...].astype(F32), their_low[...].astype(F32)]
-    blocks = []
-    for row in (-1, 0, 1):
-        moved = [row_shifted(values, -row) if row else values for values in wide]
-        blocks += lane_blocks(dot_nt(jnp.concatenate(moved, axis=1).astype(BF16), operand))
-
-    def early(pair):
-        rows = slice(PAIR_ROWS * pair, PAIR_ROWS * pair + PAIR_ROWS)
-        both = own[rows, :].astype(F32) + swapped[rows, :].astype(F32)
-        return both.reshape(SHARDS, 16, HALF)
-
-    blocks.append(early(EARLY_PAIRS - 1)[:, :ROWS, :])
-    for pair in range(len(blocks) // 2):
-        rows = jnp.concatenate(blocks[2 * pair : 2 * pair + 2], axis=1)
-        send_ref[:, 16 * pair : 16 * pair + 16, :] = rows.astype(BF16)
-    for pair in range(EARLY_PAIRS - 1):
-        to = OUT_CUT_ROWS + 16 * pair
-        send_ref[:, to : to + 16, :] = early(pair).astype(BF16)
+def second_grads_kernel(
+    core_ref, recv_ref, taps_two, normed, attended, gradients, grad_ref, their_shifts, theirs,
+    late_ref,
+):
+    core = core_ref[0]
+    low = grad_ref[...].astype(BF16)
+    second = conv_weight_grads(
+        [low, theirs[C : 2 * C, :]], [taps_two[core], their_shifts[3 * HALF : 6 * HALF, :]]
+    )
+    operand = jnp.concatenate([normed[core], theirs[0:HALF, :]], axis=1)
+    grads = jnp.concatenate([gradients[...].reshape(3 * C, POS), theirs[2 * C :, :]], axis=1)
+    qkv = dot_nt(grads, operand)
+    query, key, value = [lane_blocks(qkv[C * k : C * k + C])[0] for k in range(3)]
+    operand = jnp.concatenate([attended[core], theirs[HALF:C, :]], axis=1)
+    cotangent = load_image(recv_ref, AT_COTANGENT).astype(BF16)
+    cotangents = jnp.concatenate([cotangent, their_shifts[6 * HALF :, :]], axis=1)
+    out = lane_blocks(dot_nt(cotangents, operand))[0]
+    store_blocks(late_ref, [query, key, *second, value, out, jnp.zeros_like(out)])
+
+
+def gather_kernel(
+    core_ref, taps_one, low_ref, their_shifts, their_low, late, outputs, tail, send_ref
+):
+    first = conv_weight_grads(
+        [low_ref[...], their_low[...]], [taps_one[core_ref[0]], their_shifts[0 : 3 * HALF, :]]
+    )
+    cut = WROWS - IN_CUT_ROWS + 16
+    out = late[:, cut : cut + 16, :].astype(F32)[:, :ROWS, :]
+    store_blocks(send_ref, first + [out])
+    send_ref[:, IN_CUT_ROWS - 16 : WROWS, :] = late[:, :cut, :]
     send_ref[:, WROWS : WROWS + 16, :] = outputs[...]
     send_ref[:, WROWS + 16 : WROWS + 40, :] = tail[:, :24, :]
 
@@ -373,10 +396,8 @@
 IN_ROWS = WROWS + 56
 OUT_ROWS = WROWS + 40
 OUT_BLOCK, QUERY_BLOCK, KEY_BLOCK, SECOND_CONV, VALUE_BLOCK = 9, 10, 11, 12, 21
-IN_CUT, OUT_CUT = 12, 10
-IN_CUT_ROWS, OUT_CUT_ROWS = IN_CUT * ROWS, OUT_CUT * ROWS
-EARLY_PAIRS, PAIR_ROWS = (WBLOCKS - OUT_CUT) // 2 + 1, 16 * SHARDS
-EARLY_ROWS = EARLY_PAIRS * PAIR_ROWS
+IN_CUT = 12
+IN_CUT_ROWS = IN_CUT * ROWS
 
 
 def local_call(kernel, core, *operands, out):
@@ -398,41 +419,49 @@
 
 
 def run_block(core, received, swap):
-    other_one = swap(received[:, :IN_CUT_ROWS])
-    other_two = swap(received[:, IN_CUT_ROWS:WROWS])
+    swapped_one = swap(received[:, :IN_CUT_ROWS])
+    swapped_two = swap(received[:, IN_CUT_ROWS:WROWS])
     image, table = ((C, POS), F32), ((C, HALF), F32)
     taps, low = ((2, 3, HALF, POS), BF16), ((C, POS), BF16)
     halves = ((2, HALF, POS), BF16)
 
-    taps_one, hat_one, params, stats_one = local_call(
-        first_kernel, None, received, out=(taps, image, table, table)
-    )
-    weights_one, taps_two, hat_two, stats_two = local_call(
-        middle_kernel, core, received, other_one, taps_one, params,
-        out=(((IN_CUT, C, C), BF16), taps, image, table),
+    def matrices(count):
+        return ((count, C, HALF), BF16)
+
+
+    taps_one, hat_one, params, stats_one, own_weights, partial = local_call(
+        first_kernel, core, received, out=(taps, image, table, table, matrices(WBLOCKS), image)
+    )
+    other_weights, taps_two, hat_two, stats_two, halves_out = local_call(
+        middle_kernel, core, received, swapped_one, taps_one, params, partial,
+        out=(matrices(IN_CUT), taps, image, table, ((6 * HALF + C, POS), BF16)),
     )
     rows = ((SHARDS, 16, HALF), BF16)
-    weights_two, outputs, residual_grad, sums, normed, attended, gradients = local_call(
-        attention_kernel, core, received, other_two, taps_two, params, weights_one,
-        out=(((WBLOCKS - IN_CUT, C, C), BF16), rows, image, table, halves, halves, ((3, C, POS), BF16)),
-    )
-    own, swap_early = local_call(
-        early_grads_kernel, core, received, taps_one, taps_two, residual_grad, normed, attended,
-        gradients,
-        out=(((EARLY_ROWS, HALF), BF16), ((EARLY_ROWS + 6 * HALF, HALF), BF16)),
-    )
-    swapped = swap(swap_early)
+    their_shifts = swap(halves_out)
+    other_two, outputs, residual_grad, sums, normed, attended, gradients, swapping = local_call(
+        attention_kernel, core, received, swapped_two, taps_two, params, own_weights, other_weights,
+        out=(
+            matrices(WBLOCKS - IN_CUT), rows, image, table, halves, halves, ((3, C, POS), BF16),
+            ((5 * C, POS), BF16),
+        ),
+    )
+    theirs = swap(swapping)
+    residual_grad, their_shifts = lax.optimization_barrier((residual_grad, their_shifts))
     low_one, sums = local_call(
-        middle_back_kernel, None, received, weights_two, hat_two, stats_two, params,
+        middle_back_kernel, core, received, own_weights, other_two, hat_two, stats_two, params,
         residual_grad, sums, out=(low, table),
     )
     their_low = swap(low_one)
     (tail,) = local_call(
-        first_back_kernel, None, weights_one, hat_one, stats_one, params, low_one,
+        first_back_kernel, core, own_weights, other_weights, hat_one, stats_one, params, low_one,
         residual_grad, sums, out=(((SHARDS, 32, HALF), BF16),),
     )
+    (late,) = local_call(
+        second_grads_kernel, core, received, taps_two, normed, attended, gradients, residual_grad,
+        their_shifts, theirs, out=(((SHARDS, WROWS - IN_CUT_ROWS + 32, HALF), BF16),),
+    )
     (send,) = local_call(
-        gather_kernel, core, taps_one, low_one, their_low, own, swapped, outputs, tail,
+        gather_kernel, core, taps_one, low_one, their_shifts, their_low, late, outputs, tail,
         out=(((SHARDS, OUT_ROWS, HALF), BF16),),
     )
     return send

time: 89.6 us -> 89.2 us (level)
  waiting for transfers between devices: 4.3 us -> 3.22 us
    ppermute x4 -> x5, waiting for transfers between devices: 1.83 us -> 0.75 us  [on_device(): lax.ppermute(values, 'img', core_pairs)]
    ppermute x4 -> x5, starting transfers between devices: 3.32 us -> 3.77 us  [on_device(): lax.ppermute(values, 'img', core_pairs)]
  transfers between devices with their start and end apart: 6 -> 7, of which waited for: 4 -> 3; matrix products, arithmetic and copies ran while one was open for 0% -> 0% of each run, Pallas kernels for 5% -> 9%
where the time goes in v6:
time: 89.2 us; the launch traced here: 89.1 us
  blocking collectives  66.1 us (74%)
  Pallas kernels  11.3 us (13%)
  starting transfers between devices  7.53 us (8%)
  waiting for transfers between devices  3.22 us (4%)
    all_to_all x1, blocking collectives, on_device(): lax.all_to_all(sent, 'ch', split_axis=0, concat_axis=0, tiled=True)  37 us
    all_to_all x1, blocking collectives, on_device(): back = lax.all_to_all(send, 'ch', split_axis=0, concat_axis=0, tiled=True)  29.1 us
    pallas_call x7, Pallas kernels, local_call(): pl.pallas_call(kernel, out_shape=shapes, in_specs=in_specs, out_specs=tup...  7.72 us
    ppermute x5, starting transfers between devices, on_device(): lax.ppermute(values, 'img', core_pairs)  3.77 us
    ppermute x1, starting transfers between devices, on_device(): theirs = lax.ppermute(sums, 'img', core_pairs)  2.93 us
  transfers between devices with their start and end apart: 7, of which 3 were waited for; matrix products, arithmetic and copies ran while one was open for 0% of the time, Pallas kernels for 9%

profile of v6, /device:TPU:1, one launch (start us, length us, event | category | flops | bytes accessed | tf_op | source)
XLA Modules:
  0.0 89.1 jit_solution(6308028799807875849)
XLA Ops:
  0.7 1.7 %shard_map.229 = (bf16[32,232,128]{2,1,0:T(8,128)(2,1)S(1)}, f32[32,512]{1,0:T(8,128)S(1)}) custom-call(s32[1]{0:T(128)} %bitcast.core_ref, s32[32]{0:T(128)} %refs_0_.1, f32[3,8]{1,0:T(4,128)} %refs_1_.1, f32[3,8]{1,0:T(4,128)} %refs_2_.1, f32[2,8]{1,0:T(2,128)} %refs_3_.1, f32[2,8]{1,0:T(2,128)} %refs_4_.1, f32[1,8]{1,0:T(1,128)} %bitcast.8, ...), custom_call_target="tpu_custom_call" | custom-call | tf_op jit(solution)/shard_map/pallas_call | solution.py:682
  2.4 37.0 %all_to_all.10.recv_ref = bf16[32,232,128]{2,1,0:T(8,128)(2,1)S(1)} all-to-all(bf16[32,232,128]{2,1,0:T(8,128)(2,1)S(1)} %get-tuple-element.52), channel_id=1, replica_groups=mesh['ch'=32,'img'=4] {'ch'}, dimensions={0} | all-to-all | bytes 3801088 | tf_op jit(solution)/shard_map/all_to_all | solution.py:734
  39.4 0.1 slice.9
  39.4 2.6 %collective-permute-start.1 = (bf16[32,96,128]{2,1,0:T(8,128)(2,1)S(1)}, bf16[32,96,128]{2,1,0:T(8,128)(2,1)S(1)}, u32[]{:S(2)}, u32[]{:S(2)}) collective-permute-start(bf16[32,96,128]{2,1,0:T(8,128)(2,1)S(1)} %slice.9), channel_id=1, source_target_pairs={{0,1},{1,0},{2,3},{3,2},{4,5},{5,4},{6,7},{7,6},{8,9},{9,8},{10,11... | collective-permute-start | bytes 2359304 | tf_op jit(solution)/shard_map/ppermute | solution.py:736
  42.1 0.1 collective-permute-start
  42.1 1.0 %shard_map.230 = (bf16[2,3,128,256]{3,2,1,0:T(8,128)(2,1)S(1)}, f32[256,256]{1,0:T(8,128)S(1)}, f32[256,128]{1,0:T(8,128)S(1)}, f32[256,128]{1,0:T(8,128)S(1)}, ...) custom-call(s32[1]{0:T(128)} %bitcast.core_ref, bf16[32,232,128]{2,1,0:T(8,128)(2,1)S(1)} %all_to_all.10.recv_ref), custom_call_target="tpu_custom_call" | custom-call | tf_op jit(solution)/shard_map/pallas_call | solution.py:409
  43.2 0.7 collective-permute-done.1.swapped
  43.9 0.9 shard_map.231
  44.8 0.5 collective-permute-start.2
  45.2 0.0 collective-permute-done.swapped
  45.2 2.5 %shard_map.232 = (bf16[10,256,128]{2,1,0:T(8,128)(2,1)S(1)}, bf16[32,16,128]{2,1,0:T(8,128)(2,1)S(1)}, f32[256,256]{1,0:T(8,128)S(1)}, f32[256,128]{1,0:T(8,128)...) custom-call(s32[1]{0:T(128)} %bitcast.core_ref, ...), custom_call_target="tpu_custom_call" | custom-call | tf_op jit(solution)/shard_map/pallas_call | solution.py:409
  47.7 0.2 collective-permute-start.4
  47.9 0.0 collective-permute-done.2.their_shifts
  47.9 0.9 %shard_map.233 = (bf16[256,256]{1,0:T(8,128)(2,1)S(1)}, f32[256,128]{1,0:T(8,128)S(1)}) custom-call(s32[1]{0:T(128)} %bitcast.core_ref, bf16[32,232,128]{2,1,0:T(8,128)(2,1)S(1)} %all_to_all.10.recv_ref, bf16[22,256,128]{2,1,0:T(8,128)(2,1)S(1)} %get-tuple-element.54.own, bf16[10,256,128]{2,1,0:T(8,128)(2,1)S(1)} %get-tuple-element.59.other, ...), custom_call_target="tpu_custom_call" | custom-call | tf_op jit(solution)/shard_map/pallas_call | solution.py:409
  48.9 0.4 collective-permute-start.3
  49.3 0.9 shard_map.235.tail
  50.2 0.0 collective-permute-done.4.theirs
  50.2 0.9 %shard_map.234.late = bf16[32,112,128]{2,1,0:T(8,128)(2,1)S(1)} custom-call(s32[1]{0:T(128)} %bitcast.core_ref, bf16[32,232,128]{2,1,0:T(8,128)(2,1)S(1)} %all_to_all.10.recv_ref, bf16[2,3,128,256]{3,2,1,0:T(8,128)(2,1)S(1)} %get-tuple-element.57.taps_two, bf16[2,128,256]{2,1,0:T(8,128)(2,1)S(1)} %get-tuple-element.68.normed, ...), custom_call_target="tpu_custom_call" | custom-call | tf_op jit(solution)/shard_map/pallas_call | solution.py:409
  51.1 0.0 collective-permute-done.3.their_low
  51.2 0.6 shard_map.236
  51.8 29.1 %all_to_all.11.back_ref = bf16[32,216,128]{2,1,0:T(8,128)(2,1)S(1)} all-to-all(bf16[32,216,128]{2,1,0:T(8,128)(2,1)S(1)} %shard_map.236), channel_id=1, replica_groups=mesh['ch'=32,'img'=4] {'ch'}, dimensions={0} | all-to-all | bytes 3538944 | tf_op jit(solution)/shard_map/all_to_all | solution.py:738
  80.9 0.3 shard_map.237
  81.2 0.8 collective-permute-start.5
  82.0 0.8 shard_map.238
  82.8 1.5 %collective-permute-done.5 = bf16[224,128]{1,0:T(8,128)(2,1)S(1)} collective-permute-done((bf16[224,128]{1,0:T(8,128)(2,1)S(1)}, bf16[224,128]{1,0:T(8,128)(2,1)S(1)}, u32[]{:S(2)}, u32[]{:S(2)}) %collective-permute-start.5) | collective-permute-done | bytes 57376 | tf_op jit(solution)/shard_map/ppermute | solution.py:741
  84.3 2.9 %collective-permute-start.6 = (f32[224,128]{1,0:T(8,128)S(1)}, f32[224,128]{1,0:T(8,128)S(1)}, u32[]{:S(2)}, u32[]{:S(2)}) collective-permute-start(f32[224,128]{1,0:T(8,128)S(1)} %convert_add_fusion.mine_ref), channel_id=1, source_target_pairs={{0,1},{1,0},{2,3},{3,2},{4,5},{5,4},{6,7},{7,6},{8,9},{9,8},{10,11... | collective-permute-start | bytes 344072 | tf_op jit(solution)/shard_map/ppermute | solution.py:745
  87.3 1.0 %collective-permute-done.6.theirs_ref = f32[224,128]{1,0:T(8,128)S(1)} collective-permute-done((f32[224,128]{1,0:T(8,128)S(1)}, f32[224,128]{1,0:T(8,128)S(1)}, u32[]{:S(2)}, u32[]{:S(2)}) %collective-permute-start.6) | collective-permute-done | bytes 114720 | tf_op jit(solution)/shard_map/ppermute | solution.py:745
  88.2 0.8 shard_map.239
  (2 shorter events, 0.1 us)
Async XLA Ops:
  39.4 4.5 %collective-permute-start.1 = (bf16[32,96,128]{2,1,0:T(8,128)(2,1)S(1)}, bf16[32,96,128]{2,1,0:T(8,128)(2,1)S(1)}, u32[]{:S(2)}, u32[]{:S(2)}) collective-permute-start(bf16[32,96,128]{2,1,0:T(8,128)(2,1)S(1)} %slice.9), channel_id=1, source_target_pairs={{0,1},{1,0},{2,3},{3,2},{4,5},{5,4},{6,7},{7,6},{8,9},{9,8},{10,11... | collective-permute-start | bytes 2359304 | tf_op jit(solution)/shard_map/ppermute | solution.py:736
  42.1 3.2 %collective-permute-start = (bf16[32,80,128]{2,1,0:T(8,128)(2,1)S(1)}, bf16[32,80,128]{2,1,0:T(8,128)(2,1)S(1)}, u32[]{:S(2)}, u32[]{:S(2)}) collective-permute-start(bf16[32,80,128]{2,1,0:T(8,128)(2,1)S(1)} %slice.8), channel_id=1, source_target_pairs={{0,1},{1,0},{2,3},{3,2},{4,5},{5,4},{6,7},{7,6},{8,9},{9,8},{10,11... | collective-permute-start | bytes 1966088 | tf_op jit(solution)/shard_map/ppermute | solution.py:736
  44.8 3.2 %collective-permute-start.2 = (bf16[1024,256]{1,0:T(8,128)(2,1)S(1)}, bf16[1024,256]{1,0:T(8,128)(2,1)S(1)}, u32[]{:S(2)}, u32[]{:S(2)}) collective-permute-start(bf16[1024,256]{1,0:T(8,128)(2,1)S(1)} %get-tuple-element.63), channel_id=1, source_target_pairs={{0,1},{1,0},{2,3},{3,2},{4,5},{5,4},{6,7},{7,6},{8,9},{9,8},{10,11... | collective-permute-start | bytes 1572872 | tf_op jit(solution)/shard_map/ppermute | solution.py:736
  47.7 2.5 %collective-permute-start.4 = (bf16[1280,256]{1,0:T(8,128)(2,1)S(1)}, bf16[1280,256]{1,0:T(8,128)(2,1)S(1)}, u32[]{:S(2)}, u32[]{:S(2)}) collective-permute-start(bf16[1280,256]{1,0:T(8,128)(2,1)S(1)} %get-tuple-element.71), channel_id=1, source_target_pairs={{0,1},{1,0},{2,3},{3,2},{4,5},{5,4},{6,7},{7,6},{8,9},{9,8},{10,11... | collective-permute-start | bytes 1966088 | tf_op jit(solution)/shard_map/ppermute | solution.py:736
  48.9 2.3 %collective-permute-start.3 = (bf16[256,256]{1,0:T(8,128)(2,1)S(1)}, bf16[256,256]{1,0:T(8,128)(2,1)S(1)}, u32[]{:S(2)}, u32[]{:S(2)}) collective-permute-start(bf16[256,256]{1,0:T(8,128)(2,1)S(1)} %get-tuple-element.66.low_ref), channel_id=1, source_target_pairs={{0,1},{1,0},{2,3},{3,2},{4,5},{5,4},{6,7},{7,6},{8,9},{9,8},{10,11... | collective-permute-start | bytes 393224 | tf_op jit(solution)/shard_map/ppermute | solution.py:736
  81.2 3.1 %collective-permute-start.5 = (bf16[224,128]{1,0:T(8,128)(2,1)S(1)}, bf16[224,128]{1,0:T(8,128)(2,1)S(1)}, u32[]{:S(2)}, u32[]{:S(2)}) collective-permute-start(bf16[224,128]{1,0:T(8,128)(2,1)S(1)} %shard_map.237), channel_id=1, source_target_pairs={{0,2},{1,3},{2,0},{3,1},{4,6},{5,7},{6,4},{7,5},{8,10},{9,11},{10,... | collective-permute-start | bytes 172040 | tf_op jit(solution)/shard_map/ppermute | solution.py:741
  84.3 3.9 %collective-permute-start.6 = (f32[224,128]{1,0:T(8,128)S(1)}, f32[224,128]{1,0:T(8,128)S(1)}, u32[]{:S(2)}, u32[]{:S(2)}) collective-permute-start(f32[224,128]{1,0:T(8,128)S(1)} %convert_add_fusion.mine_ref), channel_id=1, source_target_pairs={{0,1},{1,0},{2,3},{3,2},{4,5},{5,4},{6,7},{7,6},{8,9},{9,8},{10,11... | collective-permute-start | bytes 344072 | tf_op jit(solution)/shard_map/ppermute | solution.py:745

commit v7 on v6

--- a/solution.py
+++ b/solution.py
@@ -181,13 +181,12 @@
 
 
 def conv_weight_grads(lows, shifts):
-    operand = jnp.concatenate([part.reshape(3 * HALF, POS) for part in shifts], axis=1)
-    wide = [low.astype(F32) for low in lows]
-    blocks = []
+    wide = [part.reshape(3 * HALF, POS) for part in shifts]
+    rows = []
     for row in (-1, 0, 1):
-        moved = [row_shifted(values, -row) if row else values for values in wide]
-        blocks += lane_blocks(dot_nt(jnp.concatenate(moved, axis=1).astype(BF16), operand))
-    return blocks
+        moved = [row_shifted(part.astype(F32), row).astype(BF16) if row else part for part in wide]
+        rows.append(jnp.concatenate(moved, axis=1))
+    return lane_blocks(dot_nt(jnp.concatenate(lows, axis=1), jnp.concatenate(rows, axis=0)))
 
 
 def store_blocks(target, blocks):
@@ -205,6 +204,10 @@
 
 def column(ref, lane):
     return ref[:, lane : lane + 1]
+
+
+def by_rows(dot, left, right):
+    return jnp.concatenate([dot(left[:HALF], right), dot(left[HALF:], right)], axis=0)
 
 
 def row_sum(values):
@@ -255,7 +258,7 @@
 
 def attention_kernel(
     core_ref, recv_ref, swapped, taps_two, params, own, other_one,
-    other, outputs_ref, grad_ref, sums_ref, normed_ref, halves_ref, grads_ref, swap_ref,
+    other, outputs_ref, grad_ref, sums_ref, normed_ref, halves_ref, grads_ref, swap_ref, turned,
 ):
     core = core_ref[0]
     store_matrices(swapped, 0, other)
@@ -265,6 +268,8 @@
         matrix(own, other_one, KEY_BLOCK, 0),
         matrix(own, other, VALUE_BLOCK, IN_CUT),
     ]
+    for k in range(3):
+        turned[:, C * k : C * k + C] = qkv[k].T
     cotangent = load_image(recv_ref, AT_COTANGENT)
     cot_low = cotangent.astype(BF16)
     attended_grad = in_order(dot_tn(out_matrix, cot_low), core).astype(BF16)
@@ -277,29 +282,27 @@
     normed_ref[0] = normed[:HALF]
     normed_ref[1] = normed[HALF:]
     operand = own_first(normed_ref, core)
-    queries = (dot_nn(qkv[0], operand) + column(params, QV_BIAS)).astype(BF16)
-    keys = dot_nn(qkv[1], operand).astype(BF16)
-    vals = (dot_nn(qkv[2], operand) + column(params, QV_BIAS + 1)).astype(BF16)
+    queries = (by_rows(dot_nn, qkv[0], operand) + column(params, QV_BIAS)).astype(BF16)
+    keys = by_rows(dot_nn, qkv[1], operand).astype(BF16)
+    vals = (by_rows(dot_nn, qkv[2], operand) + column(params, QV_BIAS + 1)).astype(BF16)
     scores = dot_tn(queries, keys) * scale
     dprobs = dot_tn(attended_grad, vals)
     exps = jnp.exp(scores - jnp.max(scores, axis=1, keepdims=True))
     probs = exps / row_sum(exps)
     probs_low = probs.astype(BF16)
     dscores = (probs * (dprobs - row_sum(probs * dprobs))).astype(BF16)
-    query_grad = (dot_nt(keys, dscores) * scale).astype(BF16)
-    key_grad = (dot_nn(queries, dscores) * scale).astype(BF16)
-    value_grad = dot_nn(attended_grad, probs_low).astype(BF16)
-    normed_grad = dot_tn(
-        jnp.concatenate(qkv, axis=0),
-        jnp.concatenate([query_grad, key_grad, value_grad], axis=0),
-    )
+    query_grad = (by_rows(dot_nt, keys, dscores) * scale).astype(BF16)
+    key_grad = (by_rows(dot_nn, queries, dscores) * scale).astype(BF16)
+    value_grad = by_rows(dot_nn, attended_grad, probs_low).astype(BF16)
+    grads = jnp.concatenate([query_grad, key_grad, value_grad], axis=0)
+    normed_grad = by_rows(dot_nn, turned, grads)
     normed_grad = in_order(normed_grad, core)
     for k, gradient in enumerate((query_grad, key_grad, value_grad)):
         grads_ref[k, :, :] = gradient
-    attended = dot_nt(vals, probs_low).astype(BF16)
+    attended = by_rows(dot_nt, vals, probs_low).astype(BF16)
     halves_ref[0] = attended[:HALF]
     halves_ref[1] = attended[HALF:]
-    product = dot_nn(out_matrix, own_first(halves_ref, core))
+    product = by_rows(dot_nn, out_matrix, own_first(halves_ref, core))
     outputs = residual + product + column(params, OUT_BIAS)
     outputs_ref[...] = image_rows(outputs)
     branch, gain_grad, bias_grad = norm_back(hat, inverse, normed_grad, column(params, GAINS + 2))
@@ -400,7 +403,7 @@
 IN_CUT_ROWS = IN_CUT * ROWS
 
 
-def local_call(kernel, core, *operands, out):
+def local_call(kernel, core, *operands, out, scratch=()):
     in_specs = [pl.BlockSpec(memory_space=pltpu.VMEM) for _ in operands]
     if core is not None:
         in_specs = [pl.BlockSpec(memory_space=pltpu.SMEM)] + in_specs
@@ -411,6 +414,7 @@
         out_shape=shapes,
         in_specs=in_specs,
         out_specs=tuple(pl.BlockSpec(memory_space=pltpu.VMEM) for _ in out),
+        scratch_shapes=[pltpu.VMEM(shape, dtype) for shape, dtype in scratch],
         compiler_params=pltpu.CompilerParams(vmem_limit_bytes=VMEM_LIMIT),
     )(*operands)
 
@@ -444,6 +448,7 @@
             matrices(WBLOCKS - IN_CUT), rows, image, table, halves, halves, ((3, C, POS), BF16),
             ((5 * C, POS), BF16),
         ),
+        scratch=(((C, 3 * C), BF16),),
     )
     theirs = swap(swapping)
     residual_grad, their_shifts = lax.optimization_barrier((residual_grad, their_shifts))
@@ -607,7 +612,25 @@
     rates = jnp.exp(-math.log(10000.0) * index / (half_dim - 1))
     for image in range(SHARDS):
         angles[image : image + 1, :] = rates * steps_ref[image].astype(F32)
-    features = jnp.concatenate([jnp.sin(angles[...]), jnp.cos(angles[...])], axis=1)
+    angle = angles[...]
+    turns = jnp.floor(angle * (2.0 / math.pi) + 0.5)
+    rest = angle - turns * 1.5703125
+    rest = rest - turns * 4.837512969970703125e-4
+    rest = rest - turns * 7.549789954891882e-8
+    square = rest * rest
+    sine = rest + rest * square * (
+        -1.6666654611e-1 + square * (8.3321608736e-3 + square * -1.9515295891e-4)
+    )
+    cosine = 1.0 - 0.5 * square + square * square * (
+        4.166664568298827e-2 + square * (-1.388731625493765e-3 + square * 2.443315711809948e-5)
+    )
+    quarter = turns.astype(jnp.int32) & 3
+    odd = (quarter & 1) == 1
+    sines = jnp.where(odd, cosine, sine)
+    cosines = jnp.where(odd, sine, cosine)
+    sines = jnp.where(quarter >= 2, -sines, sines)
+    cosines = jnp.where((quarter == 1) | (quarter == 2), -cosines, cosines)
+    features = jnp.concatenate([sines, cosines], axis=1)
     swished = features * sigmoid(features)
     swished_ref[...] = swished
     offsets = None

time: 89.2 us -> 89.1 us (level)
  no operation moved by 1% of the time
where the time goes in v7:
time: 89.1 us; the launch traced here: 88.9 us
  blocking collectives  66.1 us (74%)
  Pallas kernels  11.1 us (12%)
  starting transfers between devices  7.53 us (8%)
  waiting for transfers between devices  3.22 us (4%)
    all_to_all x1, blocking collectives, on_device(): lax.all_to_all(sent, 'ch', split_axis=0, concat_axis=0, tiled=True)  37 us
    all_to_all x1, blocking collectives, on_device(): back = lax.all_to_all(send, 'ch', split_axis=0, concat_axis=0, tiled=True)  29.1 us
    pallas_call x7, Pallas kernels, local_call(): pl.pallas_call(kernel, out_shape=shapes, in_specs=in_specs, out_specs=tup...  7.62 us
    ppermute x5, starting transfers between devices, on_device(): lax.ppermute(values, 'img', core_pairs)  3.77 us
    ppermute x1, starting transfers between devices, on_device(): theirs = lax.ppermute(sums, 'img', core_pairs)  2.93 us
  transfers between devices with their start and end apart: 7, of which 3 were waited for; matrix products, arithmetic and copies ran while one was open for 0% of the time, Pallas kernels for 9%

profile of v7, /device:TPU:1, one launch (start us, length us, event | category | flops | bytes accessed | tf_op | source)
XLA Modules:
  0.0 88.9 jit_solution(14454207082078772926)
XLA Ops:
  0.7 1.6 %shard_map.229 = (bf16[32,232,128]{2,1,0:T(8,128)(2,1)S(1)}, f32[32,512]{1,0:T(8,128)S(1)}) custom-call(s32[1]{0:T(128)} %bitcast.core_ref, s32[32]{0:T(128)} %refs_0_.1, f32[3,8]{1,0:T(4,128)} %refs_1_.1, f32[3,8]{1,0:T(4,128)} %refs_2_.1, f32[2,8]{1,0:T(2,128)} %refs_3_.1, f32[2,8]{1,0:T(2,128)} %refs_4_.1, f32[1,8]{1,0:T(1,128)} %bitcast.8, ...), custom_call_target="tpu_custom_call" | custom-call | tf_op jit(solution)/shard_map/pallas_call | solution.py:705
  2.3 37.0 %all_to_all.10.recv_ref = bf16[32,232,128]{2,1,0:T(8,128)(2,1)S(1)} all-to-all(bf16[32,232,128]{2,1,0:T(8,128)(2,1)S(1)} %get-tuple-element.52), channel_id=1, replica_groups=mesh['ch'=32,'img'=4] {'ch'}, dimensions={0} | all-to-all | bytes 3801088 | tf_op jit(solution)/shard_map/all_to_all | solution.py:757
  39.3 0.1 slice.9
  39.4 2.6 %collective-permute-start.1 = (bf16[32,96,128]{2,1,0:T(8,128)(2,1)S(1)}, bf16[32,96,128]{2,1,0:T(8,128)(2,1)S(1)}, u32[]{:S(2)}, u32[]{:S(2)}) collective-permute-start(bf16[32,96,128]{2,1,0:T(8,128)(2,1)S(1)} %slice.9), channel_id=1, source_target_pairs={{0,1},{1,0},{2,3},{3,2},{4,5},{5,4},{6,7},{7,6},{8,9},{9,8},{10,11... | collective-permute-start | bytes 2359304 | tf_op jit(solution)/shard_map/ppermute | solution.py:759
  42.0 0.1 collective-permute-start
  42.1 1.0 %shard_map.230 = (bf16[2,3,128,256]{3,2,1,0:T(8,128)(2,1)S(1)}, f32[256,256]{1,0:T(8,128)S(1)}, f32[256,128]{1,0:T(8,128)S(1)}, f32[256,128]{1,0:T(8,128)S(1)}, ...) custom-call(s32[1]{0:T(128)} %bitcast.core_ref, bf16[32,232,128]{2,1,0:T(8,128)(2,1)S(1)} %all_to_all.10.recv_ref), custom_call_target="tpu_custom_call" | custom-call | tf_op jit(solution)/shard_map/pallas_call | solution.py:412
  43.1 0.7 collective-permute-done.1.swapped
  43.8 0.9 shard_map.231
  44.7 0.5 collective-permute-start.2
  45.2 0.0 collective-permute-done.swapped
  45.2 2.4 %shard_map.232 = (bf16[10,256,128]{2,1,0:T(8,128)(2,1)S(1)}, bf16[32,16,128]{2,1,0:T(8,128)(2,1)S(1)}, f32[256,256]{1,0:T(8,128)S(1)}, f32[256,128]{1,0:T(8,128)...) custom-call(s32[1]{0:T(128)} %bitcast.core_ref, ...), custom_call_target="tpu_custom_call" | custom-call | tf_op jit(solution)/shard_map/pallas_call | solution.py:412
  47.5 0.2 collective-permute-start.4
  47.8 0.0 collective-permute-done.2.their_shifts
  47.8 0.9 %shard_map.233 = (bf16[256,256]{1,0:T(8,128)(2,1)S(1)}, f32[256,128]{1,0:T(8,128)S(1)}) custom-call(s32[1]{0:T(128)} %bitcast.core_ref, bf16[32,232,128]{2,1,0:T(8,128)(2,1)S(1)} %all_to_all.10.recv_ref, bf16[22,256,128]{2,1,0:T(8,128)(2,1)S(1)} %get-tuple-element.54.own, bf16[10,256,128]{2,1,0:T(8,128)(2,1)S(1)} %get-tuple-element.59.other, ...), custom_call_target="tpu_custom_call" | custom-call | tf_op jit(solution)/shard_map/pallas_call | solution.py:412
  48.7 0.4 collective-permute-start.3
  49.1 0.9 shard_map.235.tail
  50.0 0.0 collective-permute-done.4.theirs
  50.0 0.9 %shard_map.234.late = bf16[32,112,128]{2,1,0:T(8,128)(2,1)S(1)} custom-call(s32[1]{0:T(128)} %bitcast.core_ref, bf16[32,232,128]{2,1,0:T(8,128)(2,1)S(1)} %all_to_all.10.recv_ref, bf16[2,3,128,256]{3,2,1,0:T(8,128)(2,1)S(1)} %get-tuple-element.57.taps_two, bf16[2,128,256]{2,1,0:T(8,128)(2,1)S(1)} %get-tuple-element.68.normed, ...), custom_call_target="tpu_custom_call" | custom-call | tf_op jit(solution)/shard_map/pallas_call | solution.py:412
  51.0 0.0 collective-permute-done.3.their_low
  51.0 0.6 shard_map.236
  51.6 29.1 %all_to_all.11.back_ref = bf16[32,216,128]{2,1,0:T(8,128)(2,1)S(1)} all-to-all(bf16[32,216,128]{2,1,0:T(8,128)(2,1)S(1)} %shard_map.236), channel_id=1, replica_groups=mesh['ch'=32,'img'=4] {'ch'}, dimensions={0} | all-to-all | bytes 3538944 | tf_op jit(solution)/shard_map/all_to_all | solution.py:761
  80.7 0.3 shard_map.237
  81.0 0.8 collective-permute-start.5
  81.9 0.8 shard_map.238
  82.6 1.5 %collective-permute-done.5 = bf16[224,128]{1,0:T(8,128)(2,1)S(1)} collective-permute-done((bf16[224,128]{1,0:T(8,128)(2,1)S(1)}, bf16[224,128]{1,0:T(8,128)(2,1)S(1)}, u32[]{:S(2)}, u32[]{:S(2)}) %collective-permute-start.5) | collective-permute-done | bytes 57376 | tf_op jit(solution)/shard_map/ppermute | solution.py:764
  84.2 2.9 %collective-permute-start.6 = (f32[224,128]{1,0:T(8,128)S(1)}, f32[224,128]{1,0:T(8,128)S(1)}, u32[]{:S(2)}, u32[]{:S(2)}) collective-permute-start(f32[224,128]{1,0:T(8,128)S(1)} %convert_add_fusion.mine_ref), channel_id=1, source_target_pairs={{0,1},{1,0},{2,3},{3,2},{4,5},{5,4},{6,7},{7,6},{8,9},{9,8},{10,11... | collective-permute-start | bytes 344072 | tf_op jit(solution)/shard_map/ppermute | solution.py:768
  87.1 1.0 %collective-permute-done.6.theirs_ref = f32[224,128]{1,0:T(8,128)S(1)} collective-permute-done((f32[224,128]{1,0:T(8,128)S(1)}, f32[224,128]{1,0:T(8,128)S(1)}, u32[]{:S(2)}, u32[]{:S(2)}) %collective-permute-start.6) | collective-permute-done | bytes 114720 | tf_op jit(solution)/shard_map/ppermute | solution.py:768
  88.1 0.8 shard_map.239
  (2 shorter events, 0.1 us)
Async XLA Ops:
  39.4 4.5 %collective-permute-start.1 = (bf16[32,96,128]{2,1,0:T(8,128)(2,1)S(1)}, bf16[32,96,128]{2,1,0:T(8,128)(2,1)S(1)}, u32[]{:S(2)}, u32[]{:S(2)}) collective-permute-start(bf16[32,96,128]{2,1,0:T(8,128)(2,1)S(1)} %slice.9), channel_id=1, source_target_pairs={{0,1},{1,0},{2,3},{3,2},{4,5},{5,4},{6,7},{7,6},{8,9},{9,8},{10,11... | collective-permute-start | bytes 2359304 | tf_op jit(solution)/shard_map/ppermute | solution.py:759
  42.0 3.2 %collective-permute-start = (bf16[32,80,128]{2,1,0:T(8,128)(2,1)S(1)}, bf16[32,80,128]{2,1,0:T(8,128)(2,1)S(1)}, u32[]{:S(2)}, u32[]{:S(2)}) collective-permute-start(bf16[32,80,128]{2,1,0:T(8,128)(2,1)S(1)} %slice.8), channel_id=1, source_target_pairs={{0,1},{1,0},{2,3},{3,2},{4,5},{5,4},{6,7},{7,6},{8,9},{9,8},{10,11... | collective-permute-start | bytes 1966088 | tf_op jit(solution)/shard_map/ppermute | solution.py:759
  44.7 3.1 %collective-permute-start.2 = (bf16[1024,256]{1,0:T(8,128)(2,1)S(1)}, bf16[1024,256]{1,0:T(8,128)(2,1)S(1)}, u32[]{:S(2)}, u32[]{:S(2)}) collective-permute-start(bf16[1024,256]{1,0:T(8,128)(2,1)S(1)} %get-tuple-element.63), channel_id=1, source_target_pairs={{0,1},{1,0},{2,3},{3,2},{4,5},{5,4},{6,7},{7,6},{8,9},{9,8},{10,11... | collective-permute-start | bytes 1572872 | tf_op jit(solution)/shard_map/ppermute | solution.py:759
  47.5 2.5 %collective-permute-start.4 = (bf16[1280,256]{1,0:T(8,128)(2,1)S(1)}, bf16[1280,256]{1,0:T(8,128)(2,1)S(1)}, u32[]{:S(2)}, u32[]{:S(2)}) collective-permute-start(bf16[1280,256]{1,0:T(8,128)(2,1)S(1)} %get-tuple-element.71), channel_id=1, source_target_pairs={{0,1},{1,0},{2,3},{3,2},{4,5},{5,4},{6,7},{7,6},{8,9},{9,8},{10,11... | collective-permute-start | bytes 1966088 | tf_op jit(solution)/shard_map/ppermute | solution.py:759
  48.7 2.3 %collective-permute-start.3 = (bf16[256,256]{1,0:T(8,128)(2,1)S(1)}, bf16[256,256]{1,0:T(8,128)(2,1)S(1)}, u32[]{:S(2)}, u32[]{:S(2)}) collective-permute-start(bf16[256,256]{1,0:T(8,128)(2,1)S(1)} %get-tuple-element.66.low_ref), channel_id=1, source_target_pairs={{0,1},{1,0},{2,3},{3,2},{4,5},{5,4},{6,7},{7,6},{8,9},{9,8},{10,11... | collective-permute-start | bytes 393224 | tf_op jit(solution)/shard_map/ppermute | solution.py:759
  81.0 3.1 %collective-permute-start.5 = (bf16[224,128]{1,0:T(8,128)(2,1)S(1)}, bf16[224,128]{1,0:T(8,128)(2,1)S(1)}, u32[]{:S(2)}, u32[]{:S(2)}) collective-permute-start(bf16[224,128]{1,0:T(8,128)(2,1)S(1)} %shard_map.237), channel_id=1, source_target_pairs={{0,2},{1,3},{2,0},{3,1},{4,6},{5,7},{6,4},{7,5},{8,10},{9,11},{10,... | collective-permute-start | bytes 172040 | tf_op jit(solution)/shard_map/ppermute | solution.py:764
  84.2 3.9 %collective-permute-start.6 = (f32[224,128]{1,0:T(8,128)S(1)}, f32[224,128]{1,0:T(8,128)S(1)}, u32[]{:S(2)}, u32[]{:S(2)}) collective-permute-start(f32[224,128]{1,0:T(8,128)S(1)} %convert_add_fusion.mine_ref), channel_id=1, source_target_pairs={{0,1},{1,0},{2,3},{3,2},{4,5},{5,4},{6,7},{7,6},{8,9},{9,8},{10,11... | collective-permute-start | bytes 344072 | tf_op jit(solution)/shard_map/ppermute | solution.py:768

commit v8 on v7

--- a/solution.py
+++ b/solution.py
@@ -92,12 +92,12 @@
     return jnp.concatenate([edge, moved[:, HALF:]], axis=1)
 
 
-def store_matrices(ref, first_row, target):
-    for pair in range(target.shape[0] // 2):
-        rows = ref[:, first_row + 16 * pair : first_row + 16 * pair + 16, :].astype(F32)
+def store_matrices(ref, target, first, count):
+    for pair in range(count // 2):
+        rows = ref[:, 16 * pair : 16 * pair + 16, :].astype(F32)
         for part in range(2):
             cut = rows[:, ROWS * part : ROWS * part + ROWS, :]
-            target[2 * pair + part, :, :] = cut.reshape(C, HALF).astype(BF16)
+            target[first + 2 * pair + part, :, :] = cut.reshape(C, HALF).astype(BF16)
 
 
 def matrix(own, other, block, first_other):
@@ -157,7 +157,7 @@
 
 
 def convolve_back(matrices, low, core):
-    turned = low.astype(F32).T.astype(BF16)
+    turned = low.T
     edge = jnp.zeros((SIDE, C), BF16)
     stacked = jnp.concatenate(
         [
@@ -232,7 +232,7 @@
     stats_ref[...] = jnp.broadcast_to(inverse, (C, HALF))
     pre = hat * columns[:, GAINS : GAINS + 1] + columns[:, BIASES : BIASES + 1]
     store_shifts(taps_ref, (pre * sigmoid(pre)).astype(BF16).astype(F32))
-    store_matrices(recv_ref, 0, own_ref)
+    store_matrices(recv_ref, own_ref, 0, WBLOCKS)
     partial_ref[...] = half_convolve([own_ref[tap] for tap in range(9)], taps_ref[core_ref[0]])
 
 
@@ -240,7 +240,7 @@
     core_ref, recv_ref, swapped, taps_one, params, partial,
     other, taps_ref, hat_ref, stats_ref, halves_ref,
 ):
-    store_matrices(swapped, 0, other)
+    store_matrices(swapped, other, 0, IN_CUT)
     rest = half_convolve([other[tap] for tap in range(9)], taps_one[1 - core_ref[0]])
     middle = partial[...] + rest
     middle = middle + (column(params, CONV_BIAS) + column(params, OFFSETS))
@@ -257,15 +257,17 @@
 
 
 def attention_kernel(
-    core_ref, recv_ref, swapped, taps_two, params, own, other_one,
+    core_ref, recv_ref, swapped_two, swapped_three, taps_two, params, own, other_one,
     other, outputs_ref, grad_ref, sums_ref, normed_ref, halves_ref, grads_ref, swap_ref, turned,
 ):
     core = core_ref[0]
-    store_matrices(swapped, 0, other)
+    half = (WBLOCKS - IN_CUT) // 2
+    store_matrices(swapped_two, other, 0, half)
+    store_matrices(swapped_three, other, half, half)
     out_matrix = matrix(own, other_one, OUT_BLOCK, 0)
     qkv = [
-        matrix(own, other_one, QUERY_BLOCK, 0),
-        matrix(own, other_one, KEY_BLOCK, 0),
+        matrix(own, other, QUERY_BLOCK, IN_CUT),
+        matrix(own, other, KEY_BLOCK, IN_CUT),
         matrix(own, other, VALUE_BLOCK, IN_CUT),
     ]
     for k in range(3):
@@ -387,10 +389,10 @@
     first = conv_weight_grads(
         [low_ref[...], their_low[...]], [taps_one[core_ref[0]], their_shifts[0 : 3 * HALF, :]]
     )
-    cut = WROWS - IN_CUT_ROWS + 16
+    cut = WROWS - IN_CUT_ROWS
     out = late[:, cut : cut + 16, :].astype(F32)[:, :ROWS, :]
     store_blocks(send_ref, first + [out])
-    send_ref[:, IN_CUT_ROWS - 16 : WROWS, :] = late[:, :cut, :]
+    send_ref[:, IN_CUT_ROWS:WROWS, :] = late[:, :cut, :]
     send_ref[:, WROWS : WROWS + 16, :] = outputs[...]
     send_ref[:, WROWS + 16 : WROWS + 40, :] = tail[:, :24, :]
 
@@ -399,7 +401,7 @@
 IN_ROWS = WROWS + 56
 OUT_ROWS = WROWS + 40
 OUT_BLOCK, QUERY_BLOCK, KEY_BLOCK, SECOND_CONV, VALUE_BLOCK = 9, 10, 11, 12, 21
-IN_CUT = 12
+IN_CUT = 10
 IN_CUT_ROWS = IN_CUT * ROWS
 
 
@@ -424,7 +426,9 @@
 
 def run_block(core, received, swap):
     swapped_one = swap(received[:, :IN_CUT_ROWS])
-    swapped_two = swap(received[:, IN_CUT_ROWS:WROWS])
+    middle_row = (IN_CUT_ROWS + WROWS) // 2
+    swapped_two = swap(received[:, IN_CUT_ROWS:middle_row])
+    swapped_three = swap(received[:, middle_row:WROWS])
     image, table = ((C, POS), F32), ((C, HALF), F32)
     taps, low = ((2, 3, HALF, POS), BF16), ((C, POS), BF16)
     halves = ((2, HALF, POS), BF16)
@@ -443,7 +447,8 @@
     rows = ((SHARDS, 16, HALF), BF16)
     their_shifts = swap(halves_out)
     other_two, outputs, residual_grad, sums, normed, attended, gradients, swapping = local_call(
-        attention_kernel, core, received, swapped_two, taps_two, params, own_weights, other_weights,
+        attention_kernel, core, received, swapped_two, swapped_three, taps_two, params, own_weights,
+        other_weights,
         out=(
             matrices(WBLOCKS - IN_CUT), rows, image, table, halves, halves, ((3, C, POS), BF16),
             ((5 * C, POS), BF16),
@@ -463,7 +468,7 @@
     )
     (late,) = local_call(
         second_grads_kernel, core, received, taps_two, normed, attended, gradients, residual_grad,
-        their_shifts, theirs, out=(((SHARDS, WROWS - IN_CUT_ROWS + 32, HALF), BF16),),
+        their_shifts, theirs, out=(((SHARDS, WROWS - IN_CUT_ROWS + 16, HALF), BF16),),
     )
     (send,) = local_call(
         gather_kernel, core, taps_one, low_one, their_shifts, their_low, late, outputs, tail,

time: 89.1 us -> 88.8 us (level)
    ppermute x5 -> x6, starting transfers between devices: 3.77 us -> 4.27 us  [on_device(): lax.ppermute(values, 'img', core_pairs)]
  transfers between devices with their start and end apart: 7 -> 8, of which waited for: 3 -> 3; matrix products, arithmetic and copies ran while one was open for 0% -> 0% of each run, Pallas kernels for 9% -> 9%
where the time goes in v8:
time: 88.8 us; the launch traced here: 88.6 us
  blocking collectives  66.1 us (74%)
  Pallas kernels  11.1 us (12%)
  starting transfers between devices  8.04 us (9%)
  waiting for transfers between devices  2.55 us (3%)
    all_to_all x1, blocking collectives, on_device(): lax.all_to_all(sent, 'ch', split_axis=0, concat_axis=0, tiled=True)  37 us
    all_to_all x1, blocking collectives, on_device(): back = lax.all_to_all(send, 'ch', split_axis=0, concat_axis=0, tiled=True)  29.1 us
    pallas_call x7, Pallas kernels, local_call(): pl.pallas_call(kernel, out_shape=shapes, in_specs=in_specs, out_specs=tup...  7.55 us
    ppermute x6, starting transfers between devices, on_device(): lax.ppermute(values, 'img', core_pairs)  4.27 us
    ppermute x1, starting transfers between devices, on_device(): theirs = lax.ppermute(sums, 'img', core_pairs)  2.96 us
  transfers between devices with their start and end apart: 8, of which 3 were waited for; matrix products, arithmetic and copies ran while one was open for 0% of the time, Pallas kernels for 9%

profile of v8, /device:TPU:1, one launch (start us, length us, event | category | flops | bytes accessed | tf_op | source)
XLA Modules:
  0.0 88.6 jit_solution(16307050291211417073)
XLA Ops:
  0.7 1.6 %shard_map.229 = (bf16[32,232,128]{2,1,0:T(8,128)(2,1)S(1)}, f32[32,512]{1,0:T(8,128)S(1)}) custom-call(s32[1]{0:T(128)} %bitcast.core_ref, s32[32]{0:T(128)} %refs_0_.1, f32[3,8]{1,0:T(4,128)} %refs_1_.1, f32[3,8]{1,0:T(4,128)} %refs_2_.1, f32[2,8]{1,0:T(2,128)} %refs_3_.1, f32[2,8]{1,0:T(2,128)} %refs_4_.1, f32[1,8]{1,0:T(1,128)} %bitcast.8, ...), custom_call_target="tpu_custom_call" | custom-call | tf_op jit(solution)/shard_map/pallas_call | solution.py:710
  2.3 37.0 %all_to_all.10.recv_ref = bf16[32,232,128]{2,1,0:T(8,128)(2,1)S(1)} all-to-all(bf16[32,232,128]{2,1,0:T(8,128)(2,1)S(1)} %get-tuple-element.52), channel_id=1, replica_groups=mesh['ch'=32,'img'=4] {'ch'}, dimensions={0} | all-to-all | bytes 3801088 | tf_op jit(solution)/shard_map/all_to_all | solution.py:762
  39.3 2.6 %collective-permute-start.2 = (bf16[32,80,128]{2,1,0:T(8,128)(2,1)S(1)}, bf16[32,80,128]{2,1,0:T(8,128)(2,1)S(1)}, u32[]{:S(2)}, u32[]{:S(2)}) collective-permute-start(bf16[32,80,128]{2,1,0:T(8,128)(2,1)S(1)} %slice.14), channel_id=1, source_target_pairs={{0,1},{1,0},{2,3},{3,2},{4,5},{5,4},{6,7},{7,6},{8,9},{9,8},{10,11... | collective-permute-start | bytes 1966088 | tf_op jit(solution)/shard_map/ppermute | solution.py:764
  41.9 0.1 fusion
  42.0 0.1 collective-permute-start.1
  42.1 0.5 collective-permute-start
  42.6 1.0 %shard_map.230 = (bf16[2,3,128,256]{3,2,1,0:T(8,128)(2,1)S(1)}, f32[256,256]{1,0:T(8,128)S(1)}, f32[256,128]{1,0:T(8,128)S(1)}, f32[256,128]{1,0:T(8,128)S(1)}, ...) custom-call(s32[1]{0:T(128)} %bitcast.core_ref, bf16[32,232,128]{2,1,0:T(8,128)(2,1)S(1)} %all_to_all.10.recv_ref), custom_call_target="tpu_custom_call" | custom-call | tf_op jit(solution)/shard_map/pallas_call | solution.py:414
  43.6 0.1 collective-permute-done.2.swapped
  43.6 0.8 shard_map.231
  44.5 0.5 collective-permute-start.3
  44.9 0.0 collective-permute-done.1.swapped_three
  44.9 0.0 collective-permute-done.swapped_two
  44.9 2.4 %shard_map.232 = (bf16[12,256,128]{2,1,0:T(8,128)(2,1)S(1)}, bf16[32,16,128]{2,1,0:T(8,128)(2,1)S(1)}, f32[256,256]{1,0:T(8,128)S(1)}, f32[256,128]{1,0:T(8,128)...) custom-call(s32[1]{0:T(128)} %bitcast.core_ref, ...), custom_call_target="tpu_custom_call" | custom-call | tf_op jit(solution)/shard_map/pallas_call | solution.py:414
  47.3 0.3 collective-permute-start.5
  47.6 0.0 collective-permute-done.3.their_shifts
  47.6 0.9 %shard_map.233 = (bf16[256,256]{1,0:T(8,128)(2,1)S(1)}, f32[256,128]{1,0:T(8,128)S(1)}) custom-call(s32[1]{0:T(128)} %bitcast.core_ref, bf16[32,232,128]{2,1,0:T(8,128)(2,1)S(1)} %all_to_all.10.recv_ref, bf16[22,256,128]{2,1,0:T(8,128)(2,1)S(1)} %get-tuple-element.54.own, bf16[12,256,128]{2,1,0:T(8,128)(2,1)S(1)} %get-tuple-element.59.other, ...), custom_call_target="tpu_custom_call" | custom-call | tf_op jit(solution)/shard_map/pallas_call | solution.py:414
  48.5 0.4 collective-permute-start.4
  48.9 0.9 shard_map.235.tail
  49.8 0.0 collective-permute-done.5.theirs
  49.8 0.9 %shard_map.234.late = bf16[32,112,128]{2,1,0:T(8,128)(2,1)S(1)} custom-call(s32[1]{0:T(128)} %bitcast.core_ref, bf16[32,232,128]{2,1,0:T(8,128)(2,1)S(1)} %all_to_all.10.recv_ref, bf16[2,3,128,256]{3,2,1,0:T(8,128)(2,1)S(1)} %get-tuple-element.57.taps_two, bf16[2,128,256]{2,1,0:T(8,128)(2,1)S(1)} %get-tuple-element.68.normed, ...), custom_call_target="tpu_custom_call" | custom-call | tf_op jit(solution)/shard_map/pallas_call | solution.py:414
  50.7 0.0 collective-permute-done.4.their_low
  50.7 0.6 shard_map.236
  51.4 29.1 %all_to_all.11.back_ref = bf16[32,216,128]{2,1,0:T(8,128)(2,1)S(1)} all-to-all(bf16[32,216,128]{2,1,0:T(8,128)(2,1)S(1)} %shard_map.236), channel_id=1, replica_groups=mesh['ch'=32,'img'=4] {'ch'}, dimensions={0} | all-to-all | bytes 3538944 | tf_op jit(solution)/shard_map/all_to_all | solution.py:766
  80.4 0.3 shard_map.237
  80.8 0.8 collective-permute-start.6
  81.6 0.8 shard_map.238
  82.3 1.5 %collective-permute-done.6 = bf16[224,128]{1,0:T(8,128)(2,1)S(1)} collective-permute-done((bf16[224,128]{1,0:T(8,128)(2,1)S(1)}, bf16[224,128]{1,0:T(8,128)(2,1)S(1)}, u32[]{:S(2)}, u32[]{:S(2)}) %collective-permute-start.6) | collective-permute-done | bytes 57376 | tf_op jit(solution)/shard_map/ppermute | solution.py:769
  83.9 3.0 %collective-permute-start.7 = (f32[224,128]{1,0:T(8,128)S(1)}, f32[224,128]{1,0:T(8,128)S(1)}, u32[]{:S(2)}, u32[]{:S(2)}) collective-permute-start(f32[224,128]{1,0:T(8,128)S(1)} %convert_add_fusion.mine_ref), channel_id=1, source_target_pairs={{0,1},{1,0},{2,3},{3,2},{4,5},{5,4},{6,7},{7,6},{8,9},{9,8},{10,11... | collective-permute-start | bytes 344072 | tf_op jit(solution)/shard_map/ppermute | solution.py:773
  86.8 1.0 %collective-permute-done.7.theirs_ref = f32[224,128]{1,0:T(8,128)S(1)} collective-permute-done((f32[224,128]{1,0:T(8,128)S(1)}, f32[224,128]{1,0:T(8,128)S(1)}, u32[]{:S(2)}, u32[]{:S(2)}) %collective-permute-start.7) | collective-permute-done | bytes 114720 | tf_op jit(solution)/shard_map/ppermute | solution.py:773
  87.8 0.8 shard_map.239
  (2 shorter events, 0.1 us)
Async XLA Ops:
  39.3 4.3 %collective-permute-start.2 = (bf16[32,80,128]{2,1,0:T(8,128)(2,1)S(1)}, bf16[32,80,128]{2,1,0:T(8,128)(2,1)S(1)}, u32[]{:S(2)}, u32[]{:S(2)}) collective-permute-start(bf16[32,80,128]{2,1,0:T(8,128)(2,1)S(1)} %slice.14), channel_id=1, source_target_pairs={{0,1},{1,0},{2,3},{3,2},{4,5},{5,4},{6,7},{7,6},{8,9},{9,8},{10,11... | collective-permute-start | bytes 1966088 | tf_op jit(solution)/shard_map/ppermute | solution.py:764
  42.0 3.0 %collective-permute-start.1 = (bf16[32,48,128]{2,1,0:T(8,128)(2,1)S(1)}, bf16[32,48,128]{2,1,0:T(8,128)(2,1)S(1)}, u32[]{:S(2)}, u32[]{:S(2)}) collective-permute-start(bf16[32,48,128]{2,1,0:T(8,128)(2,1)S(1)} %get-tuple-element.92), channel_id=1, source_target_pairs={{0,1},{1,0},{2,3},{3,2},{4,5},{5,4},{6,7},{7,6},{8,9},{9,8},{10,11... | collective-permute-start | bytes 1179656 | tf_op jit(solution)/shard_map/ppermute | solution.py:764
  42.1 2.9 %collective-permute-start = (bf16[32,48,128]{2,1,0:T(8,128)(2,1)S(1)}, bf16[32,48,128]{2,1,0:T(8,128)(2,1)S(1)}, u32[]{:S(2)}, u32[]{:S(2)}) collective-permute-start(bf16[32,48,128]{2,1,0:T(8,128)(2,1)S(1)} %get-tuple-element.93), channel_id=1, source_target_pairs={{0,1},{1,0},{2,3},{3,2},{4,5},{5,4},{6,7},{7,6},{8,9},{9,8},{10,11... | collective-permute-start | bytes 1179656 | tf_op jit(solution)/shard_map/ppermute | solution.py:764
  44.5 3.1 %collective-permute-start.3 = (bf16[1024,256]{1,0:T(8,128)(2,1)S(1)}, bf16[1024,256]{1,0:T(8,128)(2,1)S(1)}, u32[]{:S(2)}, u32[]{:S(2)}) collective-permute-start(bf16[1024,256]{1,0:T(8,128)(2,1)S(1)} %get-tuple-element.63), channel_id=1, source_target_pairs={{0,1},{1,0},{2,3},{3,2},{4,5},{5,4},{6,7},{7,6},{8,9},{9,8},{10,11... | collective-permute-start | bytes 1572872 | tf_op jit(solution)/shard_map/ppermute | solution.py:764
  47.3 2.5 %collective-permute-start.5 = (bf16[1280,256]{1,0:T(8,128)(2,1)S(1)}, bf16[1280,256]{1,0:T(8,128)(2,1)S(1)}, u32[]{:S(2)}, u32[]{:S(2)}) collective-permute-start(bf16[1280,256]{1,0:T(8,128)(2,1)S(1)} %get-tuple-element.71), channel_id=1, source_target_pairs={{0,1},{1,0},{2,3},{3,2},{4,5},{5,4},{6,7},{7,6},{8,9},{9,8},{10,11... | collective-permute-start | bytes 1966088 | tf_op jit(solution)/shard_map/ppermute | solution.py:764
  48.5 2.2 %collective-permute-start.4 = (bf16[256,256]{1,0:T(8,128)(2,1)S(1)}, bf16[256,256]{1,0:T(8,128)(2,1)S(1)}, u32[]{:S(2)}, u32[]{:S(2)}) collective-permute-start(bf16[256,256]{1,0:T(8,128)(2,1)S(1)} %get-tuple-element.66.low_ref), channel_id=1, source_target_pairs={{0,1},{1,0},{2,3},{3,2},{4,5},{5,4},{6,7},{7,6},{8,9},{9,8},{10,11... | collective-permute-start | bytes 393224 | tf_op jit(solution)/shard_map/ppermute | solution.py:764
  80.8 3.1 %collective-permute-start.6 = (bf16[224,128]{1,0:T(8,128)(2,1)S(1)}, bf16[224,128]{1,0:T(8,128)(2,1)S(1)}, u32[]{:S(2)}, u32[]{:S(2)}) collective-permute-start(bf16[224,128]{1,0:T(8,128)(2,1)S(1)} %shard_map.237), channel_id=1, source_target_pairs={{0,2},{1,3},{2,0},{3,1},{4,6},{5,7},{6,4},{7,5},{8,10},{9,11},{10,... | collective-permute-start | bytes 172040 | tf_op jit(solution)/shard_map/ppermute | solution.py:769
  83.9 3.9 %collective-permute-start.7 = (f32[224,128]{1,0:T(8,128)S(1)}, f32[224,128]{1,0:T(8,128)S(1)}, u32[]{:S(2)}, u32[]{:S(2)}) collective-permute-start(f32[224,128]{1,0:T(8,128)S(1)} %convert_add_fusion.mine_ref), channel_id=1, source_target_pairs={{0,1},{1,0},{2,3},{3,2},{4,5},{5,4},{6,7},{7,6},{8,9},{9,8},{10,11... | collective-permute-start | bytes 344072 | tf_op jit(solution)/shard_map/ppermute | solution.py:773

commit v9 on v8

--- a/solution.py
+++ b/solution.py
@@ -17,6 +17,11 @@
 HALF = 128
 WBLOCKS = 22
 WROWS = WBLOCKS * ROWS
+ORDER = (
+    22, 13, 6, 20, 19, 23, 5, 14, 1, 24, 26, 10, 7, 21, 9, 28, 18, 2, 11, 3, 12, 4, 15,
+    25, 16, 31, 29, 30, 0, 17, 8, 27,
+)
+PLACE = tuple(ORDER.index(k) for k in range(SHARDS))
 NORM_EPS = 1e-06
 GROUP_SIZE = ROWS * POS
 F32 = jnp.float32
@@ -25,6 +30,10 @@
 OFFSETS, GAINS, BIASES, CONV_BIAS, QV_BIAS, OUT_BIAS, TEMB_BIAS = 0, 1, 4, 7, 9, 11, 12
 D_GAINS, D_BIASES, D_CONV_BIAS, D_QV_BIAS, D_OUT_BIAS = 0, 3, 6, 8, 10
 PART = 16
+
+
+def arranged(values, order):
+    return jnp.concatenate([values[k : k + 1] for k in order], axis=0)
 
 
 def dot_nn(a, b):
@@ -94,7 +103,7 @@
 
 def store_matrices(ref, target, first, count):
     for pair in range(count // 2):
-        rows = ref[:, 16 * pair : 16 * pair + 16, :].astype(F32)
+        rows = arranged(ref[:, 16 * pair : 16 * pair + 16, :].astype(F32), PLACE)
         for part in range(2):
             cut = rows[:, ROWS * part : ROWS * part + ROWS, :]
             target[first + 2 * pair + part, :, :] = cut.reshape(C, HALF).astype(BF16)
@@ -118,7 +127,7 @@
 
 
 def load_image(ref, at):
-    block = ref[:, at : at + 16, :].astype(F32)
+    block = arranged(ref[:, at : at + 16, :].astype(F32), PLACE)
     left = block[:, 0:ROWS, :].reshape(C, HALF)
     right = block[:, ROWS : 2 * ROWS, :].reshape(C, HALF)
     return jnp.concatenate([left, right], axis=1)
@@ -189,10 +198,10 @@
     return lane_blocks(dot_nt(jnp.concatenate(lows, axis=1), jnp.concatenate(rows, axis=0)))
 
 
-def store_blocks(target, blocks):
+def store_blocks(target, blocks, order=range(SHARDS)):
     for pair in range(len(blocks) // 2):
         rows = jnp.concatenate(blocks[2 * pair : 2 * pair + 2], axis=1)
-        target[:, 16 * pair : 16 * pair + 16, :] = rows.astype(BF16)
+        target[:, 16 * pair : 16 * pair + 16, :] = arranged(rows, order).astype(BF16)
 
 
 def columns_of(listed, table):
@@ -220,7 +229,8 @@
 
 
 def first_kernel(core_ref, recv_ref, taps_ref, hat_ref, params_ref, stats_ref, own_ref, partial_ref):
-    columns = recv_ref[:, AT_PARAMS : AT_PARAMS + ROWS, :].astype(F32).reshape(C, HALF)
+    columns = recv_ref[:, AT_PARAMS : AT_PARAMS + ROWS, :].astype(F32)
+    columns = arranged(columns, PLACE).reshape(C, HALF)
     columns = (
         columns
         + pltpu.roll(columns, HALF - PART, 1)
@@ -391,10 +401,10 @@
     )
     cut = WROWS - IN_CUT_ROWS
     out = late[:, cut : cut + 16, :].astype(F32)[:, :ROWS, :]
-    store_blocks(send_ref, first + [out])
-    send_ref[:, IN_CUT_ROWS:WROWS, :] = late[:, :cut, :]
-    send_ref[:, WROWS : WROWS + 16, :] = outputs[...]
-    send_ref[:, WROWS + 16 : WROWS + 40, :] = tail[:, :24, :]
+    store_blocks(send_ref, first + [out], ORDER)
+    send_ref[:, IN_CUT_ROWS:WROWS, :] = arranged(late[:, :cut, :], ORDER)
+    send_ref[:, WROWS : WROWS + 16, :] = arranged(outputs[...], ORDER)
+    send_ref[:, WROWS + 16 : WROWS + 40, :] = arranged(tail[:, :24, :], ORDER)
 
 
 AT_SOURCE, AT_KEEP, AT_COTANGENT, AT_PARAMS = WROWS, WROWS + 16, WROWS + 32, WROWS + 48
@@ -491,7 +501,8 @@
         values = small[image] + pltpu.roll(small[image], HALF - PART, 1)
         table = table + values
         offsets_grad = values[:, D_CONV_BIAS : D_CONV_BIAS + 1]
-        temb = temb + offsets_grad * swished_ref[image : image + 1, :]
+        owner = ORDER[image]
+        temb = temb + offsets_grad * swished_ref[owner : owner + 1, :]
     lane = lax.broadcasted_iota(jnp.int32, (ROWS, HALF), 1)
     high = table.astype(BF16).astype(F32)
     low = pltpu.roll(table - high, PART, 1)
@@ -519,7 +530,7 @@
 
 def images_kernel(back_ref, outputs_ref, grad_ref):
     for at, target in ((WROWS, outputs_ref), (WROWS + 16, grad_ref)):
-        block = back_ref[:, at : at + 16, :].astype(F32)
+        block = arranged(back_ref[:, at : at + 16, :].astype(F32), PLACE)
         cut = jnp.concatenate([block[:, :ROWS, :], block[:, ROWS:, :]], axis=2)
         target[...] = jnp.swapaxes(cut, 0, 1).astype(BF16)
 
@@ -669,7 +680,7 @@
             high,
             jnp.where(lane < 2 * PART, mid, jnp.where(lane < 3 * PART, low, 0.0)),
         )
-        send_ref[image, WROWS + 48 : WROWS + 56, :] = parts.astype(BF16)
+        send_ref[PLACE[image], WROWS + 48 : WROWS + 56, :] = parts.astype(BF16)
 
     for copy in copies[8:]:
         copy.wait()
@@ -694,7 +705,7 @@
     def put(at, values):
         turned = jnp.swapaxes(values.astype(F32), 0, 1)
         cut = jnp.concatenate([turned[:, :, :HALF], turned[:, :, HALF:]], axis=1)
-        send_ref[:, at : at + 16, :] = cut.astype(BF16)
+        send_ref[:, at : at + 16, :] = arranged(cut, ORDER).astype(BF16)
 
     put(WROWS, inputs_ref[...])
     put(WROWS + 16, mask_ref[...])
@@ -720,6 +731,12 @@
         + [pltpu.VMEM((SHARDS, TEMB // 2), F32), pltpu.SemaphoreType.DMA((PREPARE_ARRAYS,))],
         compiler_params=pltpu.CompilerParams(vmem_limit_bytes=16 * 1024 * 1024),
     )(core, *[pltpu.with_memory_space_constraint(a, pltpu.HBM) for a in (timesteps, *arrays)])
+
+
+def exchange(values):
+    return lax.all_to_all(
+        values, "ch", split_axis=0, concat_axis=0, tiled=True, axis_index_groups=[list(ORDER)]
+    )
 
 
 def on_device(
@@ -759,11 +776,11 @@
         keep_mask,
         cotangent,
     )
-    received = lax.all_to_all(sent, "ch", split_axis=0, concat_axis=0, tiled=True)
+    received = exchange(sent)
     send = run_block(
         core.reshape(1), received, lambda values: lax.ppermute(values, "img", core_pairs)
     )
-    back = lax.all_to_all(send, "ch", split_axis=0, concat_axis=0, tiled=True)
+    back = exchange(send)
 
     sums = collect(back, swished)
     plane = lax.ppermute(sums, "img", plane_pairs)

time: 88.8 us -> 84.3 us (0.949)
  blocking collectives: 66.1 us -> 63.5 us
  starting transfers between devices: 8.04 us -> 6.14 us
    all_to_all x2, blocking collectives: 66.1 us -> 63.5 us  [exchange(): lax.all_to_all(values, 'ch', split_axis=0, concat_axis=0, tiled=True, axi...]
    ppermute x6, starting transfers between devices: 4.27 us -> 2.89 us  [on_device(): lax.ppermute(values, 'img', core_pairs)]
where the time goes in v9:
time: 84.3 us; the launch traced here: 84.1 us
  blocking collectives  63.5 us (75%)
  Pallas kernels  11.1 us (13%)
  starting transfers between devices  6.14 us (7%)
  waiting for transfers between devices  2.54 us (3%)
    all_to_all x2, blocking collectives, exchange(): lax.all_to_all(values, 'ch', split_axis=0, concat_axis=0, tiled=True, axi...  63.5 us
    pallas_call x7, Pallas kernels, local_call(): pl.pallas_call(kernel, out_shape=shapes, in_specs=in_specs, out_specs=tup...  7.55 us
    ppermute x6, starting transfers between devices, on_device(): lax.ppermute(values, 'img', core_pairs)  2.89 us
    ppermute x1, starting transfers between devices, on_device(): theirs = lax.ppermute(sums, 'img', core_pairs)  2.42 us
  transfers between devices with their start and end apart: 8, of which 3 were waited for; matrix products, arithmetic and copies ran while one was open for 0% of the time, Pallas kernels for 9%

profile of v9, /device:TPU:1, one launch (start us, length us, event | category | flops | bytes accessed | tf_op | source)
XLA Modules:
  0.0 84.1 jit_solution(11179700208338957838)
XLA Ops:
  0.7 1.6 %shard_map.229 = (bf16[32,232,128]{2,1,0:T(8,128)(2,1)S(1)}, f32[32,512]{1,0:T(8,128)S(1)}) custom-call(s32[1]{0:T(128)} %bitcast.core_ref, s32[32]{0:T(128)} %refs_0_.1, f32[3,8]{1,0:T(4,128)} %refs_1_.1, f32[3,8]{1,0:T(4,128)} %refs_2_.1, f32[2,8]{1,0:T(2,128)} %refs_3_.1, f32[2,8]{1,0:T(2,128)} %refs_4_.1, f32[1,8]{1,0:T(1,128)} %bitcast.8, ...), custom_call_target="tpu_custom_call" | custom-call | tf_op jit(solution)/shard_map/pallas_call | solution.py:721
  2.3 33.9 %all_to_all.10.recv_ref = bf16[32,232,128]{2,1,0:T(8,128)(2,1)S(1)} all-to-all(bf16[32,232,128]{2,1,0:T(8,128)(2,1)S(1)} %get-tuple-element.52), channel_id=1, replica_groups={{88,52,24,80,76,92,20,56,4,96,104,40,28,84,36,112,72,8,44,12,48,16,60,1..., dimensions={0} | all-to-all | bytes 3801088 | tf_op jit(solution)/shard_map/all_to_all | solution.py:737
  36.3 1.2 %collective-permute-start.2 = (bf16[32,80,128]{2,1,0:T(8,128)(2,1)S(1)}, bf16[32,80,128]{2,1,0:T(8,128)(2,1)S(1)}, u32[]{:S(2)}, u32[]{:S(2)}) collective-permute-start(bf16[32,80,128]{2,1,0:T(8,128)(2,1)S(1)} %slice.14), channel_id=1, source_target_pairs={{0,1},{1,0},{2,3},{3,2},{4,5},{5,4},{6,7},{7,6},{8,9},{9,8},{10,11... | collective-permute-start | bytes 1966088 | tf_op jit(solution)/shard_map/ppermute | solution.py:781
  37.5 0.1 fusion
  37.5 0.1 collective-permute-start.1
  37.6 0.5 collective-permute-start
  38.1 1.0 %shard_map.230 = (bf16[2,3,128,256]{3,2,1,0:T(8,128)(2,1)S(1)}, f32[256,256]{1,0:T(8,128)S(1)}, f32[256,128]{1,0:T(8,128)S(1)}, f32[256,128]{1,0:T(8,128)S(1)}, ...) custom-call(s32[1]{0:T(128)} %bitcast.core_ref, bf16[32,232,128]{2,1,0:T(8,128)(2,1)S(1)} %all_to_all.10.recv_ref), custom_call_target="tpu_custom_call" | custom-call | tf_op jit(solution)/shard_map/pallas_call | solution.py:424
  39.1 0.1 collective-permute-done.2.swapped
  39.2 0.8 %shard_map.231 = (bf16[10,256,128]{2,1,0:T(8,128)(2,1)S(1)}, bf16[2,3,128,256]{3,2,1,0:T(8,128)(2,1)S(1)}, f32[256,256]{1,0:T(8,128)S(1)}, f32[256,128]{1,0:T(8,128)S(1)}, bf16[1024,256]{1,0:T(8,128)(2,1)S(1)}) custom-call(s32[1]{0:T(128)} %bitcast.core_ref, bf16[32,232,128]{2,1,0:T(8,128)(2,1)S(1)} %all_to_all.10.recv_ref, ...), custom_call_target="tpu_custom_call" | custom-call | tf_op jit(solution)/shard_map/pallas_call | solution.py:424
  40.0 0.5 collective-permute-start.3
  40.5 0.0 collective-permute-done.1.swapped_three
  40.5 0.0 collective-permute-done.swapped_two
  40.5 2.4 %shard_map.232 = (bf16[12,256,128]{2,1,0:T(8,128)(2,1)S(1)}, bf16[32,16,128]{2,1,0:T(8,128)(2,1)S(1)}, f32[256,256]{1,0:T(8,128)S(1)}, f32[256,128]{1,0:T(8,128)...) custom-call(s32[1]{0:T(128)} %bitcast.core_ref, ...), custom_call_target="tpu_custom_call" | custom-call | tf_op jit(solution)/shard_map/pallas_call | solution.py:424
  42.9 0.3 collective-permute-start.5
  43.2 0.0 collective-permute-done.3.their_shifts
  43.2 0.9 %shard_map.233 = (bf16[256,256]{1,0:T(8,128)(2,1)S(1)}, f32[256,128]{1,0:T(8,128)S(1)}) custom-call(s32[1]{0:T(128)} %bitcast.core_ref, bf16[32,232,128]{2,1,0:T(8,128)(2,1)S(1)} %all_to_all.10.recv_ref, bf16[22,256,128]{2,1,0:T(8,128)(2,1)S(1)} %get-tuple-element.54.own, bf16[12,256,128]{2,1,0:T(8,128)(2,1)S(1)} %get-tuple-element.59.other, ...), custom_call_target="tpu_custom_call" | custom-call | tf_op jit(solution)/shard_map/pallas_call | solution.py:424
  44.1 0.4 collective-permute-start.4
  44.5 0.9 %shard_map.235.tail = bf16[32,32,128]{2,1,0:T(8,128)(2,1)S(1)} custom-call(s32[1]{0:T(128)} %bitcast.core_ref, bf16[22,256,128]{2,1,0:T(8,128)(2,1)S(1)} %get-tuple-element.54.own, bf16[10,256,128]{2,1,0:T(8,128)(2,1)S(1)} %get-tuple-element.58.other_one.other, f32[256,256]{1,0:T(8,128)S(1)} %get-tuple-element.73.hat_ref, ...), custom_call_target="tpu_custom_call" | custom-call | tf_op jit(solution)/shard_map/pallas_call | solution.py:424
  45.3 0.0 collective-permute-done.5.theirs
  45.4 0.9 %shard_map.234.late = bf16[32,112,128]{2,1,0:T(8,128)(2,1)S(1)} custom-call(s32[1]{0:T(128)} %bitcast.core_ref, bf16[32,232,128]{2,1,0:T(8,128)(2,1)S(1)} %all_to_all.10.recv_ref, bf16[2,3,128,256]{3,2,1,0:T(8,128)(2,1)S(1)} %get-tuple-element.57.taps_two, bf16[2,128,256]{2,1,0:T(8,128)(2,1)S(1)} %get-tuple-element.68.normed, ...), custom_call_target="tpu_custom_call" | custom-call | tf_op jit(solution)/shard_map/pallas_call | solution.py:424
  46.3 0.0 collective-permute-done.4.their_low
  46.3 0.6 shard_map.236
  46.9 29.5 %all_to_all.11.back_ref = bf16[32,216,128]{2,1,0:T(8,128)(2,1)S(1)} all-to-all(bf16[32,216,128]{2,1,0:T(8,128)(2,1)S(1)} %shard_map.236), channel_id=1, replica_groups={{88,52,24,80,76,92,20,56,4,96,104,40,28,84,36,112,72,8,44,12,48,16,60,1..., dimensions={0} | all-to-all | bytes 3538944 | tf_op jit(solution)/shard_map/all_to_all | solution.py:737
  76.5 0.3 shard_map.237
  76.8 0.8 collective-permute-start.6
  77.6 0.8 shard_map.238
  78.4 1.5 %collective-permute-done.6 = bf16[224,128]{1,0:T(8,128)(2,1)S(1)} collective-permute-done((bf16[224,128]{1,0:T(8,128)(2,1)S(1)}, bf16[224,128]{1,0:T(8,128)(2,1)S(1)}, u32[]{:S(2)}, u32[]{:S(2)}) %collective-permute-start.6) | collective-permute-done | bytes 57376 | tf_op jit(solution)/shard_map/ppermute | solution.py:786
  79.9 2.4 %collective-permute-start.7 = (f32[224,128]{1,0:T(8,128)S(1)}, f32[224,128]{1,0:T(8,128)S(1)}, u32[]{:S(2)}, u32[]{:S(2)}) collective-permute-start(f32[224,128]{1,0:T(8,128)S(1)} %convert_add_fusion.mine_ref), channel_id=1, source_target_pairs={{0,1},{1,0},{2,3},{3,2},{4,5},{5,4},{6,7},{7,6},{8,9},{9,8},{10,11... | collective-permute-start | bytes 344072 | tf_op jit(solution)/shard_map/ppermute | solution.py:790
  82.3 1.0 %collective-permute-done.7.theirs_ref = f32[224,128]{1,0:T(8,128)S(1)} collective-permute-done((f32[224,128]{1,0:T(8,128)S(1)}, f32[224,128]{1,0:T(8,128)S(1)}, u32[]{:S(2)}, u32[]{:S(2)}) %collective-permute-start.7) | collective-permute-done | bytes 114720 | tf_op jit(solution)/shard_map/ppermute | solution.py:790
  83.3 0.8 shard_map.239
  (2 shorter events, 0.1 us)
Async XLA Ops:
  36.3 2.9 %collective-permute-start.2 = (bf16[32,80,128]{2,1,0:T(8,128)(2,1)S(1)}, bf16[32,80,128]{2,1,0:T(8,128)(2,1)S(1)}, u32[]{:S(2)}, u32[]{:S(2)}) collective-permute-start(bf16[32,80,128]{2,1,0:T(8,128)(2,1)S(1)} %slice.14), channel_id=1, source_target_pairs={{0,1},{1,0},{2,3},{3,2},{4,5},{5,4},{6,7},{7,6},{8,9},{9,8},{10,11... | collective-permute-start | bytes 1966088 | tf_op jit(solution)/shard_map/ppermute | solution.py:781
  37.5 3.0 %collective-permute-start.1 = (bf16[32,48,128]{2,1,0:T(8,128)(2,1)S(1)}, bf16[32,48,128]{2,1,0:T(8,128)(2,1)S(1)}, u32[]{:S(2)}, u32[]{:S(2)}) collective-permute-start(bf16[32,48,128]{2,1,0:T(8,128)(2,1)S(1)} %get-tuple-element.92), channel_id=1, source_target_pairs={{0,1},{1,0},{2,3},{3,2},{4,5},{5,4},{6,7},{7,6},{8,9},{9,8},{10,11... | collective-permute-start | bytes 1179656 | tf_op jit(solution)/shard_map/ppermute | solution.py:781
  37.6 2.9 %collective-permute-start = (bf16[32,48,128]{2,1,0:T(8,128)(2,1)S(1)}, bf16[32,48,128]{2,1,0:T(8,128)(2,1)S(1)}, u32[]{:S(2)}, u32[]{:S(2)}) collective-permute-start(bf16[32,48,128]{2,1,0:T(8,128)(2,1)S(1)} %get-tuple-element.93), channel_id=1, source_target_pairs={{0,1},{1,0},{2,3},{3,2},{4,5},{5,4},{6,7},{7,6},{8,9},{9,8},{10,11... | collective-permute-start | bytes 1179656 | tf_op jit(solution)/shard_map/ppermute | solution.py:781
  40.0 3.1 %collective-permute-start.3 = (bf16[1024,256]{1,0:T(8,128)(2,1)S(1)}, bf16[1024,256]{1,0:T(8,128)(2,1)S(1)}, u32[]{:S(2)}, u32[]{:S(2)}) collective-permute-start(bf16[1024,256]{1,0:T(8,128)(2,1)S(1)} %get-tuple-element.63), channel_id=1, source_target_pairs={{0,1},{1,0},{2,3},{3,2},{4,5},{5,4},{6,7},{7,6},{8,9},{9,8},{10,11... | collective-permute-start | bytes 1572872 | tf_op jit(solution)/shard_map/ppermute | solution.py:781
  42.9 2.5 %collective-permute-start.5 = (bf16[1280,256]{1,0:T(8,128)(2,1)S(1)}, bf16[1280,256]{1,0:T(8,128)(2,1)S(1)}, u32[]{:S(2)}, u32[]{:S(2)}) collective-permute-start(bf16[1280,256]{1,0:T(8,128)(2,1)S(1)} %get-tuple-element.71), channel_id=1, source_target_pairs={{0,1},{1,0},{2,3},{3,2},{4,5},{5,4},{6,7},{7,6},{8,9},{9,8},{10,11... | collective-permute-start | bytes 1966088 | tf_op jit(solution)/shard_map/ppermute | solution.py:781
  44.1 2.2 %collective-permute-start.4 = (bf16[256,256]{1,0:T(8,128)(2,1)S(1)}, bf16[256,256]{1,0:T(8,128)(2,1)S(1)}, u32[]{:S(2)}, u32[]{:S(2)}) collective-permute-start(bf16[256,256]{1,0:T(8,128)(2,1)S(1)} %get-tuple-element.66.low_ref), channel_id=1, source_target_pairs={{0,1},{1,0},{2,3},{3,2},{4,5},{5,4},{6,7},{7,6},{8,9},{9,8},{10,11... | collective-permute-start | bytes 393224 | tf_op jit(solution)/shard_map/ppermute | solution.py:781
  76.8 3.1 %collective-permute-start.6 = (bf16[224,128]{1,0:T(8,128)(2,1)S(1)}, bf16[224,128]{1,0:T(8,128)(2,1)S(1)}, u32[]{:S(2)}, u32[]{:S(2)}) collective-permute-start(bf16[224,128]{1,0:T(8,128)(2,1)S(1)} %shard_map.237), channel_id=1, source_target_pairs={{0,2},{1,3},{2,0},{3,1},{4,6},{5,7},{6,4},{7,5},{8,10},{9,11},{10,... | collective-permute-start | bytes 172040 | tf_op jit(solution)/shard_map/ppermute | solution.py:786
  79.9 3.4 %collective-permute-start.7 = (f32[224,128]{1,0:T(8,128)S(1)}, f32[224,128]{1,0:T(8,128)S(1)}, u32[]{:S(2)}, u32[]{:S(2)}) collective-permute-start(f32[224,128]{1,0:T(8,128)S(1)} %convert_add_fusion.mine_ref), channel_id=1, source_target_pairs={{0,1},{1,0},{2,3},{3,2},{4,5},{5,4},{6,7},{7,6},{8,9},{9,8},{10,11... | collective-permute-start | bytes 344072 | tf_op jit(solution)/shard_map/ppermute | solution.py:790

commit v10 on v9

--- a/solution.py
+++ b/solution.py
@@ -17,10 +17,8 @@
 HALF = 128
 WBLOCKS = 22
 WROWS = WBLOCKS * ROWS
-ORDER = (
-    22, 13, 6, 20, 19, 23, 5, 14, 1, 24, 26, 10, 7, 21, 9, 28, 18, 2, 11, 3, 12, 4, 15,
-    25, 16, 31, 29, 30, 0, 17, 8, 27,
-)
+FARTHEST = 22
+ORDER = tuple((FARTHEST + k) % SHARDS for k in range(SHARDS))
 PLACE = tuple(ORDER.index(k) for k in range(SHARDS))
 NORM_EPS = 1e-06
 GROUP_SIZE = ROWS * POS

time: 84.3 us -> 83.9 us (level)
  blocking collectives: 63.5 us -> 62.3 us
    all_to_all x2, blocking collectives: 63.5 us -> 62.3 us  [exchange(): lax.all_to_all(values, 'ch', split_axis=0, concat_axis=0, tiled=True, axi...]
where the time goes in v10:
time: 83.9 us; the launch traced here: 83.7 us
  blocking collectives  62.3 us (74%)
  Pallas kernels  11.1 us (13%)
  starting transfers between devices  6.94 us (8%)
  waiting for transfers between devices  2.54 us (3%)
    all_to_all x2, blocking collectives, exchange(): lax.all_to_all(values, 'ch', split_axis=0, concat_axis=0, tiled=True, axi...  62.3 us
    pallas_call x7, Pallas kernels, local_call(): pl.pallas_call(kernel, out_shape=shapes, in_specs=in_specs, out_specs=tup...  7.55 us
    ppermute x6, starting transfers between devices, on_device(): lax.ppermute(values, 'img', core_pairs)  3.54 us
    ppermute x1, starting transfers between devices, on_device(): theirs = lax.ppermute(sums, 'img', core_pairs)  2.59 us
  transfers between devices with their start and end apart: 8, of which 3 were waited for; matrix products, arithmetic and copies ran while one was open for 0% of the time, Pallas kernels for 9%

profile of v10, /device:TPU:1, one launch (start us, length us, event | category | flops | bytes accessed | tf_op | source)
XLA Modules:
  0.0 83.7 jit_solution(10852545577549305657)
XLA Ops:
  0.7 1.6 %shard_map.229 = (bf16[32,232,128]{2,1,0:T(8,128)(2,1)S(1)}, f32[32,512]{1,0:T(8,128)S(1)}) custom-call(s32[1]{0:T(128)} %bitcast.core_ref, s32[32]{0:T(128)} %refs_0_.1, f32[3,8]{1,0:T(4,128)} %refs_1_.1, f32[3,8]{1,0:T(4,128)} %refs_2_.1, f32[2,8]{1,0:T(2,128)} %refs_3_.1, f32[2,8]{1,0:T(2,128)} %refs_4_.1, f32[1,8]{1,0:T(1,128)} %bitcast.8, ...), custom_call_target="tpu_custom_call" | custom-call | tf_op jit(solution)/shard_map/pallas_call | solution.py:719
  2.3 32.8 %all_to_all.10.recv_ref = bf16[32,232,128]{2,1,0:T(8,128)(2,1)S(1)} all-to-all(bf16[32,232,128]{2,1,0:T(8,128)(2,1)S(1)} %get-tuple-element.52), channel_id=1, replica_groups={{88,92,96,100,104,108,112,116,120,124,0,4,8,12,16,20,24,28,32,36,40,44,..., dimensions={0} | all-to-all | bytes 3801088 | tf_op jit(solution)/shard_map/all_to_all | solution.py:735
  35.2 1.8 %collective-permute-start.2 = (bf16[32,80,128]{2,1,0:T(8,128)(2,1)S(1)}, bf16[32,80,128]{2,1,0:T(8,128)(2,1)S(1)}, u32[]{:S(2)}, u32[]{:S(2)}) collective-permute-start(bf16[32,80,128]{2,1,0:T(8,128)(2,1)S(1)} %slice.14), channel_id=1, source_target_pairs={{0,1},{1,0},{2,3},{3,2},{4,5},{5,4},{6,7},{7,6},{8,9},{9,8},{10,11... | collective-permute-start | bytes 1966088 | tf_op jit(solution)/shard_map/ppermute | solution.py:779
  37.0 0.1 fusion
  37.1 0.1 collective-permute-start.1
  37.2 0.5 collective-permute-start
  37.7 1.0 %shard_map.230 = (bf16[2,3,128,256]{3,2,1,0:T(8,128)(2,1)S(1)}, f32[256,256]{1,0:T(8,128)S(1)}, f32[256,128]{1,0:T(8,128)S(1)}, f32[256,128]{1,0:T(8,128)S(1)}, ...) custom-call(s32[1]{0:T(128)} %bitcast.core_ref, bf16[32,232,128]{2,1,0:T(8,128)(2,1)S(1)} %all_to_all.10.recv_ref), custom_call_target="tpu_custom_call" | custom-call | tf_op jit(solution)/shard_map/pallas_call | solution.py:422
  38.7 0.1 collective-permute-done.2.swapped
  38.7 0.8 %shard_map.231 = (bf16[10,256,128]{2,1,0:T(8,128)(2,1)S(1)}, bf16[2,3,128,256]{3,2,1,0:T(8,128)(2,1)S(1)}, f32[256,256]{1,0:T(8,128)S(1)}, f32[256,128]{1,0:T(8,128)S(1)}, bf16[1024,256]{1,0:T(8,128)(2,1)S(1)}) custom-call(s32[1]{0:T(128)} %bitcast.core_ref, bf16[32,232,128]{2,1,0:T(8,128)(2,1)S(1)} %all_to_all.10.recv_ref, ...), custom_call_target="tpu_custom_call" | custom-call | tf_op jit(solution)/shard_map/pallas_call | solution.py:422
  39.6 0.5 collective-permute-start.3
  40.0 0.0 collective-permute-done.1.swapped_three
  40.0 0.0 collective-permute-done.swapped_two
  40.0 2.4 %shard_map.232 = (bf16[12,256,128]{2,1,0:T(8,128)(2,1)S(1)}, bf16[32,16,128]{2,1,0:T(8,128)(2,1)S(1)}, f32[256,256]{1,0:T(8,128)S(1)}, f32[256,128]{1,0:T(8,128)...) custom-call(s32[1]{0:T(128)} %bitcast.core_ref, ...), custom_call_target="tpu_custom_call" | custom-call | tf_op jit(solution)/shard_map/pallas_call | solution.py:422
  42.4 0.3 collective-permute-start.5
  42.7 0.0 collective-permute-done.3.their_shifts
  42.7 0.9 %shard_map.233 = (bf16[256,256]{1,0:T(8,128)(2,1)S(1)}, f32[256,128]{1,0:T(8,128)S(1)}) custom-call(s32[1]{0:T(128)} %bitcast.core_ref, bf16[32,232,128]{2,1,0:T(8,128)(2,1)S(1)} %all_to_all.10.recv_ref, bf16[22,256,128]{2,1,0:T(8,128)(2,1)S(1)} %get-tuple-element.54.own, bf16[12,256,128]{2,1,0:T(8,128)(2,1)S(1)} %get-tuple-element.59.other, ...), custom_call_target="tpu_custom_call" | custom-call | tf_op jit(solution)/shard_map/pallas_call | solution.py:422
  43.6 0.4 collective-permute-start.4
  44.0 0.9 %shard_map.235.tail = bf16[32,32,128]{2,1,0:T(8,128)(2,1)S(1)} custom-call(s32[1]{0:T(128)} %bitcast.core_ref, bf16[22,256,128]{2,1,0:T(8,128)(2,1)S(1)} %get-tuple-element.54.own, bf16[10,256,128]{2,1,0:T(8,128)(2,1)S(1)} %get-tuple-element.58.other_one.other, f32[256,256]{1,0:T(8,128)S(1)} %get-tuple-element.73.hat_ref, ...), custom_call_target="tpu_custom_call" | custom-call | tf_op jit(solution)/shard_map/pallas_call | solution.py:422
  44.9 0.0 collective-permute-done.5.theirs
  44.9 0.9 %shard_map.234.late = bf16[32,112,128]{2,1,0:T(8,128)(2,1)S(1)} custom-call(s32[1]{0:T(128)} %bitcast.core_ref, bf16[32,232,128]{2,1,0:T(8,128)(2,1)S(1)} %all_to_all.10.recv_ref, bf16[2,3,128,256]{3,2,1,0:T(8,128)(2,1)S(1)} %get-tuple-element.57.taps_two, bf16[2,128,256]{2,1,0:T(8,128)(2,1)S(1)} %get-tuple-element.68.normed, ...), custom_call_target="tpu_custom_call" | custom-call | tf_op jit(solution)/shard_map/pallas_call | solution.py:422
  45.8 0.0 collective-permute-done.4.their_low
  45.8 0.6 shard_map.236
  46.5 29.4 %all_to_all.11.back_ref = bf16[32,216,128]{2,1,0:T(8,128)(2,1)S(1)} all-to-all(bf16[32,216,128]{2,1,0:T(8,128)(2,1)S(1)} %shard_map.236), channel_id=1, replica_groups={{88,92,96,100,104,108,112,116,120,124,0,4,8,12,16,20,24,28,32,36,40,44,..., dimensions={0} | all-to-all | bytes 3538944 | tf_op jit(solution)/shard_map/all_to_all | solution.py:735
  75.9 0.3 shard_map.237
  76.2 0.8 collective-permute-start.6
  77.0 0.8 shard_map.238
  77.8 1.5 %collective-permute-done.6 = bf16[224,128]{1,0:T(8,128)(2,1)S(1)} collective-permute-done((bf16[224,128]{1,0:T(8,128)(2,1)S(1)}, bf16[224,128]{1,0:T(8,128)(2,1)S(1)}, u32[]{:S(2)}, u32[]{:S(2)}) %collective-permute-start.6) | collective-permute-done | bytes 57376 | tf_op jit(solution)/shard_map/ppermute | solution.py:784
  79.3 2.6 %collective-permute-start.7 = (f32[224,128]{1,0:T(8,128)S(1)}, f32[224,128]{1,0:T(8,128)S(1)}, u32[]{:S(2)}, u32[]{:S(2)}) collective-permute-start(f32[224,128]{1,0:T(8,128)S(1)} %convert_add_fusion.mine_ref), channel_id=1, source_target_pairs={{0,1},{1,0},{2,3},{3,2},{4,5},{5,4},{6,7},{7,6},{8,9},{9,8},{10,11... | collective-permute-start | bytes 344072 | tf_op jit(solution)/shard_map/ppermute | solution.py:788
  81.9 1.0 %collective-permute-done.7.theirs_ref = f32[224,128]{1,0:T(8,128)S(1)} collective-permute-done((f32[224,128]{1,0:T(8,128)S(1)}, f32[224,128]{1,0:T(8,128)S(1)}, u32[]{:S(2)}, u32[]{:S(2)}) %collective-permute-start.7) | collective-permute-done | bytes 114720 | tf_op jit(solution)/shard_map/ppermute | solution.py:788
  82.9 0.8 shard_map.239
  (2 shorter events, 0.1 us)
Async XLA Ops:
  35.2 3.6 %collective-permute-start.2 = (bf16[32,80,128]{2,1,0:T(8,128)(2,1)S(1)}, bf16[32,80,128]{2,1,0:T(8,128)(2,1)S(1)}, u32[]{:S(2)}, u32[]{:S(2)}) collective-permute-start(bf16[32,80,128]{2,1,0:T(8,128)(2,1)S(1)} %slice.14), channel_id=1, source_target_pairs={{0,1},{1,0},{2,3},{3,2},{4,5},{5,4},{6,7},{7,6},{8,9},{9,8},{10,11... | collective-permute-start | bytes 1966088 | tf_op jit(solution)/shard_map/ppermute | solution.py:779
  37.1 3.0 %collective-permute-start.1 = (bf16[32,48,128]{2,1,0:T(8,128)(2,1)S(1)}, bf16[32,48,128]{2,1,0:T(8,128)(2,1)S(1)}, u32[]{:S(2)}, u32[]{:S(2)}) collective-permute-start(bf16[32,48,128]{2,1,0:T(8,128)(2,1)S(1)} %get-tuple-element.92), channel_id=1, source_target_pairs={{0,1},{1,0},{2,3},{3,2},{4,5},{5,4},{6,7},{7,6},{8,9},{9,8},{10,11... | collective-permute-start | bytes 1179656 | tf_op jit(solution)/shard_map/ppermute | solution.py:779
  37.2 2.9 %collective-permute-start = (bf16[32,48,128]{2,1,0:T(8,128)(2,1)S(1)}, bf16[32,48,128]{2,1,0:T(8,128)(2,1)S(1)}, u32[]{:S(2)}, u32[]{:S(2)}) collective-permute-start(bf16[32,48,128]{2,1,0:T(8,128)(2,1)S(1)} %get-tuple-element.93), channel_id=1, source_target_pairs={{0,1},{1,0},{2,3},{3,2},{4,5},{5,4},{6,7},{7,6},{8,9},{9,8},{10,11... | collective-permute-start | bytes 1179656 | tf_op jit(solution)/shard_map/ppermute | solution.py:779
  39.6 3.1 %collective-permute-start.3 = (bf16[1024,256]{1,0:T(8,128)(2,1)S(1)}, bf16[1024,256]{1,0:T(8,128)(2,1)S(1)}, u32[]{:S(2)}, u32[]{:S(2)}) collective-permute-start(bf16[1024,256]{1,0:T(8,128)(2,1)S(1)} %get-tuple-element.63), channel_id=1, source_target_pairs={{0,1},{1,0},{2,3},{3,2},{4,5},{5,4},{6,7},{7,6},{8,9},{9,8},{10,11... | collective-permute-start | bytes 1572872 | tf_op jit(solution)/shard_map/ppermute | solution.py:779
  42.4 2.5 %collective-permute-start.5 = (bf16[1280,256]{1,0:T(8,128)(2,1)S(1)}, bf16[1280,256]{1,0:T(8,128)(2,1)S(1)}, u32[]{:S(2)}, u32[]{:S(2)}) collective-permute-start(bf16[1280,256]{1,0:T(8,128)(2,1)S(1)} %get-tuple-element.71), channel_id=1, source_target_pairs={{0,1},{1,0},{2,3},{3,2},{4,5},{5,4},{6,7},{7,6},{8,9},{9,8},{10,11... | collective-permute-start | bytes 1966088 | tf_op jit(solution)/shard_map/ppermute | solution.py:779
  43.6 2.2 %collective-permute-start.4 = (bf16[256,256]{1,0:T(8,128)(2,1)S(1)}, bf16[256,256]{1,0:T(8,128)(2,1)S(1)}, u32[]{:S(2)}, u32[]{:S(2)}) collective-permute-start(bf16[256,256]{1,0:T(8,128)(2,1)S(1)} %get-tuple-element.66.low_ref), channel_id=1, source_target_pairs={{0,1},{1,0},{2,3},{3,2},{4,5},{5,4},{6,7},{7,6},{8,9},{9,8},{10,11... | collective-permute-start | bytes 393224 | tf_op jit(solution)/shard_map/ppermute | solution.py:779
  76.2 3.1 %collective-permute-start.6 = (bf16[224,128]{1,0:T(8,128)(2,1)S(1)}, bf16[224,128]{1,0:T(8,128)(2,1)S(1)}, u32[]{:S(2)}, u32[]{:S(2)}) collective-permute-start(bf16[224,128]{1,0:T(8,128)(2,1)S(1)} %shard_map.237), channel_id=1, source_target_pairs={{0,2},{1,3},{2,0},{3,1},{4,6},{5,7},{6,4},{7,5},{8,10},{9,11},{10,... | collective-permute-start | bytes 172040 | tf_op jit(solution)/shard_map/ppermute | solution.py:784
  79.3 3.6 %collective-permute-start.7 = (f32[224,128]{1,0:T(8,128)S(1)}, f32[224,128]{1,0:T(8,128)S(1)}, u32[]{:S(2)}, u32[]{:S(2)}) collective-permute-start(f32[224,128]{1,0:T(8,128)S(1)} %convert_add_fusion.mine_ref), channel_id=1, source_target_pairs={{0,1},{1,0},{2,3},{3,2},{4,5},{5,4},{6,7},{7,6},{8,9},{9,8},{10,11... | collective-permute-start | bytes 344072 | tf_op jit(solution)/shard_map/ppermute | solution.py:788

commit v11 on v10

--- a/solution.py
+++ b/solution.py
@@ -194,6 +194,12 @@
         moved = [row_shifted(part.astype(F32), row).astype(BF16) if row else part for part in wide]
         rows.append(jnp.concatenate(moved, axis=1))
     return lane_blocks(dot_nt(jnp.concatenate(lows, axis=1), jnp.concatenate(rows, axis=0)))
+
+
+def image_weight_grads(low, shifts):
+    part = shifts.reshape(3 * HALF, POS)
+    rows = [row_shifted(part.astype(F32), row).astype(BF16) if row else part for row in (-1, 0, 1)]
+    return dot_nt(low, jnp.concatenate(rows, axis=0))
 
 
 def store_blocks(target, blocks, order=range(SHARDS)):
@@ -352,7 +358,8 @@
 
 
 def first_back_kernel(
-    core_ref, own, other, hat_ref, stats, params, low_ref, grad_ref, sums, tail_ref
+    core_ref, own, other, hat_ref, stats, params, low_ref, grad_ref, sums, taps_two,
+    tail_ref, partial_ref,
 ):
     hat = hat_ref[...]
     gain = column(params, GAINS)
@@ -362,6 +369,7 @@
     first_grad = convolve_back(matrices, low_ref[...], core_ref[0])
     branch, gain_grad, bias_grad = norm_back(hat, column(stats, 0), first_grad * factor, gain)
     tail_ref[:, :16, :] = image_rows(grad_ref[...] + branch)
+    partial_ref[...] = image_weight_grads(grad_ref[...].astype(BF16), taps_two[core_ref[0]])
 
     table = columns_of({D_GAINS: gain_grad, D_BIASES: bias_grad}, sums[...])
     high = table.astype(BF16).astype(F32)
@@ -372,14 +380,11 @@
 
 
 def second_grads_kernel(
-    core_ref, recv_ref, taps_two, normed, attended, gradients, grad_ref, their_shifts, theirs,
-    late_ref,
+    core_ref, recv_ref, partial, normed, attended, gradients, their_shifts, theirs, late_ref
 ):
     core = core_ref[0]
-    low = grad_ref[...].astype(BF16)
-    second = conv_weight_grads(
-        [low, theirs[C : 2 * C, :]], [taps_two[core], their_shifts[3 * HALF : 6 * HALF, :]]
-    )
+    product = image_weight_grads(theirs[C : 2 * C, :], their_shifts[3 * HALF : 6 * HALF, :])
+    second = lane_blocks(partial[...] + product)
     operand = jnp.concatenate([normed[core], theirs[0:HALF, :]], axis=1)
     grads = jnp.concatenate([gradients[...].reshape(3 * C, POS), theirs[2 * C :, :]], axis=1)
     qkv = dot_nt(grads, operand)
@@ -470,12 +475,12 @@
         residual_grad, sums, out=(low, table),
     )
     their_low = swap(low_one)
-    (tail,) = local_call(
+    tail, partial = local_call(
         first_back_kernel, core, own_weights, other_weights, hat_one, stats_one, params, low_one,
-        residual_grad, sums, out=(((SHARDS, 32, HALF), BF16),),
+        residual_grad, sums, taps_two, out=(((SHARDS, 32, HALF), BF16), ((C, 9 * HALF), F32)),
     )
     (late,) = local_call(
-        second_grads_kernel, core, received, taps_two, normed, attended, gradients, residual_grad,
+        second_grads_kernel, core, received, partial, normed, attended, gradients,
         their_shifts, theirs, out=(((SHARDS, WROWS - IN_CUT_ROWS + 16, HALF), BF16),),
     )
     (send,) = local_call(

time: 83.9 us -> 83.8 us (level)
  no operation moved by 1% of the time
where the time goes in v11:
time: 83.8 us; the launch traced here: 83.6 us
  blocking collectives  62.3 us (74%)
  Pallas kernels  11 us (13%)
  starting transfers between devices  6.94 us (8%)
  waiting for transfers between devices  2.54 us (3%)
    all_to_all x2, blocking collectives, exchange(): lax.all_to_all(values, 'ch', split_axis=0, concat_axis=0, tiled=True, axi...  62.3 us
    pallas_call x7, Pallas kernels, local_call(): pl.pallas_call(kernel, out_shape=shapes, in_specs=in_specs, out_specs=tup...  7.47 us
    ppermute x6, starting transfers between devices, on_device(): lax.ppermute(values, 'img', core_pairs)  3.54 us
    ppermute x1, starting transfers between devices, on_device(): theirs = lax.ppermute(sums, 'img', core_pairs)  2.59 us
  transfers between devices with their start and end apart: 8, of which 3 were waited for; matrix products, arithmetic and copies ran while one was open for 0% of the time, Pallas kernels for 9%

profile of v11, /device:TPU:1, one launch (start us, length us, event | category | flops | bytes accessed | tf_op | source)
XLA Modules:
  0.0 83.6 jit_solution(8495268807161724975)
XLA Ops:
  0.7 1.6 %shard_map.229 = (bf16[32,232,128]{2,1,0:T(8,128)(2,1)S(1)}, f32[32,512]{1,0:T(8,128)S(1)}) custom-call(s32[1]{0:T(128)} %bitcast.core_ref, s32[32]{0:T(128)} %refs_0_.1, f32[3,8]{1,0:T(4,128)} %refs_1_.1, f32[3,8]{1,0:T(4,128)} %refs_2_.1, f32[2,8]{1,0:T(2,128)} %refs_3_.1, f32[2,8]{1,0:T(2,128)} %refs_4_.1, f32[1,8]{1,0:T(1,128)} %bitcast.8, ...), custom_call_target="tpu_custom_call" | custom-call | tf_op jit(solution)/shard_map/pallas_call | solution.py:724
  2.3 32.8 %all_to_all.10.recv_ref = bf16[32,232,128]{2,1,0:T(8,128)(2,1)S(1)} all-to-all(bf16[32,232,128]{2,1,0:T(8,128)(2,1)S(1)} %get-tuple-element.54), channel_id=1, replica_groups={{88,92,96,100,104,108,112,116,120,124,0,4,8,12,16,20,24,28,32,36,40,44,..., dimensions={0} | all-to-all | bytes 3801088 | tf_op jit(solution)/shard_map/all_to_all | solution.py:740
  35.2 1.8 %collective-permute-start.2 = (bf16[32,80,128]{2,1,0:T(8,128)(2,1)S(1)}, bf16[32,80,128]{2,1,0:T(8,128)(2,1)S(1)}, u32[]{:S(2)}, u32[]{:S(2)}) collective-permute-start(bf16[32,80,128]{2,1,0:T(8,128)(2,1)S(1)} %slice.14), channel_id=1, source_target_pairs={{0,1},{1,0},{2,3},{3,2},{4,5},{5,4},{6,7},{7,6},{8,9},{9,8},{10,11... | collective-permute-start | bytes 1966088 | tf_op jit(solution)/shard_map/ppermute | solution.py:784
  37.0 0.1 fusion
  37.1 0.1 collective-permute-start.1
  37.2 0.5 collective-permute-start
  37.7 1.0 %shard_map.230 = (bf16[2,3,128,256]{3,2,1,0:T(8,128)(2,1)S(1)}, f32[256,256]{1,0:T(8,128)S(1)}, f32[256,128]{1,0:T(8,128)S(1)}, f32[256,128]{1,0:T(8,128)S(1)}, ...) custom-call(s32[1]{0:T(128)} %bitcast.core_ref, bf16[32,232,128]{2,1,0:T(8,128)(2,1)S(1)} %all_to_all.10.recv_ref), custom_call_target="tpu_custom_call" | custom-call | tf_op jit(solution)/shard_map/pallas_call | solution.py:427
  38.7 0.1 collective-permute-done.2.swapped
  38.7 0.8 %shard_map.231 = (bf16[10,256,128]{2,1,0:T(8,128)(2,1)S(1)}, bf16[2,3,128,256]{3,2,1,0:T(8,128)(2,1)S(1)}, f32[256,256]{1,0:T(8,128)S(1)}, f32[256,128]{1,0:T(8,128)S(1)}, bf16[1024,256]{1,0:T(8,128)(2,1)S(1)}) custom-call(s32[1]{0:T(128)} %bitcast.core_ref, bf16[32,232,128]{2,1,0:T(8,128)(2,1)S(1)} %all_to_all.10.recv_ref, ...), custom_call_target="tpu_custom_call" | custom-call | tf_op jit(solution)/shard_map/pallas_call | solution.py:427
  39.6 0.5 collective-permute-start.3
  40.0 0.0 collective-permute-done.1.swapped_three
  40.0 0.0 collective-permute-done.swapped_two
  40.0 2.4 %shard_map.232 = (bf16[12,256,128]{2,1,0:T(8,128)(2,1)S(1)}, bf16[32,16,128]{2,1,0:T(8,128)(2,1)S(1)}, f32[256,256]{1,0:T(8,128)S(1)}, f32[256,128]{1,0:T(8,128)...) custom-call(s32[1]{0:T(128)} %bitcast.core_ref, ...), custom_call_target="tpu_custom_call" | custom-call | tf_op jit(solution)/shard_map/pallas_call | solution.py:427
  42.4 0.3 collective-permute-start.5
  42.7 0.0 collective-permute-done.3.their_shifts
  42.7 0.9 %shard_map.233 = (bf16[256,256]{1,0:T(8,128)(2,1)S(1)}, f32[256,128]{1,0:T(8,128)S(1)}) custom-call(s32[1]{0:T(128)} %bitcast.core_ref, bf16[32,232,128]{2,1,0:T(8,128)(2,1)S(1)} %all_to_all.10.recv_ref, bf16[22,256,128]{2,1,0:T(8,128)(2,1)S(1)} %get-tuple-element.56.own, bf16[12,256,128]{2,1,0:T(8,128)(2,1)S(1)} %get-tuple-element.61.other, ...), custom_call_target="tpu_custom_call" | custom-call | tf_op jit(solution)/shard_map/pallas_call | solution.py:427
  43.6 0.4 collective-permute-start.4
  44.0 1.0 %shard_map.234 = (bf16[32,32,128]{2,1,0:T(8,128)(2,1)S(1)}, f32[256,1152]{1,0:T(8,128)S(1)}) custom-call(s32[1]{0:T(128)} %bitcast.core_ref, bf16[22,256,128]{2,1,0:T(8,128)(2,1)S(1)} %get-tuple-element.56.own, bf16[10,256,128]{2,1,0:T(8,128)(2,1)S(1)} %get-tuple-element.60.other_one.other, f32[256,256]{1,0:T(8,128)S(1)} %get-tuple-element.70.hat_ref, ...), custom_call_target="tpu_custom_call" | custom-call | tf_op jit(solution)/shard_map/pallas_call | solution.py:427
  45.0 0.0 collective-permute-done.5.theirs
  45.0 0.7 shard_map.235.late
  45.7 0.0 collective-permute-done.4.their_low
  45.7 0.6 shard_map.236
  46.4 29.4 %all_to_all.11.back_ref = bf16[32,216,128]{2,1,0:T(8,128)(2,1)S(1)} all-to-all(bf16[32,216,128]{2,1,0:T(8,128)(2,1)S(1)} %shard_map.236), channel_id=1, replica_groups={{88,92,96,100,104,108,112,116,120,124,0,4,8,12,16,20,24,28,32,36,40,44,..., dimensions={0} | all-to-all | bytes 3538944 | tf_op jit(solution)/shard_map/all_to_all | solution.py:740
  75.8 0.3 shard_map.237
  76.1 0.8 collective-permute-start.6
  77.0 0.8 shard_map.238
  77.7 1.5 %collective-permute-done.6 = bf16[224,128]{1,0:T(8,128)(2,1)S(1)} collective-permute-done((bf16[224,128]{1,0:T(8,128)(2,1)S(1)}, bf16[224,128]{1,0:T(8,128)(2,1)S(1)}, u32[]{:S(2)}, u32[]{:S(2)}) %collective-permute-start.6) | collective-permute-done | bytes 57376 | tf_op jit(solution)/shard_map/ppermute | solution.py:789
  79.3 2.6 %collective-permute-start.7 = (f32[224,128]{1,0:T(8,128)S(1)}, f32[224,128]{1,0:T(8,128)S(1)}, u32[]{:S(2)}, u32[]{:S(2)}) collective-permute-start(f32[224,128]{1,0:T(8,128)S(1)} %convert_add_fusion.mine_ref), channel_id=1, source_target_pairs={{0,1},{1,0},{2,3},{3,2},{4,5},{5,4},{6,7},{7,6},{8,9},{9,8},{10,11... | collective-permute-start | bytes 344072 | tf_op jit(solution)/shard_map/ppermute | solution.py:793
  81.9 1.0 %collective-permute-done.7.theirs_ref = f32[224,128]{1,0:T(8,128)S(1)} collective-permute-done((f32[224,128]{1,0:T(8,128)S(1)}, f32[224,128]{1,0:T(8,128)S(1)}, u32[]{:S(2)}, u32[]{:S(2)}) %collective-permute-start.7) | collective-permute-done | bytes 114720 | tf_op jit(solution)/shard_map/ppermute | solution.py:793
  82.8 0.8 shard_map.239
  (2 shorter events, 0.1 us)
Async XLA Ops:
  35.2 3.6 %collective-permute-start.2 = (bf16[32,80,128]{2,1,0:T(8,128)(2,1)S(1)}, bf16[32,80,128]{2,1,0:T(8,128)(2,1)S(1)}, u32[]{:S(2)}, u32[]{:S(2)}) collective-permute-start(bf16[32,80,128]{2,1,0:T(8,128)(2,1)S(1)} %slice.14), channel_id=1, source_target_pairs={{0,1},{1,0},{2,3},{3,2},{4,5},{5,4},{6,7},{7,6},{8,9},{9,8},{10,11... | collective-permute-start | bytes 1966088 | tf_op jit(solution)/shard_map/ppermute | solution.py:784
  37.1 3.0 %collective-permute-start.1 = (bf16[32,48,128]{2,1,0:T(8,128)(2,1)S(1)}, bf16[32,48,128]{2,1,0:T(8,128)(2,1)S(1)}, u32[]{:S(2)}, u32[]{:S(2)}) collective-permute-start(bf16[32,48,128]{2,1,0:T(8,128)(2,1)S(1)} %get-tuple-element.96), channel_id=1, source_target_pairs={{0,1},{1,0},{2,3},{3,2},{4,5},{5,4},{6,7},{7,6},{8,9},{9,8},{10,11... | collective-permute-start | bytes 1179656 | tf_op jit(solution)/shard_map/ppermute | solution.py:784
  37.2 2.9 %collective-permute-start = (bf16[32,48,128]{2,1,0:T(8,128)(2,1)S(1)}, bf16[32,48,128]{2,1,0:T(8,128)(2,1)S(1)}, u32[]{:S(2)}, u32[]{:S(2)}) collective-permute-start(bf16[32,48,128]{2,1,0:T(8,128)(2,1)S(1)} %get-tuple-element.97), channel_id=1, source_target_pairs={{0,1},{1,0},{2,3},{3,2},{4,5},{5,4},{6,7},{7,6},{8,9},{9,8},{10,11... | collective-permute-start | bytes 1179656 | tf_op jit(solution)/shard_map/ppermute | solution.py:784
  39.6 3.1 %collective-permute-start.3 = (bf16[1024,256]{1,0:T(8,128)(2,1)S(1)}, bf16[1024,256]{1,0:T(8,128)(2,1)S(1)}, u32[]{:S(2)}, u32[]{:S(2)}) collective-permute-start(bf16[1024,256]{1,0:T(8,128)(2,1)S(1)} %get-tuple-element.65), channel_id=1, source_target_pairs={{0,1},{1,0},{2,3},{3,2},{4,5},{5,4},{6,7},{7,6},{8,9},{9,8},{10,11... | collective-permute-start | bytes 1572872 | tf_op jit(solution)/shard_map/ppermute | solution.py:784
  42.4 2.6 %collective-permute-start.5 = (bf16[1280,256]{1,0:T(8,128)(2,1)S(1)}, bf16[1280,256]{1,0:T(8,128)(2,1)S(1)}, u32[]{:S(2)}, u32[]{:S(2)}) collective-permute-start(bf16[1280,256]{1,0:T(8,128)(2,1)S(1)} %get-tuple-element.77), channel_id=1, source_target_pairs={{0,1},{1,0},{2,3},{3,2},{4,5},{5,4},{6,7},{7,6},{8,9},{9,8},{10,11... | collective-permute-start | bytes 1966088 | tf_op jit(solution)/shard_map/ppermute | solution.py:784
  43.6 2.1 %collective-permute-start.4 = (bf16[256,256]{1,0:T(8,128)(2,1)S(1)}, bf16[256,256]{1,0:T(8,128)(2,1)S(1)}, u32[]{:S(2)}, u32[]{:S(2)}) collective-permute-start(bf16[256,256]{1,0:T(8,128)(2,1)S(1)} %get-tuple-element.68.low_ref), channel_id=1, source_target_pairs={{0,1},{1,0},{2,3},{3,2},{4,5},{5,4},{6,7},{7,6},{8,9},{9,8},{10,11... | collective-permute-start | bytes 393224 | tf_op jit(solution)/shard_map/ppermute | solution.py:784
  76.1 3.1 %collective-permute-start.6 = (bf16[224,128]{1,0:T(8,128)(2,1)S(1)}, bf16[224,128]{1,0:T(8,128)(2,1)S(1)}, u32[]{:S(2)}, u32[]{:S(2)}) collective-permute-start(bf16[224,128]{1,0:T(8,128)(2,1)S(1)} %shard_map.237), channel_id=1, source_target_pairs={{0,2},{1,3},{2,0},{3,1},{4,6},{5,7},{6,4},{7,5},{8,10},{9,11},{10,... | collective-permute-start | bytes 172040 | tf_op jit(solution)/shard_map/ppermute | solution.py:789
  79.3 3.6 %collective-permute-start.7 = (f32[224,128]{1,0:T(8,128)S(1)}, f32[224,128]{1,0:T(8,128)S(1)}, u32[]{:S(2)}, u32[]{:S(2)}) collective-permute-start(f32[224,128]{1,0:T(8,128)S(1)} %convert_add_fusion.mine_ref), channel_id=1, source_target_pairs={{0,1},{1,0},{2,3},{3,2},{4,5},{5,4},{6,7},{7,6},{8,9},{9,8},{10,11... | collective-permute-start | bytes 344072 | tf_op jit(solution)/shard_map/ppermute | solution.py:793

commit v12 on v11

--- a/solution.py
+++ b/solution.py
@@ -654,7 +654,7 @@
     swished_ref[...] = swished
     offsets = None
     rest = swished
-    for _ in range(3):
+    for _ in range(2):
         part = rest.astype(BF16)
         rest = rest - part.astype(F32)
         product = dot_nt(temb_ref[...], part)

time: 83.8 us -> 83.8 us (level)
  no operation moved by 1% of the time
where the time goes in v12:
time: 83.8 us; the launch traced here: 83.6 us
  blocking collectives  62.3 us (74%)
  Pallas kernels  11 us (13%)
  starting transfers between devices  6.95 us (8%)
  waiting for transfers between devices  2.54 us (3%)
    all_to_all x2, blocking collectives, exchange(): lax.all_to_all(values, 'ch', split_axis=0, concat_axis=0, tiled=True, axi...  62.3 us
    pallas_call x7, Pallas kernels, local_call(): pl.pallas_call(kernel, out_shape=shapes, in_specs=in_specs, out_specs=tup...  7.47 us
    ppermute x6, starting transfers between devices, on_device(): lax.ppermute(values, 'img', core_pairs)  3.54 us
    ppermute x1, starting transfers between devices, on_device(): theirs = lax.ppermute(sums, 'img', core_pairs)  2.6 us
  transfers between devices with their start and end apart: 8, of which 3 were waited for; matrix products, arithmetic and copies ran while one was open for 0% of the time, Pallas kernels for 9%

profile of v12, /device:TPU:1, one launch (start us, length us, event | category | flops | bytes accessed | tf_op | source)
XLA Modules:
  0.0 83.6 jit_solution(16577369454632260676)
XLA Ops:
  0.7 1.6 %shard_map.229 = (bf16[32,232,128]{2,1,0:T(8,128)(2,1)S(1)}, f32[32,512]{1,0:T(8,128)S(1)}) custom-call(s32[1]{0:T(128)} %bitcast.core_ref, s32[32]{0:T(128)} %refs_0_.1, f32[3,8]{1,0:T(4,128)} %refs_1_.1, f32[3,8]{1,0:T(4,128)} %refs_2_.1, f32[2,8]{1,0:T(2,128)} %refs_3_.1, f32[2,8]{1,0:T(2,128)} %refs_4_.1, f32[1,8]{1,0:T(1,128)} %bitcast.8, ...), custom_call_target="tpu_custom_call" | custom-call | tf_op jit(solution)/shard_map/pallas_call | solution.py:724
  2.3 32.8 %all_to_all.10.recv_ref = bf16[32,232,128]{2,1,0:T(8,128)(2,1)S(1)} all-to-all(bf16[32,232,128]{2,1,0:T(8,128)(2,1)S(1)} %get-tuple-element.54), channel_id=1, replica_groups={{88,92,96,100,104,108,112,116,120,124,0,4,8,12,16,20,24,28,32,36,40,44,..., dimensions={0} | all-to-all | bytes 3801088 | tf_op jit(solution)/shard_map/all_to_all | solution.py:740
  35.2 1.8 %collective-permute-start.2 = (bf16[32,80,128]{2,1,0:T(8,128)(2,1)S(1)}, bf16[32,80,128]{2,1,0:T(8,128)(2,1)S(1)}, u32[]{:S(2)}, u32[]{:S(2)}) collective-permute-start(bf16[32,80,128]{2,1,0:T(8,128)(2,1)S(1)} %slice.14), channel_id=1, source_target_pairs={{0,1},{1,0},{2,3},{3,2},{4,5},{5,4},{6,7},{7,6},{8,9},{9,8},{10,11... | collective-permute-start | bytes 1966088 | tf_op jit(solution)/shard_map/ppermute | solution.py:784
  37.0 0.1 fusion
  37.1 0.1 collective-permute-start.1
  37.2 0.5 collective-permute-start
  37.6 1.0 %shard_map.230 = (bf16[2,3,128,256]{3,2,1,0:T(8,128)(2,1)S(1)}, f32[256,256]{1,0:T(8,128)S(1)}, f32[256,128]{1,0:T(8,128)S(1)}, f32[256,128]{1,0:T(8,128)S(1)}, ...) custom-call(s32[1]{0:T(128)} %bitcast.core_ref, bf16[32,232,128]{2,1,0:T(8,128)(2,1)S(1)} %all_to_all.10.recv_ref), custom_call_target="tpu_custom_call" | custom-call | tf_op jit(solution)/shard_map/pallas_call | solution.py:427
  38.7 0.1 collective-permute-done.2.swapped
  38.7 0.8 %shard_map.231 = (bf16[10,256,128]{2,1,0:T(8,128)(2,1)S(1)}, bf16[2,3,128,256]{3,2,1,0:T(8,128)(2,1)S(1)}, f32[256,256]{1,0:T(8,128)S(1)}, f32[256,128]{1,0:T(8,128)S(1)}, bf16[1024,256]{1,0:T(8,128)(2,1)S(1)}) custom-call(s32[1]{0:T(128)} %bitcast.core_ref, bf16[32,232,128]{2,1,0:T(8,128)(2,1)S(1)} %all_to_all.10.recv_ref, ...), custom_call_target="tpu_custom_call" | custom-call | tf_op jit(solution)/shard_map/pallas_call | solution.py:427
  39.6 0.5 collective-permute-start.3
  40.0 0.0 collective-permute-done.1.swapped_three
  40.0 0.0 collective-permute-done.swapped_two
  40.0 2.4 %shard_map.232 = (bf16[12,256,128]{2,1,0:T(8,128)(2,1)S(1)}, bf16[32,16,128]{2,1,0:T(8,128)(2,1)S(1)}, f32[256,256]{1,0:T(8,128)S(1)}, f32[256,128]{1,0:T(8,128)...) custom-call(s32[1]{0:T(128)} %bitcast.core_ref, ...), custom_call_target="tpu_custom_call" | custom-call | tf_op jit(solution)/shard_map/pallas_call | solution.py:427
  42.4 0.3 collective-permute-start.5
  42.7 0.0 collective-permute-done.3.their_shifts
  42.7 0.9 %shard_map.233 = (bf16[256,256]{1,0:T(8,128)(2,1)S(1)}, f32[256,128]{1,0:T(8,128)S(1)}) custom-call(s32[1]{0:T(128)} %bitcast.core_ref, bf16[32,232,128]{2,1,0:T(8,128)(2,1)S(1)} %all_to_all.10.recv_ref, bf16[22,256,128]{2,1,0:T(8,128)(2,1)S(1)} %get-tuple-element.56.own, bf16[12,256,128]{2,1,0:T(8,128)(2,1)S(1)} %get-tuple-element.61.other, ...), custom_call_target="tpu_custom_call" | custom-call | tf_op jit(solution)/shard_map/pallas_call | solution.py:427
  43.6 0.4 collective-permute-start.4
  44.0 1.0 %shard_map.234 = (bf16[32,32,128]{2,1,0:T(8,128)(2,1)S(1)}, f32[256,1152]{1,0:T(8,128)S(1)}) custom-call(s32[1]{0:T(128)} %bitcast.core_ref, bf16[22,256,128]{2,1,0:T(8,128)(2,1)S(1)} %get-tuple-element.56.own, bf16[10,256,128]{2,1,0:T(8,128)(2,1)S(1)} %get-tuple-element.60.other_one.other, f32[256,256]{1,0:T(8,128)S(1)} %get-tuple-element.70.hat_ref, ...), custom_call_target="tpu_custom_call" | custom-call | tf_op jit(solution)/shard_map/pallas_call | solution.py:427
  45.0 0.0 collective-permute-done.5.theirs
  45.0 0.7 shard_map.235.late
  45.7 0.0 collective-permute-done.4.their_low
  45.7 0.6 shard_map.236
  46.4 29.4 %all_to_all.11.back_ref = bf16[32,216,128]{2,1,0:T(8,128)(2,1)S(1)} all-to-all(bf16[32,216,128]{2,1,0:T(8,128)(2,1)S(1)} %shard_map.236), channel_id=1, replica_groups={{88,92,96,100,104,108,112,116,120,124,0,4,8,12,16,20,24,28,32,36,40,44,..., dimensions={0} | all-to-all | bytes 3538944 | tf_op jit(solution)/shard_map/all_to_all | solution.py:740
  75.8 0.3 shard_map.237
  76.1 0.8 collective-permute-start.6
  76.9 0.8 shard_map.238
  77.7 1.5 %collective-permute-done.6 = bf16[224,128]{1,0:T(8,128)(2,1)S(1)} collective-permute-done((bf16[224,128]{1,0:T(8,128)(2,1)S(1)}, bf16[224,128]{1,0:T(8,128)(2,1)S(1)}, u32[]{:S(2)}, u32[]{:S(2)}) %collective-permute-start.6) | collective-permute-done | bytes 57376 | tf_op jit(solution)/shard_map/ppermute | solution.py:789
  79.3 2.6 %collective-permute-start.7 = (f32[224,128]{1,0:T(8,128)S(1)}, f32[224,128]{1,0:T(8,128)S(1)}, u32[]{:S(2)}, u32[]{:S(2)}) collective-permute-start(f32[224,128]{1,0:T(8,128)S(1)} %convert_add_fusion.mine_ref), channel_id=1, source_target_pairs={{0,1},{1,0},{2,3},{3,2},{4,5},{5,4},{6,7},{7,6},{8,9},{9,8},{10,11... | collective-permute-start | bytes 344072 | tf_op jit(solution)/shard_map/ppermute | solution.py:793
  81.9 1.0 %collective-permute-done.7.theirs_ref = f32[224,128]{1,0:T(8,128)S(1)} collective-permute-done((f32[224,128]{1,0:T(8,128)S(1)}, f32[224,128]{1,0:T(8,128)S(1)}, u32[]{:S(2)}, u32[]{:S(2)}) %collective-permute-start.7) | collective-permute-done | bytes 114720 | tf_op jit(solution)/shard_map/ppermute | solution.py:793
  82.8 0.8 shard_map.239
  (2 shorter events, 0.1 us)
Async XLA Ops:
  35.2 3.6 %collective-permute-start.2 = (bf16[32,80,128]{2,1,0:T(8,128)(2,1)S(1)}, bf16[32,80,128]{2,1,0:T(8,128)(2,1)S(1)}, u32[]{:S(2)}, u32[]{:S(2)}) collective-permute-start(bf16[32,80,128]{2,1,0:T(8,128)(2,1)S(1)} %slice.14), channel_id=1, source_target_pairs={{0,1},{1,0},{2,3},{3,2},{4,5},{5,4},{6,7},{7,6},{8,9},{9,8},{10,11... | collective-permute-start | bytes 1966088 | tf_op jit(solution)/shard_map/ppermute | solution.py:784
  37.1 3.0 %collective-permute-start.1 = (bf16[32,48,128]{2,1,0:T(8,128)(2,1)S(1)}, bf16[32,48,128]{2,1,0:T(8,128)(2,1)S(1)}, u32[]{:S(2)}, u32[]{:S(2)}) collective-permute-start(bf16[32,48,128]{2,1,0:T(8,128)(2,1)S(1)} %get-tuple-element.96), channel_id=1, source_target_pairs={{0,1},{1,0},{2,3},{3,2},{4,5},{5,4},{6,7},{7,6},{8,9},{9,8},{10,11... | collective-permute-start | bytes 1179656 | tf_op jit(solution)/shard_map/ppermute | solution.py:784
  37.2 2.9 %collective-permute-start = (bf16[32,48,128]{2,1,0:T(8,128)(2,1)S(1)}, bf16[32,48,128]{2,1,0:T(8,128)(2,1)S(1)}, u32[]{:S(2)}, u32[]{:S(2)}) collective-permute-start(bf16[32,48,128]{2,1,0:T(8,128)(2,1)S(1)} %get-tuple-element.97), channel_id=1, source_target_pairs={{0,1},{1,0},{2,3},{3,2},{4,5},{5,4},{6,7},{7,6},{8,9},{9,8},{10,11... | collective-permute-start | bytes 1179656 | tf_op jit(solution)/shard_map/ppermute | solution.py:784
  39.6 3.1 %collective-permute-start.3 = (bf16[1024,256]{1,0:T(8,128)(2,1)S(1)}, bf16[1024,256]{1,0:T(8,128)(2,1)S(1)}, u32[]{:S(2)}, u32[]{:S(2)}) collective-permute-start(bf16[1024,256]{1,0:T(8,128)(2,1)S(1)} %get-tuple-element.65), channel_id=1, source_target_pairs={{0,1},{1,0},{2,3},{3,2},{4,5},{5,4},{6,7},{7,6},{8,9},{9,8},{10,11... | collective-permute-start | bytes 1572872 | tf_op jit(solution)/shard_map/ppermute | solution.py:784
  42.4 2.6 %collective-permute-start.5 = (bf16[1280,256]{1,0:T(8,128)(2,1)S(1)}, bf16[1280,256]{1,0:T(8,128)(2,1)S(1)}, u32[]{:S(2)}, u32[]{:S(2)}) collective-permute-start(bf16[1280,256]{1,0:T(8,128)(2,1)S(1)} %get-tuple-element.77), channel_id=1, source_target_pairs={{0,1},{1,0},{2,3},{3,2},{4,5},{5,4},{6,7},{7,6},{8,9},{9,8},{10,11... | collective-permute-start | bytes 1966088 | tf_op jit(solution)/shard_map/ppermute | solution.py:784
  43.6 2.1 %collective-permute-start.4 = (bf16[256,256]{1,0:T(8,128)(2,1)S(1)}, bf16[256,256]{1,0:T(8,128)(2,1)S(1)}, u32[]{:S(2)}, u32[]{:S(2)}) collective-permute-start(bf16[256,256]{1,0:T(8,128)(2,1)S(1)} %get-tuple-element.68.low_ref), channel_id=1, source_target_pairs={{0,1},{1,0},{2,3},{3,2},{4,5},{5,4},{6,7},{7,6},{8,9},{9,8},{10,11... | collective-permute-start | bytes 393224 | tf_op jit(solution)/shard_map/ppermute | solution.py:784
  76.1 3.1 %collective-permute-start.6 = (bf16[224,128]{1,0:T(8,128)(2,1)S(1)}, bf16[224,128]{1,0:T(8,128)(2,1)S(1)}, u32[]{:S(2)}, u32[]{:S(2)}) collective-permute-start(bf16[224,128]{1,0:T(8,128)(2,1)S(1)} %shard_map.237), channel_id=1, source_target_pairs={{0,2},{1,3},{2,0},{3,1},{4,6},{5,7},{6,4},{7,5},{8,10},{9,11},{10,... | collective-permute-start | bytes 172040 | tf_op jit(solution)/shard_map/ppermute | solution.py:789
  79.3 3.6 %collective-permute-start.7 = (f32[224,128]{1,0:T(8,128)S(1)}, f32[224,128]{1,0:T(8,128)S(1)}, u32[]{:S(2)}, u32[]{:S(2)}) collective-permute-start(f32[224,128]{1,0:T(8,128)S(1)} %convert_add_fusion.mine_ref), channel_id=1, source_target_pairs={{0,1},{1,0},{2,3},{3,2},{4,5},{5,4},{6,7},{7,6},{8,9},{9,8},{10,11... | collective-permute-start | bytes 344072 | tf_op jit(solution)/shard_map/ppermute | solution.py:793
